TPU v7x, 32 devices: a whole 2x2x4 slice. The times are simulated.
32 devices in a mesh: dp: 8 (over z, core), tensor: 4 (over y, x).
Axes of the slice: x: 2, y: 2, z: 4, core: 2. Of those that a mesh axis runs over, the one named last changes fastest.
Arguments:
- tokens: bfloat16 [8192, 1024], P('dp'), may hold values from -6 to 6
- segment: int32 [8, 1024], P('dp'), may hold values from 0 to 3, never falling along the last dimension, each value on 1 to 512 neighbouring positions
- attn_gain: float32 [1024], replicated, may hold values from 0.5 to 1.5
- attn_shift: float32 [1024], replicated, may hold values from -1.5 to 1.5
- mlp_gain: float32 [1024], replicated, may hold values from 0.5 to 1.5
- mlp_shift: float32 [1024], replicated, may hold values from -1.5 to 1.5
- w_qkv: bfloat16 [1024, 3072], P(None, 'tensor'), may hold values from -0.1875 to 0.1875
- b_qkv: float32 [3072], P('tensor'), may hold values from -1.5 to 1.5
- w_out: bfloat16 [1024, 1024], P('tensor'), may hold values from -1.5 to 1.5
- w_up: bfloat16 [1024, 4096], P(None, 'tensor'), may hold values from -0.1875 to 0.1875
- b_up: float32 [4096], P('tensor'), may hold values from -1.5 to 1.5
- w_down: bfloat16 [4096, 1024], P('tensor'), may hold values from -0.09375 to 0.09375
- b_branch: float32 [1024], replicated, may hold values from -1.5 to 1.5
- cotangent: bfloat16 [8192, 1024], P('dp'), may hold values from -6 to 6
Outputs:
- result: bfloat16 [8192, 1024], P('dp')
- d_tokens: float32 [8192, 1024], P('dp')
- d_w_qkv: float32 [1024, 3072], P(None, 'tensor')
- d_b_qkv: float32 [3072], P('tensor')
- d_w_out: float32 [1024, 1024], P('tensor')
- d_w_up: float32 [1024, 4096], P(None, 'tensor')
- d_b_up: float32 [4096], P('tensor')
- d_w_down: float32 [4096, 1024], P('tensor')
- d_b_branch: float32 [1024], replicated
- d_attn_gain: float32 [1024], replicated
- d_attn_shift: float32 [1024], replicated
- d_mlp_gain: float32 [1024], replicated
- d_mlp_shift: float32 [1024], replicated
Inputs may be any that keep to these rules, and one draw needn't show every extreme that they name: Within each sequence segment numbers never fall; each document holds 1 to 512 tokens.
All inputs are finite; a program needn't handle non-finite values.
Results may differ from a plain program's by a relative error of at most 0.012.
Values sent between devices are 32-bit elements; how exact they have to be, the bound alone decides.
No kernel may reach another device: no remote copies, remote signals or barrier semaphores. Data moves between devices by JAX's collectives and lax.ppermute only.
A program may use at most 128 MiB of HBM per device.

v0:
```python
import jax
import jax.numpy as jnp
from jax import lax
from jax.sharding import PartitionSpec as P

HD = 64
ROT = 16


EPS = 1e-05
NEG = -1e30


def norm_parts(token_rows, ln_gain, ln_shift):
    row_mean = jnp.mean(token_rows, axis=-1, keepdims=True)
    centred = token_rows - row_mean
    spread = jnp.mean(centred * centred, axis=-1, keepdims=True)
    scale_inv = lax.rsqrt(spread + EPS)
    normed = centred * scale_inv
    return (normed * ln_gain + ln_shift, normed, scale_inv)


def norm_back(upstream, normed, scale_inv, ln_gain):
    scaled = upstream * ln_gain
    return scale_inv * (
        scaled
        - jnp.mean(scaled, axis=-1, keepdims=True)
        - normed * jnp.mean(scaled * normed, axis=-1, keepdims=True)
    )


def norm_stats(upstream, normed):
    return (jnp.sum(upstream * normed, axis=0), jnp.sum(upstream, axis=0))


def inner_rows(first_mat, second_mat):
    return lax.dot_general(
        first_mat, second_mat, (((0,), (0,)), ((), ())), preferred_element_type=jnp.float32
    )


def times_trans(first_mat, second_mat):
    return lax.dot_general(
        first_mat, second_mat, (((1,), (1,)), ((), ())), preferred_element_type=jnp.float32
    )


def rotary_tables(segment):
    spots = lax.broadcasted_iota(jnp.int32, segment.shape, 1)
    opening = jnp.concatenate(
        [jnp.ones((segment.shape[0], 1), jnp.bool_), segment[:, 1:] != segment[:, :-1]], axis=1
    )
    starts = lax.cummax(jnp.where(opening, spots, 0), axis=1)
    offsets = (spots - starts).astype(jnp.float32)
    frequency = 10000.0 ** (-2.0 * jnp.arange(ROT // 2, dtype=jnp.float32) / ROT)
    angles = offsets[:, :, None, None] * frequency
    return (jnp.cos(angles), jnp.sin(angles))


def rotate_pair(vectors, cosine, sine, inverse):
    half_rot = cosine.shape[-1]
    first = vectors[..., :half_rot]
    second = vectors[..., half_rot : 2 * half_rot]
    remain = vectors[..., 2 * half_rot :]
    turn = -sine if inverse else sine
    return jnp.concatenate(
        [first * cosine - second * turn, second * cosine + first * turn, remain], axis=-1
    )


def shards(
    tokens,
    segment,
    attn_gain,
    attn_shift,
    mlp_gain,
    mlp_shift,
    w_qkv,
    b_qkv,
    w_out,
    w_up,
    b_up,
    w_down,
    b_branch,
    cotangent,
):
    token_rows = tokens.astype(jnp.float32)
    count_seq = segment.shape[0]
    seq_len = segment.shape[1]
    rows_here = tokens.shape[0]
    local_heads = w_qkv.shape[1] // (3 * HD)
    score_scale = HD ** (-0.5)
    block = min(512, seq_len)
    attn_in, attn_normed, attn_inv = norm_parts(token_rows, attn_gain, attn_shift)
    mlp_in, mlp_normed, mlp_inv = norm_parts(token_rows, mlp_gain, mlp_shift)
    attn_low = attn_in.astype(jnp.bfloat16)
    mlp_low = mlp_in.astype(jnp.bfloat16)
    cosine, sine = rotary_tables(segment)
    projected = jnp.dot(attn_low, w_qkv, preferred_element_type=jnp.float32) + b_qkv
    grouped = projected.reshape(count_seq, seq_len, local_heads, 3, HD)
    queries = rotate_pair(grouped[:, :, :, 0], cosine, sine, False).astype(jnp.bfloat16)
    keys_rot = rotate_pair(grouped[:, :, :, 1], cosine, sine, False).astype(jnp.bfloat16)
    values = grouped[:, :, :, 2].astype(jnp.bfloat16)
    key_spots = lax.broadcasted_iota(jnp.int32, (block, seq_len), 1)
    query_base = lax.broadcasted_iota(jnp.int32, (block, seq_len), 0)

    def block_scores(start, query_block):
        raw = (
            jnp.einsum("nqhd,nkhd->nhqk", query_block, keys_rot, preferred_element_type=jnp.float32)
            * score_scale
        )
        same_doc = segment[:, start : start + block, None] == segment[:, None, :]
        allowed = same_doc & (key_spots <= query_base + start)
        return jnp.where(allowed[:, None], raw, NEG)

    outputs = []
    lse_parts = []
    for start in range(0, seq_len, block):
        masked = block_scores(start, queries[:, start : start + block])
        row_max = jnp.max(masked, axis=-1, keepdims=True)
        exponent = jnp.exp(masked - row_max)
        totals = jnp.sum(exponent, axis=-1, keepdims=True)
        attn_probs = exponent / totals
        outputs.append(
            jnp.einsum(
                "nhqk,nkhd->nqhd",
                attn_probs.astype(jnp.bfloat16),
                values,
                preferred_element_type=jnp.float32,
            )
        )
        lse_parts.append(row_max + jnp.log(totals))
    attended = (
        jnp.concatenate(outputs, axis=1).astype(jnp.bfloat16).reshape(rows_here, local_heads * HD)
    )
    attn_part = jnp.dot(attended, w_out, preferred_element_type=jnp.float32)
    pre_act = jnp.dot(mlp_low, w_up, preferred_element_type=jnp.float32) + b_up
    hidden = jax.nn.gelu(pre_act, approximate=False).astype(jnp.bfloat16)
    mlp_part = jnp.dot(hidden, w_down, preferred_element_type=jnp.float32)
    branches = lax.psum(attn_part + mlp_part, "tensor")
    result = (token_rows + branches + b_branch).astype(jnp.bfloat16)
    grad_down = inner_rows(hidden, cotangent)
    grad_out = inner_rows(attended, cotangent)
    branch_grad = jnp.sum(cotangent.astype(jnp.float32), axis=0)
    d_hidden = times_trans(cotangent, w_down)
    gelu_pull = jax.vjp(lambda pre_value: jax.nn.gelu(pre_value, approximate=False), pre_act)[1]
    d_pre = gelu_pull(d_hidden)[0].astype(jnp.bfloat16)
    grad_up = inner_rows(mlp_low, d_pre)
    grad_up_bias = jnp.sum(d_pre.astype(jnp.float32), axis=0)
    d_mlp_in = times_trans(d_pre, w_up)
    d_attended = (
        times_trans(cotangent, w_out)
        .astype(jnp.bfloat16)
        .reshape(count_seq, seq_len, local_heads, HD)
    )
    d_queries = []
    d_keys = jnp.zeros((count_seq, seq_len, local_heads, HD), jnp.float32)
    d_values = jnp.zeros((count_seq, seq_len, local_heads, HD), jnp.float32)
    for start in range(0, seq_len, block):
        query_block = queries[:, start : start + block]
        masked = block_scores(start, query_block)
        attn_probs = jnp.exp(masked - lse_parts[start // block])
        grad_block = d_attended[:, start : start + block]
        d_probs = jnp.einsum(
            "nqhd,nkhd->nhqk", grad_block, values, preferred_element_type=jnp.float32
        )
        row_dot = jnp.sum(attn_probs * d_probs, axis=-1, keepdims=True)
        d_scores = (attn_probs * (d_probs - row_dot)).astype(jnp.bfloat16)
        d_queries.append(
            jnp.einsum("nhqk,nkhd->nqhd", d_scores, keys_rot, preferred_element_type=jnp.float32)
            * score_scale
        )
        d_keys = (
            d_keys
            + jnp.einsum(
                "nhqk,nqhd->nkhd", d_scores, query_block, preferred_element_type=jnp.float32
            )
            * score_scale
        )
        d_values = d_values + jnp.einsum(
            "nhqk,nqhd->nkhd",
            attn_probs.astype(jnp.bfloat16),
            grad_block,
            preferred_element_type=jnp.float32,
        )
    d_query_all = rotate_pair(jnp.concatenate(d_queries, axis=1), cosine, sine, True)
    d_key_all = rotate_pair(d_keys, cosine, sine, True)
    d_projected = (
        jnp.stack([d_query_all, d_key_all, d_values], axis=3)
        .reshape(rows_here, local_heads * 3 * HD)
        .astype(jnp.bfloat16)
    )
    grad_qkv = inner_rows(attn_low, d_projected)
    grad_qkv_bias = jnp.sum(d_projected.astype(jnp.float32), axis=0)
    d_attn_in = times_trans(d_projected, w_qkv)
    sum_attn, sum_mlp = lax.psum((d_attn_in, d_mlp_in), "tensor")
    d_tokens = (
        cotangent.astype(jnp.float32)
        + norm_back(sum_attn, attn_normed, attn_inv, attn_gain)
        + norm_back(sum_mlp, mlp_normed, mlp_inv, mlp_gain)
    )
    attn_g, attn_s = norm_stats(sum_attn, attn_normed)
    mlp_g, mlp_s = norm_stats(sum_mlp, mlp_normed)
    layer_stats = jnp.stack([attn_g, attn_s, mlp_g, mlp_s])
    summed = lax.psum(
        (
            grad_qkv,
            grad_qkv_bias,
            grad_out,
            grad_up,
            grad_up_bias,
            grad_down,
            branch_grad,
            layer_stats,
        ),
        "dp",
    )
    total_stats = summed[7]
    return (
        result,
        d_tokens,
        summed[0],
        summed[1],
        summed[2],
        summed[3],
        summed[4],
        summed[5],
        summed[6],
        total_stats[0],
        total_stats[1],
        total_stats[2],
        total_stats[3],
    )


def solution(mesh):
    placed = (
        P("dp", None),
        P("dp", None),
        P(),
        P(),
        P(),
        P(),
        P(None, "tensor"),
        P("tensor"),
        P("tensor", None),
        P(None, "tensor"),
        P("tensor"),
        P("tensor", None),
        P(),
        P("dp", None),
    )
    return jax.shard_map(
        shards,
        mesh=mesh,
        in_specs=placed,
        out_specs=(
            P("dp", None),
            P("dp", None),
            P(None, "tensor"),
            P("tensor"),
            P("tensor", None),
            P(None, "tensor"),
            P("tensor"),
            P("tensor", None),
            P(),
            P(),
            P(),
            P(),
            P(),
        ),
        check_vma=False,
    )
```

profile of v0, /device:TPU:0, one launch (start us, length us, event | category | flops | bytes accessed | tf_op | source)
XLA Modules:
  0.0 613.1 jit_solution(17872242136285181769)
XLA Ops:
  11.2 2.3 fusion.27
  13.5 2.3 convolution_add_fusion.1
  29.1 2.6 multiply_reduce_fusion.1
  39.6 4.3 multiply_reduce_fusion
  43.9 2.5 fusion.31
  46.4 3.0 fusion.57
  49.3 2.8 fusion.56
  52.1 4.4 multiply_convert_fusion
  62.5 3.9 fusion.91
  66.4 2.4 fusion.75
  68.8 12.4 %convert_reduce_fusion.2 = (f32[1024]{0:T(1024)S(1)}, bf16[1024,1024]{1,0:T(8,128)(2,1)S(1)}, f32[1024,1024]{1,0:T(8,128)S(1)}) fusion(f32[1024,1024]{1,0:T(8,128)S(1)} %fusion.75, f32[1024]{0:T(1024)S(1)} %copy-done.32, bf16[1024,1024]{1,0:T(8,128)(2,1)S(1)} %copy-done.7, bf16[1024,1024]{1,0:T(8,128)(2,1)S(1)} %copy-done), kind=kOutput, calls=%fused_computation.51 | convolution fusion | flops 2226125824 | bytes 14688256 | tf_op jit(solution)/shard_map/dot_general | solution.py:43
  82.4 2.3 fusion.90
  84.9 4.5 fusion.92
  89.3 2.8 convolution_add_fusion
  92.3 3.3 fusion.62
  95.6 6.1 fusion.77
  101.7 4.4 fusion.93
  106.1 4.7 fusion.73
  111.0 224.9 %all-reduce.8.cloned.1.call-done = (f32[1024,1024]{1,0:T(8,128)}, f32[1024,1024]{1,0:T(8,128)}, f32[1024,1024]{1,0:T(8,128)}) async-done(((f32[1024,1024]{1,0:T(8,128)}, f32[1024,1024]{1,0:T(8,128)}, f32[1024,1024]{1,0:T(8,128)}), (f32[1024,1024]{1,0:T(8,128)}, f32[1024,1024]{1,0:T(8,128)}, f32[1024,1024]{1,0:T(8,128)})) %all-reduce.8.cloned.1.call-update) | async-done | bytes 12582928 | tf_op jit(solution)/shard_map/psum | solution.py:140
  335.9 6.0 fusion.25
  343.0 7.9 %convert_reduce_fusion.1 = (f32[1024]{0:T(1024)S(1)}, f32[1024,1024]{1,0:T(8,128)}, bf16[1024,1024]{1,0:T(8,128)(2,1)}) fusion(bf16[1024,1024]{1,0:T(8,128)(2,1)} %param.27, f32[1024]{0:T(1024)S(1)} %broadcast_multiply_fusion, f32[1024]{0:T(1024)S(1)} %broadcast_multiply_fusion.1, f32[1024,1024]{1,0:T(8,128)S(1)} %copy-done.5, f32[1024]{0:T(1024)S(1)} %copy-done.30, ...), kind=kLoop, calls=%fused_computation.20 | loop fusion | flops 20970496 | bytes 23109632 | tf_op jit(solution)/shard_map/reduce_sum | solution.py:144
  350.9 31.2 %all-reduce = (f32[768]{0:T(1024)}, f32[1024]{0:T(1024)}, f32[1024]{0:T(1024)}, f32[4,1024]{1,0:T(4,128)S(1)}) all-reduce(f32[768]{0:T(1024)S(1)} %reduce_sum.174, f32[1024]{0:T(1024)S(1)} %get-tuple-element.36, f32[1024]{0:T(1024)S(1)} %get-tuple-element.46, ...), channel_id=1, replica_groups=mesh['dp'=8,'tensor'=4] {'dp'}, use_global_device_ids=true, to_apply=%region_19.20 | all-reduce | flops 6912 | bytes 55296 | tf_op jit(solution)/shard_map/psum | solution.py:205
  382.6 212.8 %all-reduce.6.cloned.1.call-done = (f32[1024,768]{1,0:T(8,128)}, f32[256,1024]{1,0:T(8,128)}, f32[1024,1024]{1,0:T(8,128)}, f32[1024,1024]{1,0:T(8,128)}) async-done(((f32[1024,768]{1,0:T(8,128)}, f32[256,1024]{1,0:T(8,128)}, f32[1024,1024]{1,0:T(8,128)}, f32[1024,1024]{1,0:T(8,128)}), (f32[1024,768]{1,0:T(8,128)}, f32[256,1024]{1,0:T(8,128)}, f32[1024,1024]{1,0:T(8,128)}, ...) | async-done | bytes 12582928 | tf_op jit(solution)/shard_map/psum | solution.py:205
  595.5 3.9 copy.58
  (143 shorter events, 40.8 us)
Async XLA Ops:
  7.2 61.6 %copy-start = (bf16[1024,1024]{1,0:T(8,128)(2,1)S(1)}, bf16[1024,1024]{1,0:T(8,128)(2,1)}, u32[]{:S(2)}) copy-start(bf16[1024,1024]{1,0:T(8,128)(2,1)} %param.25) | copy-start | bytes 6291460
  7.2 6.3 %copy-start.31 = (f32[1024]{0:T(1024)S(1)}, f32[1024]{0:T(1024)}, u32[]{:S(2)}) copy-start(f32[1024]{0:T(1024)} %param.16) | copy-start | bytes 12292
  7.2 6.3 %copy-start.38 = (f32[1024]{0:T(1024)S(1)}, f32[1024]{0:T(1024)}, u32[]{:S(2)}) copy-start(f32[1024]{0:T(1024)} %param.17) | copy-start | bytes 12292
  7.2 6.3 %copy-start.37 = (f32[768]{0:T(1024)S(1)}, f32[768]{0:T(1024)}, u32[]{:S(2)}) copy-start(f32[768]{0:T(1024)} %param.21) | copy-start | bytes 9220
  7.2 328.7 %all-reduce.8.cloned.1.call-start = ((), (), s32[]{:S(2)}) async-start(), calls=%async_computation.1 | async-start | bytes 25165824 | tf_op jit(solution)/shard_map/psum | solution.py:140
  7.3 6.2 %copy-start.1 = (bf16[1024,1024]{1,0:T(8,128)(2,1)S(1)}, bf16[1024,1024]{1,0:T(8,128)(2,1)}, u32[]{:S(2)}) copy-start(bf16[1024,1024]{1,0:T(8,128)(2,1)} %param.14) | copy-start | bytes 6291460
  7.3 6.2 %copy-start.35 = (bf16[1024,768]{1,0:T(8,128)(2,1)S(1)}, bf16[1024,768]{1,0:T(8,128)(2,1)}, u32[]{:S(2)}) copy-start(bf16[1024,768]{1,0:T(8,128)(2,1)} %param.20) | copy-start | bytes 4718596
  61.7 4.7 copy-start.22
  62.4 3.9 copy-start.34
  62.5 3.9 copy-start.39
  84.8 4.5 copy-start.23
  84.8 4.5 copy-start.24
  84.8 4.5 copy-start.27
  92.1 503.4 %all-reduce.6.cloned.1.call-start = ((), (), s32[]{:S(2)}) async-start(), calls=%async_computation | async-start | bytes 25165824 | tf_op jit(solution)/shard_map/psum | solution.py:205
  95.6 6.1 copy-start.8
  95.6 6.1 copy-start.21
  101.7 4.4 copy-start.3
  101.7 4.4 copy-start.41
  335.9 6.1 copy-start.4
  335.9 6.1 %copy-start.5 = (f32[1024,1024]{1,0:T(8,128)S(1)}, f32[1024,1024]{1,0:T(8,128)}, u32[]{:S(2)}) copy-start(f32[1024,1024]{1,0:T(8,128)} %get-tuple-element.34) | copy-start | bytes 12582916
  335.9 7.1 %copy-start.6 = (f32[1024,1024]{1,0:T(8,128)S(1)}, f32[1024,1024]{1,0:T(8,128)}, u32[]{:S(2)}) copy-start(f32[1024,1024]{1,0:T(8,128)} %get-tuple-element.35) | copy-start | bytes 12582916
  335.9 7.1 %copy-start.33 = (f32[1024]{0:T(1024)S(1)}, f32[1024]{0:T(1024)}, u32[]{:S(2)}) copy-start(f32[1024]{0:T(1024)} %param.26) | copy-start | bytes 12292
  595.5 3.9 copy-start.25
  595.5 4.9 copy-start.12
  (20 other events, 47.6 us)
Sparse Core Ops, SparseCore 0:
  92.2 243.6 all-reduce.7
  339.1 256.3 all-reduce.5
where the time goes:
time: 617 us; the launch traced here: 613 us
  waiting for transfers between devices  438 us (71%)
  matrix products  74.6 us (12%)
  other arithmetic  33.5 us (5%)
  blocking collectives  31.2 us (5%)
  local copies, waits for them, and re-layouts  20.9 us (3%)
  between operations  14.9 us (2%)
    psum x1, waiting for transfers between devices, shards(): branches = lax.psum(attn_part + mlp_part, 'tensor')  225 us
    psum x1, waiting for transfers between devices, shards(): lax.psum((grad_qkv, grad_qkv_bias, grad_out, grad_up, grad_up_bias, grad_...  213 us
    psum x1, blocking collectives, shards(): lax.psum((grad_qkv, grad_qkv_bias, grad_out, grad_up, grad_up_bias, grad_...  31.2 us
    dot_general x4, matrix products, times_trans(): lax.dot_general(first_mat, second_mat, (((1,), (1,)), ((), ())), preferre...  21.5 us
    dot_general x4, matrix products, inner_rows(): lax.dot_general(first_mat, second_mat, (((0,), (0,)), ((), ())), preferre...  18.5 us
    unnamed x88, local copies, waits for them, and re-layouts  16 us
  transfers between devices with their start and end apart: 2, of which 2 were waited for; matrix products, arithmetic and copies ran while one was open for 5% of the time, Pallas kernels for 0%

commit v1 on v0

--- a/solution.py
+++ b/solution.py
@@ -1,3 +1,5 @@
+import math
+
 import jax
 import jax.numpy as jnp
 from jax import lax
@@ -6,31 +8,8 @@
 HD = 64
 ROT = 16
 
-
 EPS = 1e-05
 NEG = -1e30
-
-
-def norm_parts(token_rows, ln_gain, ln_shift):
-    row_mean = jnp.mean(token_rows, axis=-1, keepdims=True)
-    centred = token_rows - row_mean
-    spread = jnp.mean(centred * centred, axis=-1, keepdims=True)
-    scale_inv = lax.rsqrt(spread + EPS)
-    normed = centred * scale_inv
-    return (normed * ln_gain + ln_shift, normed, scale_inv)
-
-
-def norm_back(upstream, normed, scale_inv, ln_gain):
-    scaled = upstream * ln_gain
-    return scale_inv * (
-        scaled
-        - jnp.mean(scaled, axis=-1, keepdims=True)
-        - normed * jnp.mean(scaled * normed, axis=-1, keepdims=True)
-    )
-
-
-def norm_stats(upstream, normed):
-    return (jnp.sum(upstream * normed, axis=0), jnp.sum(upstream, axis=0))
 
 
 def inner_rows(first_mat, second_mat):
@@ -47,10 +26,8 @@
 
 def rotary_tables(segment):
     spots = lax.broadcasted_iota(jnp.int32, segment.shape, 1)
-    opening = jnp.concatenate(
-        [jnp.ones((segment.shape[0], 1), jnp.bool_), segment[:, 1:] != segment[:, :-1]], axis=1
-    )
-    starts = lax.cummax(jnp.where(opening, spots, 0), axis=1)
+    smaller = segment[:, :, None] > segment[:, None, :]
+    starts = jnp.sum(smaller.astype(jnp.int32), axis=2)
     offsets = (spots - starts).astype(jnp.float32)
     frequency = 10000.0 ** (-2.0 * jnp.arange(ROT // 2, dtype=jnp.float32) / ROT)
     angles = offsets[:, :, None, None] * frequency
@@ -68,7 +45,91 @@
     )
 
 
+def swap(array, axis, size, bit):
+    return lax.ppermute(array, axis, [(i, i ^ bit) for i in range(size)])
+
+
+def bits_of(size):
+    return [1 << k for k in range(size.bit_length() - 1)]
+
+
+def scatter_sum(array, size, order):
+    where_am_i = lax.axis_index("tensor")
+    first = 0
+    for bit in order:
+        half = array.shape[0] // 2
+        mine = (where_am_i // bit) % 2
+        away = lax.dynamic_slice_in_dim(array, (1 - mine) * half, half, 0)
+        keep = lax.dynamic_slice_in_dim(array, mine * half, half, 0)
+        array = keep + swap(away, "tensor", size, bit)
+        first = first + mine * half
+    return array, first
+
+
+def gather_back(array, size, order):
+    where_am_i = lax.axis_index("tensor")
+    pieces = [(array, 0)]
+    for bit in reversed(order):
+        pieces = pieces + [(swap(piece, "tensor", size, bit), mask | bit) for piece, mask in pieces]
+    placed = []
+    for piece, mask in pieces:
+        rows = array.shape[0] << len(order)
+        first = 0
+        for bit in order:
+            rows = rows // 2
+            first = first + (((where_am_i ^ mask) // bit) % 2) * rows
+        placed.append((piece, first))
+    return placed
+
+
+def line_sum(array, size):
+    chips = size // 2
+    place = lax.axis_index("dp") // 2
+
+    def send(what, pairs):
+        return lax.ppermute(
+            what, "dp", [(2 * a + c, 2 * b + c) for a, b in pairs for c in range(2)]
+        )
+
+    if chips == 1:
+        return array
+    steps = range(chips // 2 - 1)
+    for s in steps:
+        array = array + send(array, [(s, s + 1), (chips - 1 - s, chips - 2 - s)])
+    middle = chips // 2
+    array = array + send(array, [(middle - 1, middle), (middle, middle - 1)])
+    for s in reversed(steps):
+        got = send(array, [(s + 1, s), (chips - 2 - s, chips - 1 - s)])
+        array = jnp.where((place == s) | (place == chips - 1 - s), got, array)
+    return array
+
+
+def dp_sum(array, size, chunks):
+    core = lax.axis_index("dp") % 2
+    half = array.shape[0] // 2
+    rows = half // chunks
+    total = array
+    for c in range(chunks):
+        away = lax.dynamic_slice_in_dim(array, (1 - core) * half + c * rows, rows, 0)
+        keep = lax.dynamic_slice_in_dim(array, core * half + c * rows, rows, 0)
+        mine = line_sum(keep + swap(away, "dp", size, 1), size)
+        other = swap(mine, "dp", size, 1)
+        total = lax.dynamic_update_slice_in_dim(total, mine, core * half + c * rows, 0)
+        total = lax.dynamic_update_slice_in_dim(total, other, (1 - core) * half + c * rows, 0)
+    return total
+
+
+def small_sum(array, size, axis):
+    if axis == "dp":
+        return line_sum(array + swap(array, "dp", size, 1), size)
+    for bit in bits_of(size):
+        array = array + swap(array, axis, size, bit)
+    return array
+
+
 def shards(
+    dp_size,
+    tensor_size,
     tokens,
     segment,
     attn_gain,
@@ -87,14 +148,20 @@
     token_rows = tokens.astype(jnp.float32)
     count_seq = segment.shape[0]
     seq_len = segment.shape[1]
-    rows_here = tokens.shape[0]
+    rows_here, width = tokens.shape
     local_heads = w_qkv.shape[1] // (3 * HD)
     score_scale = HD ** (-0.5)
     block = min(512, seq_len)
-    attn_in, attn_normed, attn_inv = norm_parts(token_rows, attn_gain, attn_shift)
-    mlp_in, mlp_normed, mlp_inv = norm_parts(token_rows, mlp_gain, mlp_shift)
-    attn_low = attn_in.astype(jnp.bfloat16)
-    mlp_low = mlp_in.astype(jnp.bfloat16)
+    up_order = bits_of(tensor_size)
+    orders = (up_order, up_order[::-1])
+
+    row_mean = jnp.mean(token_rows, axis=-1, keepdims=True)
+    centred = token_rows - row_mean
+    scale_inv = lax.rsqrt(jnp.mean(centred * centred, axis=-1, keepdims=True) + EPS)
+    normed = centred * scale_inv
+    attn_low = (normed * attn_gain + attn_shift).astype(jnp.bfloat16)
+    mlp_low = (normed * mlp_gain + mlp_shift).astype(jnp.bfloat16)
+
     cosine, sine = rotary_tables(segment)
     projected = jnp.dot(attn_low, w_qkv, preferred_element_type=jnp.float32) + b_qkv
     grouped = projected.reshape(count_seq, seq_len, local_heads, 3, HD)
@@ -133,21 +200,35 @@
     attended = (
         jnp.concatenate(outputs, axis=1).astype(jnp.bfloat16).reshape(rows_here, local_heads * HD)
     )
-    attn_part = jnp.dot(attended, w_out, preferred_element_type=jnp.float32)
+
     pre_act = jnp.dot(mlp_low, w_up, preferred_element_type=jnp.float32) + b_up
-    hidden = jax.nn.gelu(pre_act, approximate=False).astype(jnp.bfloat16)
-    mlp_part = jnp.dot(hidden, w_down, preferred_element_type=jnp.float32)
-    branches = lax.psum(attn_part + mlp_part, "tensor")
-    result = (token_rows + branches + b_branch).astype(jnp.bfloat16)
-    grad_down = inner_rows(hidden, cotangent)
-    grad_out = inner_rows(attended, cotangent)
+    phi_sum = 0.5 * (1.0 + lax.erf(pre_act * (0.5**0.5)))
+    hidden = (pre_act * phi_sum).astype(jnp.bfloat16)
+    slope = phi_sum + pre_act * jnp.exp(-0.5 * pre_act * pre_act) * ((2.0 * math.pi) ** -0.5)
+
+    split = rows_here // 2
+    result = jnp.zeros((rows_here, width), jnp.bfloat16)
+    for part, order in enumerate(orders):
+        rows = slice(part * split, (part + 1) * split)
+        partial = jnp.dot(attended[rows], w_out, preferred_element_type=jnp.float32) + jnp.dot(
+            hidden[rows], w_down, preferred_element_type=jnp.float32
+        )
+        mine, _ = scatter_sum(partial, tensor_size, order)
+        for piece, first in gather_back(mine, tensor_size, order):
+            at = first + part * split
+            its_tokens = lax.dynamic_slice_in_dim(tokens, at, piece.shape[0], 0)
+            done = (its_tokens.astype(jnp.float32) + piece + b_branch).astype(jnp.bfloat16)
+            result = lax.dynamic_update_slice_in_dim(result, done, at, 0)
+
+    grad_down = dp_sum(inner_rows(hidden, cotangent), dp_size, 2)
+    d_pre_wide = times_trans(cotangent, w_down) * slope
+    d_pre = d_pre_wide.astype(jnp.bfloat16)
+    grad_up = dp_sum(inner_rows(mlp_low, d_pre), dp_size, 2)
+    grad_up_bias = jnp.sum(d_pre.astype(jnp.float32), axis=0)
     branch_grad = jnp.sum(cotangent.astype(jnp.float32), axis=0)
-    d_hidden = times_trans(cotangent, w_down)
-    gelu_pull = jax.vjp(lambda pre_value: jax.nn.gelu(pre_value, approximate=False), pre_act)[1]
-    d_pre = gelu_pull(d_hidden)[0].astype(jnp.bfloat16)
-    grad_up = inner_rows(mlp_low, d_pre)
-    grad_up_bias = jnp.sum(d_pre.astype(jnp.float32), axis=0)
     d_mlp_in = times_trans(d_pre, w_up)
+    grad_out = dp_sum(inner_rows(attended, cotangent), dp_size, 1)
+
     d_attended = (
         times_trans(cotangent, w_out)
         .astype(jnp.bfloat16)
@@ -190,46 +271,64 @@
         .reshape(rows_here, local_heads * 3 * HD)
         .astype(jnp.bfloat16)
     )
+    d_attn_in = times_trans(d_projected, w_qkv)
+
+    scaled = d_attn_in * attn_gain + d_mlp_in * mlp_gain
+    d_tokens = jnp.zeros((rows_here, width), jnp.float32)
+    for part, order in enumerate(orders):
+        rows = slice(part * split, (part + 1) * split)
+        mine, first = scatter_sum(scaled[rows], tensor_size, order)
+        at = first + part * split
+
+        def here(whole, at=at, count=mine.shape[0]):
+            return lax.dynamic_slice_in_dim(whole, at, count, 0)
+
+        normed_here = here(normed)
+        back = here(cotangent).astype(jnp.float32) + here(scale_inv) * (
+            mine
+            - jnp.mean(mine, axis=-1, keepdims=True)
+            - normed_here * jnp.mean(mine * normed_here, axis=-1, keepdims=True)
+        )
+        for piece, its_first in gather_back(back, tensor_size, order):
+            d_tokens = lax.dynamic_update_slice_in_dim(
+                d_tokens, piece, its_first + part * split, 0
+            )
     grad_qkv = inner_rows(attn_low, d_projected)
     grad_qkv_bias = jnp.sum(d_projected.astype(jnp.float32), axis=0)
-    d_attn_in = times_trans(d_projected, w_qkv)
-    sum_attn, sum_mlp = lax.psum((d_attn_in, d_mlp_in), "tensor")
-    d_tokens = (
-        cotangent.astype(jnp.float32)
-        + norm_back(sum_attn, attn_normed, attn_inv, attn_gain)
-        + norm_back(sum_mlp, mlp_normed, mlp_inv, mlp_gain)
-    )
-    attn_g, attn_s = norm_stats(sum_attn, attn_normed)
-    mlp_g, mlp_s = norm_stats(sum_mlp, mlp_normed)
-    layer_stats = jnp.stack([attn_g, attn_s, mlp_g, mlp_s])
-    summed = lax.psum(
-        (
-            grad_qkv,
-            grad_qkv_bias,
-            grad_out,
-            grad_up,
-            grad_up_bias,
-            grad_down,
-            branch_grad,
-            layer_stats,
-        ),
-        "dp",
-    )
-    total_stats = summed[7]
+    grad_qkv = dp_sum(grad_qkv, dp_size, 2)
+
+    stats = jnp.stack(
+        [
+            jnp.sum(d_attn_in * normed, axis=0),
+            jnp.sum(d_attn_in, axis=0),
+            jnp.sum(d_mlp_in * normed, axis=0),
+            jnp.sum(d_mlp_in, axis=0),
+        ]
+    )
+    stats = small_sum(stats, tensor_size, "tensor")
+    vectors = jnp.concatenate(
+        [stats.reshape(-1), grad_qkv_bias, grad_up_bias, branch_grad]
+    )
+    vectors = small_sum(vectors, dp_size, "dp")
+    sizes = (width,) * 4 + (grad_qkv_bias.shape[0], grad_up_bias.shape[0], width)
+    ends = [sum(sizes[: k + 1]) for k in range(len(sizes))]
+    a_gain, a_shift, m_gain, m_shift, qkv_bias, up_bias, branch = (
+        vectors[end - size : end] for end, size in zip(ends, sizes, strict=True)
+    )
     return (
         result,
         d_tokens,
-        summed[0],
-        summed[1],
-        summed[2],
-        summed[3],
-        summed[4],
-        summed[5],
-        summed[6],
-        total_stats[0],
-        total_stats[1],
-        total_stats[2],
-        total_stats[3],
+        grad_qkv,
+        qkv_bias,
+        grad_out,
+        grad_up,
+        up_bias,
+        grad_down,
+        branch,
+        a_gain,
+        a_shift,
+        m_gain,
+        m_shift,
     )
 
 
@@ -250,8 +349,12 @@
         P(),
         P("dp", None),
     )
+
+    def body(*arrays):
+        return shards(mesh.shape["dp"], mesh.shape["tensor"], *arrays)
+
     return jax.shard_map(
-        shards,
+        body,
         mesh=mesh,
         in_specs=placed,
         out_specs=(

time: 617 us -> 506 us (0.82)
  waiting for transfers between devices: 438 us -> 178 us
  starting transfers between devices: 0.25 us -> 87.8 us
  local copies, waits for them, and re-layouts: 20.9 us -> 82.8 us
  other arithmetic: 33.5 us -> 74.2 us
  blocking collectives: 31.2 us -> 0 us
  between operations: 14.9 us -> 2.82 us
    psum x2 -> x0, waiting for transfers between devices: 438 us -> none  [the longest x1 225 us: shards(): branches = lax.psum(attn_part + mlp_part, 'tensor')]
    ppermute x0 -> x61, waiting for transfers between devices: none -> 178 us  [the longest x24 159 us: send(): lax.ppermute(what, 'dp', [(2 * a + c, 2 * b + c) for a, b in pairs for c...]
    ppermute x0 -> x61, starting transfers between devices: none -> 87.8 us  [the longest x24 59.7 us: send(): lax.ppermute(what, 'dp', [(2 * a + c, 2 * b + c) for a, b in pairs for c...]
    psum x1 -> x0, blocking collectives: 31.2 us -> none  [shards(): lax.psum((grad_qkv, grad_qkv_bias, grad_out, grad_up, grad_up_bias, grad_...]
    dynamic_update_slice x0 -> x15, other arithmetic: none -> 25.5 us  [the longest x8 14.8 us: shards(): result = lax.dynamic_update_slice_in_dim(result, done, at, 0)]
    add x0 -> x27, other arithmetic: none -> 25.5 us  [the longest x8 8.84 us: line_sum(): array = array + send(array, [(s, s + 1), (chips - 1 - s, chips - 2 - s)])]
    dynamic_update_slice x0 -> x15, local copies, waits for them, and re-layouts: none -> 17.2 us  [the longest x8 13.1 us: shards(): lax.dynamic_update_slice_in_dim(d_tokens, piece, its_first + part * split...]
    dynamic_slice x0 -> x13, local copies, waits for them, and re-layouts: none -> 16.1 us  [the longest x8 10.2 us: scatter_sum(): away = lax.dynamic_slice_in_dim(array, (1 - mine) * half, half, 0)]
  transfers between devices with their start and end apart: 2 -> 61, of which waited for: 2 -> 17; matrix products, arithmetic and copies ran while one was open for 5% -> 39% of each run, Pallas kernels for 0% -> 0%
where the time goes in v1:
time: 506 us; the launch traced here: 497 us
  waiting for transfers between devices  178 us (35%)
  starting transfers between devices  87.8 us (17%)
  local copies, waits for them, and re-layouts  82.8 us (16%)
  other arithmetic  74.2 us (15%)
  matrix products  71 us (14%)
    ppermute x24, waiting for transfers between devices, send(): lax.ppermute(what, 'dp', [(2 * a + c, 2 * b + c) for a, b in pairs for c...  159 us
    ppermute x24, starting transfers between devices, send(): lax.ppermute(what, 'dp', [(2 * a + c, 2 * b + c) for a, b in pairs for c...  59.7 us
    ppermute x37, starting transfers between devices, swap(): return lax.ppermute(array, axis, [(i, i ^ bit) for i in range(size)])  28.1 us
    unnamed x194, local copies, waits for them, and re-layouts  25 us
    ppermute x37, waiting for transfers between devices, swap(): return lax.ppermute(array, axis, [(i, i ^ bit) for i in range(size)])  19.4 us
    dot_general x4, matrix products, times_trans(): lax.dot_general(first_mat, second_mat, (((1,), (1,)), ((), ())), preferre...  16.7 us
    dynamic_update_slice x8, other arithmetic, shards(): result = lax.dynamic_update_slice_in_dim(result, done, at, 0)  14.8 us
    dynamic_update_slice x8, local copies, waits for them, and re-layouts, shards(): lax.dynamic_update_slice_in_dim(d_tokens, piece, its_first + part * split...  13.1 us
  transfers between devices with their start and end apart: 61, of which 17 were waited for; matrix products, arithmetic and copies ran while one was open for 39% of the time, Pallas kernels for 0%

profile of v1, /device:TPU:0, one launch (start us, length us, event | category | flops | bytes accessed | tf_op | source)
XLA Modules:
  0.0 496.9 jit_solution(10174750239804701137)
XLA Ops:
  9.0 5.0 %multiply_convert_fusion.2 = (bf16[1024,1024]{1,0:T(8,128)(2,1)S(1)}, f32[1024,1024]{1,0:T(8,128)S(1)}) fusion(f32[1024]{0:T(1024)S(1)} %copy-done.77, bf16[1024,1024]{1,0:T(8,128)(2,1)S(1)} %copy-done, bf16[1024,1024]{0,1:T(8,128)(2,1)} %copy.72, f32[1024]{0:T(1024)S(1)} %copy-done.78, f32[1024]{0:T(1024)S(1)} %copy-done.80, f32[1024]{0:T(1024)S(1)} %add_rsqrt_fusion, ...), kind=kOutput, calls=%fused_computation.37 | convolution fusion | flops 2160066560 | bytes 10506240 | tf_op jit(solution)/shard_map/dot_general | solution.py:204
  19.6 4.5 convert_reduce_fusion.2
  59.9 8.4 %multiply_reduce_fusion.1 = (f32[4,512]{1,0:T(4,128)S(1)}, f32[4,512,1024]{2,1,0:T(8,128)}) fusion(f32[4,512,1024]{2,1,0:T(8,128)} %copy-done.2, f32[4,512]{1,0:T(4,128)S(1)} %log_add_fusion.1, bf16[1,1024,4,64]{1,3,2,0:T(8,128)(2,1)S(1)} %bitcast.121, f32[1,1024,4,3,64]{1,4,3,2,0:T(8,128)S(1)} %bitcast.119), kind=kOutput, calls=%fused_computation.4 | convolution fusion | flops 274724864 | bytes 17580032 | tf_op jit(solution)/shard_map/nqhd,nkhd->nhqk/dot_general | solution.py:245
  68.3 5.2 %multiply_convert_fusion.1 = bf16[4,512,1024]{2,1,0:T(8,128)(2,1)S(1)} fusion(f32[4,512,1024]{2,1,0:T(8,128)} %get-tuple-element.98, f32[4,512,1024]{2,1,0:T(8,128)S(1)} %bitcast.113, f32[4,512]{1,0:T(4,128)S(1)} %get-tuple-element.97, f32[4,512]{1,0:T(4,128)S(1)} %log_add_fusion.1), kind=kLoop, calls=%fused_computation.3 | loop fusion | flops 8388608 | bytes 20987904 | tf_op jit(solution)/shard_map/convert_element_type | solution.py:249
  75.8 4.4 multiply_reduce_fusion
  82.9 4.4 fusion.78
  87.2 4.8 multiply_convert_fusion
  99.7 5.4 %multiply_reduce_fusion.3 = (f32[1024]{0:T(1024)S(1)}, f32[1024]{0:T(1024)S(1)}, f32[1024]{0:T(1024)S(1)}, f32[1024]{0:T(1024)S(1)}, f32[1024,1024]{0,1:T(8,128)}, /*index=5*/f32[1024,1024]{0,1:T(8,128)}) fusion(bf16[1024,1024]{0,1:T(8,128)(2,1)S(1)} %copy-done.5, f32[1024]{0:T(1024)S(1)} %copy-done.73, f32[1024]{0:T(1024)S(1)} %copy-done.70, ...), kind=kOutput, calls=%fused_computation.33 | convolution fusion | flops 1623191552 | bytes 17858560 | tf_op jit(solution)/shard_map/dot_general | solution.py:22
  146.3 4.9 collective-permute-done.35
  166.6 12.7 %collective-permute-done.52 = f32[256,1024]{1,0:T(8,128)} collective-permute-done((f32[256,1024]{1,0:T(8,128)}, f32[256,1024]{1,0:T(8,128)}, u32[]{:S(2)}, u32[]{:S(2)}) %collective-permute-start.52) | collective-permute-done | bytes 1048608 | tf_op jit(solution)/shard_map/ppermute | solution.py:90
  179.3 4.4 collective-permute-start.37
  190.7 22.2 %collective-permute-done.37 = f32[128,1024]{1,0:T(8,128)S(1)} collective-permute-done((f32[128,1024]{1,0:T(8,128)S(1)}, f32[128,1024]{1,0:T(8,128)S(1)}, u32[]{:S(2)}, u32[]{:S(2)}) %collective-permute-start.37) | collective-permute-done | bytes 524320 | tf_op jit(solution)/shard_map/ppermute | solution.py:90
  216.6 9.7 %collective-permute-done.21 = f32[256,768]{1,0:T(8,128)S(1)} collective-permute-done((f32[256,768]{1,0:T(8,128)S(1)}, f32[256,768]{1,0:T(8,128)S(1)}, u32[]{:S(2)}, u32[]{:S(2)}) %collective-permute-start.21) | collective-permute-done | bytes 786464 | tf_op jit(solution)/shard_map/ppermute | solution.py:90
  235.2 25.1 %collective-permute-done.54 = f32[256,1024]{1,0:T(8,128)S(1)} collective-permute-done((f32[256,1024]{1,0:T(8,128)S(1)}, f32[256,1024]{1,0:T(8,128)S(1)}, u32[]{:S(2)}, u32[]{:S(2)}) %collective-permute-start.54) | collective-permute-done | bytes 1048608 | tf_op jit(solution)/shard_map/ppermute | solution.py:90
  268.4 6.8 %collective-permute-done.1 = f32[128,1024]{1,0:T(8,128)S(1)} collective-permute-done((f32[128,1024]{1,0:T(8,128)S(1)}, f32[128,1024]{1,0:T(8,128)S(1)}, u32[]{:S(2)}, u32[]{:S(2)}) %collective-permute-start.1) | collective-permute-done | bytes 524320 | tf_op jit(solution)/shard_map/ppermute | solution.py:49
  276.5 17.7 %collective-permute-done.23 = f32[256,768]{1,0:T(8,128)S(1)} collective-permute-done((f32[256,768]{1,0:T(8,128)S(1)}, f32[256,768]{1,0:T(8,128)S(1)}, u32[]{:S(2)}, u32[]{:S(2)}) %collective-permute-start.23) | collective-permute-done | bytes 786464 | tf_op jit(solution)/shard_map/ppermute | solution.py:90
  294.2 20.9 %collective-permute-start.57 = (f32[256,1024]{1,0:T(8,128)S(1)}, f32[256,1024]{1,0:T(8,128)}, u32[]{:S(2)}, u32[]{:S(2)}) collective-permute-start(f32[256,1024]{1,0:T(8,128)S(1)} %get-tuple-element.49), channel_id=1, source_target_pairs={{0,8},{4,12},{24,16},{28,20},{1,9},{5,13},{25,17},{29,21},{2,10},{... | collective-permute-start | bytes 3145736 | tf_op jit(solution)/shard_map/ppermute | solution.py:90
  322.4 5.1 %collective-permute-done.39 = f32[128,1024]{1,0:T(8,128)S(1)} collective-permute-done((f32[128,1024]{1,0:T(8,128)S(1)}, f32[128,1024]{1,0:T(8,128)S(1)}, u32[]{:S(2)}, u32[]{:S(2)}) %collective-permute-start.39) | collective-permute-done | bytes 524320 | tf_op jit(solution)/shard_map/ppermute | solution.py:90
  336.6 4.7 collective-permute-done.17
  361.6 13.8 %collective-permute-done.47 = f32[256,1024]{1,0:T(8,128)} collective-permute-done((f32[256,1024]{1,0:T(8,128)}, f32[256,1024]{1,0:T(8,128)}, u32[]{:S(2)}, u32[]{:S(2)}) %collective-permute-start.47) | collective-permute-done | bytes 1048608 | tf_op jit(solution)/shard_map/ppermute | solution.py:90
  430.2 6.8 %collective-permute-done.7 = f32[128,1024]{1,0:T(8,128)S(1)} collective-permute-done((f32[128,1024]{1,0:T(8,128)S(1)}, f32[128,1024]{1,0:T(8,128)S(1)}, u32[]{:S(2)}, u32[]{:S(2)}) %collective-permute-start.7) | collective-permute-done | bytes 524320 | tf_op jit(solution)/shard_map/ppermute | solution.py:49
  437.7 4.1 collective-permute-done.28
  442.6 21.7 %collective-permute-done.59 = f32[256,1024]{1,0:T(8,128)S(1)} collective-permute-done((f32[256,1024]{1,0:T(8,128)S(1)}, f32[256,1024]{1,0:T(8,128)S(1)}, u32[]{:S(2)}, u32[]{:S(2)}) %collective-permute-start.59) | collective-permute-done | bytes 1048608 | tf_op jit(solution)/shard_map/ppermute | solution.py:90
  464.6 21.2 %collective-permute-done.49 = f32[256,1024]{1,0:T(8,128)S(1)} collective-permute-done((f32[256,1024]{1,0:T(8,128)S(1)}, f32[256,1024]{1,0:T(8,128)S(1)}, u32[]{:S(2)}, u32[]{:S(2)}) %collective-permute-start.49) | collective-permute-done | bytes 1048608 | tf_op jit(solution)/shard_map/ppermute | solution.py:90
  (446 shorter events, 250.3 us)
Async XLA Ops:
  18.0 124.2 %collective-permute-start.51 = (f32[256,1024]{1,0:T(8,128)}, f32[256,1024]{1,0:T(8,128)}, u32[]{:S(2)}, u32[]{:S(2)}) collective-permute-start(f32[256,1024]{1,0:T(8,128)} %get-tuple-element.51), channel_id=1, source_target_pairs={{0,4},{4,0},{8,12},{12,8},{16,20},{20,16},{24,28},{28,24},{1,5},{5... | collective-permute-start | bytes 3145736 | tf_op jit(solution)/shard_map/ppermute | solution.py:49
  30.2 130.3 %collective-permute-start.41 = (f32[256,1024]{1,0:T(8,128)}, f32[256,1024]{1,0:T(8,128)}, u32[]{:S(2)}, u32[]{:S(2)}) collective-permute-start(f32[256,1024]{1,0:T(8,128)} %get-tuple-element.54), channel_id=1, source_target_pairs={{0,4},{4,0},{8,12},{12,8},{16,20},{20,16},{24,28},{28,24},{1,5},{5... | collective-permute-start | bytes 3145736 | tf_op jit(solution)/shard_map/ppermute | solution.py:49
  56.1 96.4 %collective-permute-start.36 = (f32[128,1024]{1,0:T(8,128)}, f32[128,1024]{1,0:T(8,128)}, u32[]{:S(2)}, u32[]{:S(2)}) collective-permute-start(f32[128,1024]{1,0:T(8,128)} %constant_dynamic-slice_fusion.3), channel_id=1, source_target_pairs={{0,4},{4,0},{8,12},{12,8},{16,20},{20,16},{24,28},{28,24},{1,5},{5... | collective-permute-start | bytes 1572872 | tf_op jit(solution)/shard_map/ppermute | solution.py:49
  112.7 51.1 %collective-permute-start.20 = (f32[256,768]{1,0:T(8,128)}, f32[256,768]{1,0:T(8,128)}, u32[]{:S(2)}, u32[]{:S(2)}) collective-permute-start(f32[256,768]{1,0:T(8,128)} %get-tuple-element.61), channel_id=1, source_target_pairs={{0,4},{4,0},{8,12},{12,8},{16,20},{20,16},{24,28},{28,24},{1,5},{5... | collective-permute-start | bytes 2359304 | tf_op jit(solution)/shard_map/ppermute | solution.py:49
  141.7 43.7 %collective-permute-start.10 = (f32[256,1024]{0,1:T(8,128)}, f32[256,1024]{0,1:T(8,128)}, u32[]{:S(2)}, u32[]{:S(2)}) collective-permute-start(f32[256,1024]{0,1:T(8,128)} %constant_dynamic-slice_fusion.10), channel_id=1, source_target_pairs={{0,1},{1,0},{2,3},{3,2},{4,5},{5,4},{6,7},{7,6},{8,9},{9,8},{10,11... | collective-permute-start | bytes 3145736 | tf_op jit(solution)/shard_map/ppermute | solution.py:49
  160.5 53.1 %collective-permute-start = (f32[256,1024]{1,0:T(8,128)}, f32[256,1024]{1,0:T(8,128)S(1)}, u32[]{:S(2)}, u32[]{:S(2)}) collective-permute-start(f32[256,1024]{1,0:T(8,128)} %constant_dynamic-slice_fusion.16), channel_id=1, source_target_pairs={{0,1},{1,0},{2,3},{3,2},{4,5},{5,4},{6,7},{7,6},{8,9},{9,8},{10,11... | collective-permute-start | bytes 3145736 | tf_op jit(solution)/shard_map/ppermute | solution.py:49
  163.7 49.9 %collective-permute-start.42 = (f32[256,1024]{1,0:T(8,128)S(1)}, f32[256,1024]{1,0:T(8,128)S(1)}, u32[]{:S(2)}, u32[]{:S(2)}) collective-permute-start(f32[256,1024]{1,0:T(8,128)S(1)} %dynamic-slice_add_fusion.3), channel_id=1, source_target_pairs={{0,8},{4,12},{24,16},{28,20},{1,9},{5,13},{25,17},{29,21},{2,10},{... | collective-permute-start | bytes 3145736 | tf_op jit(solution)/shard_map/ppermute | solution.py:90
  185.4 40.9 %collective-permute-start.21 = (f32[256,768]{1,0:T(8,128)S(1)}, f32[256,768]{1,0:T(8,128)S(1)}, u32[]{:S(2)}, u32[]{:S(2)}) collective-permute-start(f32[256,768]{1,0:T(8,128)S(1)} %dynamic-slice_add_fusion.9), channel_id=1, source_target_pairs={{0,8},{4,12},{24,16},{28,20},{1,9},{5,13},{25,17},{29,21},{2,10},{... | collective-permute-start | bytes 2359304 | tf_op jit(solution)/shard_map/ppermute | solution.py:90
  186.9 40.6 %collective-permute-start.53 = (f32[256,1024]{1,0:T(8,128)S(1)}, f32[256,1024]{1,0:T(8,128)S(1)}, u32[]{:S(2)}, u32[]{:S(2)}) collective-permute-start(f32[256,1024]{1,0:T(8,128)S(1)} %add.691), channel_id=1, source_target_pairs={{8,16},{12,20},{16,8},{20,12},{9,17},{13,21},{17,9},{21,13},{10,18... | collective-permute-start | bytes 3145736 | tf_op jit(solution)/shard_map/ppermute | solution.py:90
  232.6 61.7 %collective-permute-start.23 = (f32[256,768]{1,0:T(8,128)S(1)}, f32[256,768]{1,0:T(8,128)S(1)}, u32[]{:S(2)}, u32[]{:S(2)}) collective-permute-start(f32[256,768]{1,0:T(8,128)S(1)} %add.666), channel_id=1, source_target_pairs={{8,0},{12,4},{16,24},{20,28},{9,1},{13,5},{17,25},{21,29},{10,2},{... | collective-permute-start | bytes 2359304 | tf_op jit(solution)/shard_map/ppermute | solution.py:90
  233.9 82.8 %collective-permute-start.44 = (f32[256,1024]{1,0:T(8,128)S(1)}, f32[256,1024]{1,0:T(8,128)S(1)}, u32[]{:S(2)}, u32[]{:S(2)}) collective-permute-start(f32[256,1024]{1,0:T(8,128)S(1)} %add.686), channel_id=1, source_target_pairs={{8,0},{12,4},{16,24},{20,28},{9,1},{13,5},{17,25},{21,29},{10,2},{... | collective-permute-start | bytes 3145736 | tf_op jit(solution)/shard_map/ppermute | solution.py:90
  265.6 63.4 %collective-permute-start.12 = (f32[128,1024]{0,1:T(8,128)S(1)}, f32[128,1024]{0,1:T(8,128)S(1)}, u32[]{:S(2)}, u32[]{:S(2)}) collective-permute-start(f32[128,1024]{0,1:T(8,128)S(1)} %get-tuple-element.56), channel_id=1, source_target_pairs={{0,2},{1,3},{2,0},{3,1},{4,6},{5,7},{6,4},{7,5},{8,10},{9,11},{10,... | collective-permute-start | bytes 1572872 | tf_op jit(solution)/shard_map/ppermute | solution.py:49
  266.9 63.4 %collective-permute-start.13 = (f32[128,1024]{0,1:T(8,128)S(1)}, f32[128,1024]{0,1:T(8,128)S(1)}, u32[]{:S(2)}, u32[]{:S(2)}) collective-permute-start(f32[128,1024]{0,1:T(8,128)S(1)} %get-tuple-element.56), channel_id=1, source_target_pairs={{0,1},{1,0},{2,3},{3,2},{4,5},{5,4},{6,7},{7,6},{8,9},{9,8},{10,11... | collective-permute-start | bytes 1572872 | tf_op jit(solution)/shard_map/ppermute | solution.py:49
  275.2 52.3 %collective-permute-start.39 = (f32[128,1024]{1,0:T(8,128)S(1)}, f32[128,1024]{1,0:T(8,128)S(1)}, u32[]{:S(2)}, u32[]{:S(2)}) collective-permute-start(f32[128,1024]{1,0:T(8,128)S(1)} %add.683), channel_id=1, source_target_pairs={{8,0},{12,4},{16,24},{20,28},{9,1},{13,5},{17,25},{21,29},{10,2},{... | collective-permute-start | bytes 1572872 | tf_op jit(solution)/shard_map/ppermute | solution.py:90
  294.2 52.1 %collective-permute-start.57 = (f32[256,1024]{1,0:T(8,128)S(1)}, f32[256,1024]{1,0:T(8,128)}, u32[]{:S(2)}, u32[]{:S(2)}) collective-permute-start(f32[256,1024]{1,0:T(8,128)S(1)} %get-tuple-element.49), channel_id=1, source_target_pairs={{0,8},{4,12},{24,16},{28,20},{1,9},{5,13},{25,17},{29,21},{2,10},{... | collective-permute-start | bytes 3145736 | tf_op jit(solution)/shard_map/ppermute | solution.py:90
  316.7 38.0 %collective-permute-start.26 = (f32[256,768]{1,0:T(8,128)}, f32[256,768]{1,0:T(8,128)}, u32[]{:S(2)}, u32[]{:S(2)}) collective-permute-start(f32[256,768]{1,0:T(8,128)} %get-tuple-element.59), channel_id=1, source_target_pairs={{0,8},{4,12},{24,16},{28,20},{1,9},{5,13},{25,17},{29,21},{2,10},{... | collective-permute-start | bytes 2359304 | tf_op jit(solution)/shard_map/ppermute | solution.py:90
  330.4 45.0 %collective-permute-start.47 = (f32[256,1024]{1,0:T(8,128)}, f32[256,1024]{1,0:T(8,128)}, u32[]{:S(2)}, u32[]{:S(2)}) collective-permute-start(f32[256,1024]{1,0:T(8,128)} %get-tuple-element.52), channel_id=1, source_target_pairs={{0,8},{4,12},{24,16},{28,20},{1,9},{5,13},{25,17},{29,21},{2,10},{... | collective-permute-start | bytes 3145736 | tf_op jit(solution)/shard_map/ppermute | solution.py:90
  344.8 36.7 %collective-permute-start.3 = (f32[128,1024]{1,0:T(8,128)}, f32[128,1024]{1,0:T(8,128)}, u32[]{:S(2)}, u32[]{:S(2)}) collective-permute-start(f32[128,1024]{1,0:T(8,128)} %get-tuple-element.47), channel_id=1, source_target_pairs={{0,1},{1,0},{2,3},{3,2},{4,5},{5,4},{6,7},{7,6},{8,9},{9,8},{10,11... | collective-permute-start | bytes 1572872 | tf_op jit(solution)/shard_map/ppermute | solution.py:49
  354.7 50.2 %collective-permute-start.58 = (f32[256,1024]{1,0:T(8,128)S(1)}, f32[256,1024]{1,0:T(8,128)}, u32[]{:S(2)}, u32[]{:S(2)}) collective-permute-start(f32[256,1024]{1,0:T(8,128)S(1)} %add.694), channel_id=1, source_target_pairs={{8,16},{12,20},{16,8},{20,12},{9,17},{13,21},{17,9},{21,13},{10,18... | collective-permute-start | bytes 3145736 | tf_op jit(solution)/shard_map/ppermute | solution.py:90
  418.4 45.9 %collective-permute-start.59 = (f32[256,1024]{1,0:T(8,128)S(1)}, f32[256,1024]{1,0:T(8,128)S(1)}, u32[]{:S(2)}, u32[]{:S(2)}) collective-permute-start(f32[256,1024]{1,0:T(8,128)S(1)} %add.695), channel_id=1, source_target_pairs={{8,0},{12,4},{16,24},{20,28},{9,1},{13,5},{17,25},{21,29},{10,2},{... | collective-permute-start | bytes 3145736 | tf_op jit(solution)/shard_map/ppermute | solution.py:90
  424.2 61.7 %collective-permute-start.49 = (f32[256,1024]{1,0:T(8,128)S(1)}, f32[256,1024]{1,0:T(8,128)S(1)}, u32[]{:S(2)}, u32[]{:S(2)}) collective-permute-start(f32[256,1024]{1,0:T(8,128)S(1)} %add.689), channel_id=1, source_target_pairs={{8,0},{12,4},{16,24},{20,28},{9,1},{13,5},{17,25},{21,29},{10,2},{... | collective-permute-start | bytes 3145736 | tf_op jit(solution)/shard_map/ppermute | solution.py:90
  428.8 57.2 %collective-permute-start.40 = (f32[128,1024]{1,0:T(8,128)S(1)}, f32[128,1024]{1,0:T(8,128)S(1)}, u32[]{:S(2)}, u32[]{:S(2)}) collective-permute-start(f32[128,1024]{1,0:T(8,128)S(1)} %copy-done.60), channel_id=1, source_target_pairs={{0,4},{4,0},{8,12},{12,8},{16,20},{20,16},{24,28},{28,24},{1,5},{5... | collective-permute-start | bytes 1572872 | tf_op jit(solution)/shard_map/ppermute | solution.py:49
  437.0 51.7 %collective-permute-start.8 = (f32[128,1024]{1,0:T(8,128)S(1)}, f32[128,1024]{1,0:T(8,128)S(1)}, u32[]{:S(2)}, u32[]{:S(2)}) collective-permute-start(f32[128,1024]{1,0:T(8,128)S(1)} %get-tuple-element.45), channel_id=1, source_target_pairs={{0,2},{1,3},{2,0},{3,1},{4,6},{5,7},{6,4},{7,5},{8,10},{9,11},{10,... | collective-permute-start | bytes 1572872 | tf_op jit(solution)/shard_map/ppermute | solution.py:49
  441.8 48.7 %collective-permute-start.9 = (f32[128,1024]{1,0:T(8,128)S(1)}, f32[128,1024]{1,0:T(8,128)S(1)}, u32[]{:S(2)}, u32[]{:S(2)}) collective-permute-start(f32[128,1024]{1,0:T(8,128)S(1)} %collective-permute-done.7), channel_id=1, source_target_pairs={{0,2},{1,3},{2,0},{3,1},{4,6},{5,7},{6,4},{7,5},{8,10},{9,11},{10,... | collective-permute-start | bytes 1572872 | tf_op jit(solution)/shard_map/ppermute | solution.py:49
  (132 other events, 1654.7 us)

commit v2 on v0

v2 whole, which is shorter than its diff:
```python
import functools
import math

import jax
import jax.numpy as jnp
from jax import lax
from jax.experimental import pallas as pl
from jax.experimental.pallas import tpu as pltpu
from jax.sharding import PartitionSpec as P

HD = 64
ROT = 16
MOST = 512

EPS = 1e-05
NEG = -1e30


def inner_rows(first_mat, second_mat):
    return lax.dot_general(
        first_mat, second_mat, (((0,), (0,)), ((), ())), preferred_element_type=jnp.float32
    )


def times_trans(first_mat, second_mat):
    return lax.dot_general(
        first_mat, second_mat, (((1,), (1,)), ((), ())), preferred_element_type=jnp.float32
    )


def product(first_mat, second_mat):
    return jnp.dot(first_mat, second_mat, preferred_element_type=jnp.float32)


def turn_angles(segment):
    spots = lax.broadcasted_iota(jnp.int32, segment.shape, 0)
    starts = jnp.zeros_like(segment)
    for number in range(3):
        count = jnp.sum((segment == number).astype(jnp.int32))
        starts = starts + jnp.where(segment > number, count, 0)
    offsets = (spots - starts).astype(jnp.float32)
    frequency = 10000.0 ** (-2.0 * jnp.arange(ROT // 2, dtype=jnp.float32) / ROT)
    angles = frequency[:, None] * offsets[None, :]
    number = jnp.broadcast_to(segment.astype(jnp.float32), (8, segment.shape[0]))
    return jnp.concatenate([jnp.cos(angles), jnp.sin(angles), number], axis=0)


def spread(angles, rows, take):
    return lax.dot_general(
        angles[0 : take.shape[0], rows],
        take,
        (((0,), (0,)), ((), ())),
        precision=lax.Precision.HIGHEST,
        preferred_element_type=jnp.float32,
    )


def turn_tables(angles, rows):
    tile, half = 2 * HD, ROT // 2
    source = lax.broadcasted_iota(jnp.int32, (ROT, tile), 0)
    column = lax.broadcasted_iota(jnp.int32, (ROT, tile), 1) % HD
    take_cos = ((source == column % half) & (column < ROT)).astype(jnp.float32)
    take_sin = source == column % half + half
    take_low = -(take_sin & (column < half)).astype(jnp.float32)
    take_high = (take_sin & (column >= half) & (column < ROT)).astype(jnp.float32)
    lane = lax.broadcasted_iota(jnp.int32, (rows.stop - rows.start, tile), 1)
    still = (lane % HD >= ROT).astype(jnp.float32)
    return (
        spread(angles, rows, take_cos) + still,
        spread(angles, rows, take_low),
        spread(angles, rows, take_high),
    )


def turn(wide, number, turned, low, high):
    tile, half = 2 * HD, ROT // 2
    lane = lax.broadcasted_iota(jnp.int32, wide.shape, 1)
    moved = (
        wide * turned
        + pltpu.roll(wide, tile - half, 1) * low
        + pltpu.roll(wide, half, 1) * high
    )
    if 2 * number % 3 == 2:
        return jnp.where(lane < HD, wide, moved)
    if (2 * number + 1) % 3 == 2:
        return jnp.where(lane >= HD, wide, moved)
    return moved


def key_range(start, block):
    return max(0, start - -(-MOST // block) * block), start + block


def fill_bias(bias, angles, start, block):
    first, until = key_range(start, block)
    count = until - first
    source = lax.broadcasted_iota(jnp.int32, (ROT + 8, 2 * HD), 0)
    own = spread(angles, slice(start, until), (source == ROT).astype(jnp.float32))[:, :1]
    other = angles[ROT : ROT + 1, first:until]
    query_spot = lax.broadcasted_iota(jnp.int32, (block, count), 0) + start
    key_spot = lax.broadcasted_iota(jnp.int32, (block, count), 1) + first
    bias[:, :count] = jnp.where((own == other) & (key_spot <= query_spot), 0.0, NEG)


def attend_kernel(heads, angles, projected, attended, sums, q_s, k_s, v_s, bias):
    seq_len, lanes = projected.shape
    block = min(256, seq_len)
    tile = 2 * HD
    for start in range(0, seq_len, block):
        rows = slice(start, start + block)
        turned, low, high = turn_tables(angles, rows)
        for number in range(lanes // tile):
            wide = turn(
                projected[rows, number * tile : (number + 1) * tile], number, turned, low, high
            )
            for side in range(2):
                head, kind = divmod(2 * number + side, 3)
                if head < heads:
                    part = wide[:, side * HD : (side + 1) * HD].astype(jnp.bfloat16)
                    (q_s, k_s, v_s)[kind][head, rows, :] = (
                        part * HD ** (-0.5) if kind == 0 else part
                    )
    for start in range(0, seq_len, block):
        first, until = key_range(start, block)
        count = until - first
        rows, keys = slice(start, until), slice(first, until)
        fill_bias(bias, angles, start, block)
        outs = []
        for h in range(heads):
            scores = times_trans(q_s[h, rows, :], k_s[h, keys, :]) + bias[:, :count]
            most = jnp.max(scores, axis=-1, keepdims=True)
            exponent = jnp.exp(scores - most)
            total = jnp.sum(exponent, axis=-1, keepdims=True)
            probs = (exponent * (1.0 / total)).astype(jnp.bfloat16)
            sums[rows, h : h + 1] = most + jnp.log(total)
            outs.append(product(probs, v_s[h, keys, :]))
        attended[rows, :] = jnp.concatenate(outs, axis=1).astype(jnp.bfloat16)


def attend_back_kernel(
    begin, heads, angles, q_s, k_s, v_s, sums, attended, d_attended, d_projected, dq_s, dk_s, dv_s, bias
):
    seq_len, lanes = d_projected.shape
    block = min(256, seq_len)
    tile = 2 * HD
    for start in range(0, seq_len, block):
        first, until = key_range(start, block)
        count = until - first
        rows, keys = slice(start, until), slice(first, until)
        fill_bias(bias, angles, start, block)
        for h in range(heads):
            g = begin + h
            q, k, v = q_s[g, rows, :], k_s[g, keys, :], v_s[g, keys, :]
            d_out = d_attended[rows, g * HD : (g + 1) * HD]
            out = attended[rows, g * HD : (g + 1) * HD]
            probs = jnp.exp(times_trans(q, k) + (bias[:, :count] - sums[rows, g : g + 1]))
            row_dot = jnp.sum(
                out.astype(jnp.float32) * d_out.astype(jnp.float32), axis=-1, keepdims=True
            )
            d_scores = (probs * (times_trans(d_out, v) - row_dot)).astype(jnp.bfloat16)
            dq_s[h, rows, :] = product(d_scores, k) * HD ** (-0.5)
            d_k = inner_rows(q, d_scores)
            d_v = inner_rows(d_out, probs.astype(jnp.bfloat16))
            old = count - block
            if old:
                dk_s[h, :, first:start] += d_k[:, :old]
                dv_s[h, :, first:start] += d_v[:, :old]
            dk_s[h, :, rows] = d_k[:, old:]
            dv_s[h, :, rows] = d_v[:, old:]
    for start in range(0, seq_len, block):
        rows = slice(start, start + block)
        turned, low, high = turn_tables(angles, rows)

        def section(at, rows=rows):
            head, kind = divmod(at, 3)
            if head >= heads:
                return jnp.zeros((block, HD), jnp.float32)
            return dq_s[head, rows, :] if kind == 0 else (dk_s, dv_s)[kind - 1][head, :, rows].T

        for number in range(lanes // tile):
            wide = jnp.concatenate([section(2 * number), section(2 * number + 1)], axis=1)
            d_projected[rows, number * tile : (number + 1) * tile] = turn(
                wide, number, turned, -low, -high
            ).astype(jnp.bfloat16)


VMEM = pl.BlockSpec(memory_space=pltpu.VMEM)


def bias_held(block):
    return pltpu.VMEM((block, -(-MOST // block) * block + block), jnp.float32)


def attend(angles, projected, heads):
    seq_len = projected.shape[0]
    pairs = heads * seq_len * seq_len // 2
    shape = jax.ShapeDtypeStruct
    return pl.pallas_call(
        functools.partial(attend_kernel, heads),
        out_shape=(
            shape((seq_len, heads * HD), jnp.bfloat16),
            shape((seq_len, 2 * HD), jnp.float32),
        )
        + (shape((heads, seq_len, HD), jnp.bfloat16),) * 3,
        in_specs=[VMEM] * 2,
        out_specs=(VMEM,) * 5,
        scratch_shapes=[bias_held(min(256, seq_len))],
        compiler_params=pltpu.CompilerParams(vmem_limit_bytes=24 * 2**20),
        cost_estimate=pl.CostEstimate(
            flops=80 * pairs * HD, bytes_accessed=seq_len * seq_len * 8, transcendentals=pairs
        ),
    )(angles, projected)


def attend_back(angles, kept, d_attended, begin, heads, lanes):
    attended, sums, queries, keys, values = kept
    seq_len = attended.shape[0]
    pairs = heads * seq_len * seq_len // 2
    cross = pltpu.VMEM((heads, HD, seq_len), jnp.float32)
    return pl.pallas_call(
        functools.partial(attend_back_kernel, begin, heads),
        out_shape=jax.ShapeDtypeStruct((seq_len, lanes), jnp.bfloat16),
        in_specs=[VMEM] * 7,
        out_specs=VMEM,
        scratch_shapes=[
            pltpu.VMEM((heads, seq_len, HD), jnp.float32),
            cross,
            cross,
            bias_held(min(256, seq_len)),
        ],
        compiler_params=pltpu.CompilerParams(vmem_limit_bytes=24 * 2**20),
        cost_estimate=pl.CostEstimate(
            flops=160 * pairs * HD, bytes_accessed=seq_len * seq_len * 8, transcendentals=pairs
        ),
    )(angles, queries, keys, values, sums, attended, d_attended)


class Order:
    def __init__(self, token):
        self.token = token

    def tie(self, *arrays):
        tied = lax.optimization_barrier((self.token, *arrays))
        self.token = tied[0]
        return tied[1] if len(arrays) == 1 else tied[1:]

    def run(self, step, *arrays):
        tied = lax.optimization_barrier((self.token, *arrays))
        out = step(*tied[1:])
        if isinstance(out, tuple):
            return self.tie(*out)
        return self.tie(out)


class Chain:
    def __init__(self, order, steps):
        self.order, self.steps, self.out, self.held = order, steps, None, None
        self._go(None)

    def _go(self, arrived):
        try:
            array, axis, pairs = self.steps.send(arrived)
        except StopIteration as stop:
            self.held, self.out = None, stop.value
            return
        array = self.order.tie(array)
        self.held = lax.ppermute(array, axis, pairs)

    def on(self):
        if self.held is not None:
            self._go(self.order.tie(self.held))
        return self

    def end(self):
        while self.held is not None:
            self.on()
        return self.out


def swap_pairs(size, bit):
    return [(i, i ^ bit) for i in range(size)]


def tensor_steps(array, size, order, between):
    place = lax.axis_index("tensor")
    first = 0
    for bit in order:
        half = array.shape[0] // 2
        mine = (place // bit) % 2
        away = lax.dynamic_slice_in_dim(array, (1 - mine) * half, half, 0)
        got = yield away, "tensor", swap_pairs(size, bit)
        array = lax.dynamic_slice_in_dim(array, mine * half, half, 0) + got
        first = first + mine * half
    array = between(array, first)
    for bit in reversed(order):
        got = yield array, "tensor", swap_pairs(size, bit)
        mine = (place // bit) % 2
        array = jnp.where(
            mine == 0,
            jnp.concatenate([array, got], axis=0),
            jnp.concatenate([got, array], axis=0),
        )
    return array


def core_steps(array, size):
    core = lax.axis_index("dp") % 2
    half = array.shape[0] // 2
    away = lax.dynamic_slice_in_dim(array, (1 - core) * half, half, 0)
    got = yield away, "dp", swap_pairs(size, 1)
    return lax.dynamic_slice_in_dim(array, core * half, half, 0) + got


def line_steps(array, size, back=True):
    chips = size // 2
    place = lax.axis_index("dp") // 2

    def pairs(moves):
        return [(2 * a + c, 2 * b + c) for a, b in moves for c in range(2)]

    if chips > 1:
        steps = range(chips // 2 - 1)
        for s in steps:
            got = yield array, "dp", pairs([(s, s + 1), (chips - 1 - s, chips - 2 - s)])
            array = array + got
        middle = chips // 2
        got = yield array, "dp", pairs([(middle - 1, middle), (middle, middle - 1)])
        array = array + got
        for s in reversed(steps):
            got = yield array, "dp", pairs([(s + 1, s), (chips - 2 - s, chips - 1 - s)])
            array = jnp.where((place == s) | (place == chips - 1 - s), got, array)
    if not back:
        return array
    got = yield array, "dp", swap_pairs(size, 1)
    return array, got


def small_steps(stats, rest, tensor_size, dp_size):
    for bit in (1 << k for k in range(tensor_size.bit_length() - 1)):
        got = yield stats, "tensor", swap_pairs(tensor_size, bit)
        stats = stats + got
    vectors = jnp.concatenate([stats.reshape(-1), *rest])
    got = yield vectors, "dp", swap_pairs(dp_size, 1)
    return (yield from line_steps(vectors + got, dp_size, back=False))


def assemble(core, parts):
    low = [jnp.where(core == 0, mine, other) for mine, other in parts]
    high = [jnp.where(core == 0, other, mine) for mine, other in parts]
    return jnp.concatenate(low + high, axis=0)


def halves(array, chunks):
    rows = array.shape[0] // chunks
    return [array[c * rows : (c + 1) * rows] for c in range(chunks)]


def shards(
    dp_size,
    tensor_size,
    tokens,
    segment,
    attn_gain,
    attn_shift,
    mlp_gain,
    mlp_shift,
    w_qkv,
    b_qkv,
    w_out,
    w_up,
    b_up,
    w_down,
    b_branch,
    cotangent,
):
    rows_here, width = tokens.shape
    heads = w_qkv.shape[1] // (3 * HD)
    group = 2 if heads % 2 == 0 else heads
    lanes = -(-3 * HD * group // 128) * 128
    bits = [1 << k for k in range(tensor_size.bit_length() - 1)]
    orders = (bits, bits[::-1])
    split = rows_here // 2
    order = Order(lax.axis_index("dp") % 2)
    run = order.run

    def chain(steps):
        return Chain(order, steps)

    def norm(tokens):
        rows = tokens.astype(jnp.float32)
        centred = rows - jnp.mean(rows, axis=-1, keepdims=True)
        scale_inv = lax.rsqrt(jnp.mean(centred * centred, axis=-1, keepdims=True) + EPS)
        normed = centred * scale_inv
        return (
            (normed * attn_gain + attn_shift).astype(jnp.bfloat16),
            (normed * mlp_gain + mlp_shift).astype(jnp.bfloat16),
            normed,
            scale_inv,
        )

    def feed(mlp_low, w_up):
        pre_act = product(mlp_low, w_up) + b_up
        below = 0.5 * (1.0 + lax.erf(pre_act * (0.5**0.5)))
        bell = jnp.exp(-0.5 * pre_act * pre_act) * ((2.0 * math.pi) ** -0.5)
        return (pre_act * below).astype(jnp.bfloat16), below + pre_act * bell

    def project(attn_low, w_qkv):
        projected = product(attn_low, w_qkv) + b_qkv
        if group * 3 * HD != lanes:
            projected = jnp.pad(projected, ((0, 0), (0, lanes - group * 3 * HD)))
        return projected

    attn_low, mlp_low, normed, scale_inv = run(norm, tokens)
    hidden, slope = run(feed, mlp_low, w_up)
    core_down = chain(core_steps(run(inner_rows, hidden, cotangent), dp_size))
    projected = run(project, attn_low, w_qkv)
    angles = run(turn_angles, segment[0])
    d_attended = run(
        lambda dy, w: times_trans(dy, w).astype(jnp.bfloat16), cotangent, w_out
    )
    down = [line_steps(part, dp_size) for part in halves(core_down.end(), 2)]
    down[0] = chain(down[0])
    kept = run(functools.partial(attend, heads=heads), angles, projected)
    attended = kept[0]

    def branches(attended, hidden):
        return tuple(
            product(attended[rows], w_out) + product(hidden[rows], w_down)
            for rows in (slice(0, split), slice(split, None))
        )

    partial = run(branches, attended, hidden)
    result = [
        chain(tensor_steps(part, tensor_size, its, lambda rows, first: rows))
        for part, its in zip(partial, orders, strict=True)
    ]
    d_pre = run(
        lambda dy, w, slope: (times_trans(dy, w) * slope).astype(jnp.bfloat16),
        cotangent,
        w_down,
        slope,
    )
    core_up = chain(core_steps(run(inner_rows, mlp_low, d_pre), dp_size))
    down[0].on()
    down[1] = chain(down[1])
    d_mlp_in = run(times_trans, d_pre, w_up)
    up = [line_steps(part, dp_size) for part in halves(core_up.end(), 2)]
    result[0].on()
    result[1].on()

    back = []
    for begin in range(0, heads, group):
        def step(angles, d_attended, *kept, begin=begin):
            return attend_back(angles, kept, d_attended, begin, group, lanes)

        back.append(run(step, angles, d_attended, *kept)[:, : group * 3 * HD])
        result[0].on()
        result[1].on()
        if begin == 0:
            down[0].on()
            down[1].on()
            up[0] = chain(up[0])

    def backward(w_qkv, d_mlp_in, *back):
        d_projected = jnp.concatenate(back, axis=1)
        d_attn_in = times_trans(d_projected, w_qkv)
        return d_projected, d_attn_in, d_attn_in * attn_gain + d_mlp_in * mlp_gain

    d_projected, d_attn_in, scaled = run(backward, w_qkv, d_mlp_in, *back)

    def norm_back(part):
        def between(rows, first):
            at = first + part * split

            def here(whole):
                return lax.dynamic_slice_in_dim(whole, at, rows.shape[0], 0)

            normed_here = here(normed)
            return here(cotangent).astype(jnp.float32) + here(scale_inv) * (
                rows
                - jnp.mean(rows, axis=-1, keepdims=True)
                - normed_here * jnp.mean(rows * normed_here, axis=-1, keepdims=True)
            )

        return between

    d_tokens = [
        chain(tensor_steps(scaled[p * split : (p + 1) * split], tensor_size, its, norm_back(p)))
        for p, its in enumerate(orders)
    ]
    core_qkv = chain(core_steps(run(inner_rows, attn_low, d_projected), dp_size))
    down[0].on()
    down[1].on()
    up[0].on()
    up[1] = chain(up[1])
    core_out = chain(core_steps(run(inner_rows, attended, cotangent), dp_size))

    def sums(d_attn_in, d_mlp_in, normed):
        return jnp.stack(
            [
                jnp.sum(d_attn_in * normed, axis=0),
                jnp.sum(d_attn_in, axis=0),
                jnp.sum(d_mlp_in * normed, axis=0),
                jnp.sum(d_mlp_in, axis=0),
            ]
        )

    def columns(*arrays):
        return tuple(jnp.sum(array.astype(jnp.float32), axis=0) for array in arrays)

    stats = run(sums, d_attn_in, d_mlp_in, normed)
    rest = run(columns, d_projected, d_pre, cotangent)
    small = chain(small_steps(stats, rest, tensor_size, dp_size))
    qkv = [line_steps(part, dp_size) for part in halves(core_qkv.end(), 2)]
    out = line_steps(core_out.end(), dp_size)
    small.on()

    def finish(tokens, *parts):
        summed = jnp.concatenate(parts, axis=0)
        return (tokens.astype(jnp.float32) + summed + b_branch).astype(jnp.bfloat16)

    result = run(finish, tokens, *(part.end() for part in result))
    small.on()
    for part in d_tokens:
        part.on()
    for part in (down[0], down[1], up[0], up[1]):
        part.on()
    qkv[0] = chain(qkv[0])
    small.on()
    for part in d_tokens:
        part.on()
    small.on()
    for part in (down[1], up[0], up[1], qkv[0]):
        part.on()
    qkv[1] = chain(qkv[1])
    small.on()
    for part in d_tokens:
        part.on()
    grad_down = run(lambda *p: assemble(p[0], (p[1:3], p[3:5])), order.token, *down[0].end(), *down[1].end())
    for part in (up[0], up[1], qkv[0], qkv[1]):
        part.on()
    out = chain(out)
    for part in d_tokens:
        part.on()
    for part in (up[1], qkv[0], qkv[1], out):
        part.on()
    d_tokens = run(lambda *p: jnp.concatenate(p, axis=0), *(part.end() for part in d_tokens))
    grad_up = run(lambda *p: assemble(p[0], (p[1:3], p[3:5])), order.token, *up[0].end(), *up[1].end())
    vectors = small.end()
    for part in (qkv[0], qkv[1], out):
        part.on()
    qkv[0].end(), qkv[1].end()
    out.on()
    grad_qkv = run(lambda *p: assemble(p[0], (p[1:3], p[3:5])), order.token, *qkv[0].end(), *qkv[1].end())
    grad_out = out.end()
    grad_out = assemble(order.token, (grad_out,))

    sizes = (width,) * 4 + (w_qkv.shape[1], w_up.shape[1], width)
    ends = [sum(sizes[: k + 1]) for k in range(len(sizes))]
    a_gain, a_shift, m_gain, m_shift, qkv_bias, up_bias, branch = (
        vectors[end - size : end] for end, size in zip(ends, sizes, strict=True)
    )
    return (
        result,
        d_tokens,
        grad_qkv,
        qkv_bias,
        grad_out,
        grad_up,
        up_bias,
        grad_down,
        branch,
        a_gain,
        a_shift,
        m_gain,
        m_shift,
    )


def solution(mesh):
    placed = (
        P("dp", None),
        P("dp", None),
        P(),
        P(),
        P(),
        P(),
        P(None, "tensor"),
        P("tensor"),
        P("tensor", None),
        P(None, "tensor"),
        P("tensor"),
        P("tensor", None),
        P(),
        P("dp", None),
    )

    def body(*arrays):
        return shards(mesh.shape["dp"], mesh.shape["tensor"], *arrays)

    return jax.shard_map(
        body,
        mesh=mesh,
        in_specs=placed,
        out_specs=(
            P("dp", None),
            P("dp", None),
            P(None, "tensor"),
            P("tensor"),
            P("tensor", None),
            P(None, "tensor"),
            P("tensor"),
            P("tensor", None),
            P(),
            P(),
            P(),
            P(),
            P(),
        ),
        check_vma=False,
    )
```

time: 617 us -> 377 us (0.61)
  waiting for transfers between devices: 438 us -> 130 us
  starting transfers between devices: 0.25 us -> 82.5 us
  matrix products: 74.6 us -> 31.3 us
  other arithmetic: 33.5 us -> 74 us
  blocking collectives: 31.2 us -> 0 us
  Pallas kernels: 0 us -> 27.7 us
  between operations: 14.9 us -> 2.42 us
    psum x2 -> x0, waiting for transfers between devices: 438 us -> none  [the longest x1 225 us: shards(): branches = lax.psum(attn_part + mlp_part, 'tensor')]
    ppermute x0 -> x54, waiting for transfers between devices: none -> 130 us  [_go(): self.held = lax.ppermute(array, axis, pairs)]
    ppermute x0 -> x54, starting transfers between devices: none -> 82.5 us  [_go(): self.held = lax.ppermute(array, axis, pairs)]
    psum x1 -> x0, blocking collectives: 31.2 us -> none  [shards(): lax.psum((grad_qkv, grad_qkv_bias, grad_out, grad_up, grad_up_bias, grad_...]
    pallas_call x0 -> x3, Pallas kernels: none -> 27.7 us  [the longest x2 14.5 us: attend_back(): pl.pallas_call(functools.partial(attend_back_kernel, begin, heads), out_s...]
    select_n x1 -> x23, other arithmetic: 0.01 us -> 26.7 us  [the longest x8 13.5 us: tensor_steps(): jnp.where(mine == 0, jnp.concatenate([array, got], axis=0), jnp.concatena...]
    dot_general x16 -> x6, matrix products: 34.6 us -> 14.5 us  [product(): return jnp.dot(first_mat, second_mat, preferred_element_type=jnp.float32)]
    add x3 -> x27, other arithmetic: 0.02 us -> 16.9 us  [the longest x13 7.78 us: line_steps(): array = array + got]
  transfers between devices with their start and end apart: 2 -> 54, of which waited for: 2 -> 19; matrix products, arithmetic and copies ran while one was open for 5% -> 22% of each run, Pallas kernels for 0% -> 4%
where the time goes in v2:
time: 377 us; the launch traced here: 373 us
  waiting for transfers between devices  130 us (34%)
  starting transfers between devices  82.5 us (22%)
  other arithmetic  74 us (20%)
  matrix products  31.3 us (8%)
  Pallas kernels  27.7 us (7%)
  local copies, waits for them, and re-layouts  25 us (7%)
    ppermute x54, waiting for transfers between devices, _go(): self.held = lax.ppermute(array, axis, pairs)  130 us
    ppermute x54, starting transfers between devices, _go(): self.held = lax.ppermute(array, axis, pairs)  82.5 us
    dot_general x6, matrix products, product(): return jnp.dot(first_mat, second_mat, preferred_element_type=jnp.float32)  14.5 us
    pallas_call x2, Pallas kernels, attend_back(): pl.pallas_call(functools.partial(attend_back_kernel, begin, heads), out_s...  14.5 us
    select_n x8, other arithmetic, tensor_steps(): jnp.where(mine == 0, jnp.concatenate([array, got], axis=0), jnp.concatena...  13.5 us
    pallas_call x1, Pallas kernels, attend(): pl.pallas_call(functools.partial(attend_kernel, heads), out_shape=(shape(...  13.2 us
    unnamed x144, local copies, waits for them, and re-layouts  11.8 us
    dot_general x4, matrix products, inner_rows(): lax.dot_general(first_mat, second_mat, (((0,), (0,)), ((), ())), preferre...  9.44 us
  transfers between devices with their start and end apart: 54, of which 19 were waited for; matrix products, arithmetic and copies ran while one was open for 22% of the time, Pallas kernels for 4%

profile of v2, /device:TPU:0, one launch (start us, length us, event | category | flops | bytes accessed | tf_op | source)
XLA Modules:
  0.0 372.7 jit_solution(7738877946999524312)
XLA Ops:
  7.3 5.4 %fusion.6 = (f32[1024,1024]{1,0:T(8,128)}, bf16[1024,1024]{1,0:T(8,128)(2,1)S(1)}) fusion(f32[1024]{0:T(1024)S(1)} %copy-done.65, bf16[1024,1024]{1,0:T(8,128)(2,1)S(1)} %get-tuple-element.411, bf16[1024,1024]{1,0:T(8,128)(2,1)S(1)} %copy-done), kind=kOutput, calls=%fused_computation.9 | convolution fusion | flops 2159017984 | bytes 10489856 | tf_op jit(solution)/shard_map/dot_general | solution.py:32
  14.0 4.4 %fusion.24 = f32[1024,1024]{1,0:T(8,128)} fusion(bf16[1024,1024]{1,0:T(8,128)(2,1)S(1)} %get-tuple-element.399, bf16[1024,1024]{1,0:T(8,128)(2,1)S(1)} %copy-done.18), kind=kOutput, calls=%fused_computation.136 | convolution fusion | flops 2147483648 | bytes 8388608 | tf_op jit(solution)/shard_map/dot_general | solution.py:20
  22.1 5.6 %convolution_add_fusion.projected = f32[1024,768]{1,0:T(8,128)} fusion(bf16[1024,1024]{1,0:T(8,128)(2,1)} %get-tuple-element.493, bf16[1024,768]{1,0:T(8,128)(2,1)} %param.20, f32[768]{0:T(1024)S(1)} %copy-done.66), kind=kOutput, calls=%fused_computation.34 | convolution fusion | flops 1611399168 | bytes 6818816 | tf_op jit(solution)/shard_map/dot_general | solution.py:32
  36.6 13.2 %shard_map.237 = (bf16[1024,256]{1,0:T(8,128)(2,1)S(1)}, f32[1024,128]{1,0:T(8,128)S(1)}, bf16[4,1024,64]{2,1,0:T(8,128)(2,1)S(1)}, bf16[4,1024,64]{2,1,0:T(8,128)(2,1)S(1)}, bf16[4,1024,64]{2,1,0:T(8,128)(2,1)S(1)}) custom-call(f32[24,1024]{1,0:T(8,128)S(1)} %pad_maximum_fusion.5.angles, f32[1024,768]{1,0:T(8,128)S(1)} %copy-done.2), custom_call_target="tpu_custom_call" | custom-call | flops 10737418240 | bytes 8388608 | tf_op jit(solution)/shard_map/pallas_call | solution.py:198
  66.1 5.9 %collective-permute-start.1 = (f32[256,1024]{1,0:T(8,128)}, f32[256,1024]{1,0:T(8,128)}, u32[]{:S(2)}, u32[]{:S(2)}) collective-permute-start(f32[256,1024]{1,0:T(8,128)} %slice.76), channel_id=1, source_target_pairs={{0,8},{4,12},{24,16},{28,20},{1,9},{5,13},{25,17},{29,21},{2,10},{... | collective-permute-start | bytes 3145736 | tf_op jit(solution)/shard_map/ppermute | solution.py:267
  75.0 18.9 %collective-permute-done.1 = f32[256,1024]{1,0:T(8,128)} collective-permute-done((f32[256,1024]{1,0:T(8,128)}, f32[256,1024]{1,0:T(8,128)}, u32[]{:S(2)}, u32[]{:S(2)}) %collective-permute-start.1) | collective-permute-done | bytes 1048608 | tf_op jit(solution)/shard_map/ppermute | solution.py:267
  99.4 7.4 %collective-permute-start.8 = (f32[256,1024]{1,0:T(8,128)S(1)}, f32[256,1024]{1,0:T(8,128)S(1)}, u32[]{:S(2)}, u32[]{:S(2)}) collective-permute-start(f32[256,1024]{1,0:T(8,128)S(1)} %get-tuple-element.459), channel_id=1, source_target_pairs={{0,8},{4,12},{24,16},{28,20},{1,9},{5,13},{25,17},{29,21},{2,10},{... | collective-permute-start | bytes 3145736 | tf_op jit(solution)/shard_map/ppermute | solution.py:267
  111.7 7.1 %shard_map.238 = bf16[1024,384]{1,0:T(8,128)(2,1)S(1)} custom-call(f32[24,1024]{1,0:T(8,128)S(1)} %pad_maximum_fusion.5.angles, bf16[4,1024,64]{2,1,0:T(8,128)(2,1)S(1)} %copy-done.4, bf16[4,1024,64]{2,1,0:T(8,128)(2,1)S(1)} %copy-done.6, bf16[4,1024,64]{2,1,0:T(8,128)(2,1)S(1)} %copy-done.8, f32[1024,128]{1,0:T(8,128)S(1)} %copy-done.10, ...), custom_call_target="tpu_custom_call" | custom-call | flops 10737418240 | bytes 8388608 | tf_op jit(solution)/shard_map/pallas_call | solution.py:220
  122.6 5.4 %collective-permute-done.8 = f32[256,1024]{1,0:T(8,128)S(1)} collective-permute-done((f32[256,1024]{1,0:T(8,128)S(1)}, f32[256,1024]{1,0:T(8,128)S(1)}, u32[]{:S(2)}, u32[]{:S(2)}) %collective-permute-start.8) | collective-permute-done | bytes 1048608 | tf_op jit(solution)/shard_map/ppermute | solution.py:267
  131.3 7.4 %shard_map.239 = bf16[1024,384]{1,0:T(8,128)(2,1)S(1)} custom-call(f32[24,1024]{1,0:T(8,128)S(1)} %pad_maximum_fusion.5.angles, bf16[4,1024,64]{2,1,0:T(8,128)(2,1)S(1)} %copy-done.4, bf16[4,1024,64]{2,1,0:T(8,128)(2,1)S(1)} %copy-done.6, bf16[4,1024,64]{2,1,0:T(8,128)(2,1)S(1)} %copy-done.8, f32[1024,128]{1,0:T(8,128)S(1)} %copy-done.10, ...), custom_call_target="tpu_custom_call" | custom-call | flops 10737418240 | bytes 8388608 | tf_op jit(solution)/shard_map/pallas_call | solution.py:220
  140.7 6.3 %collective-permute-start.13 = (f32[256,1024]{1,0:T(8,128)S(1)}, f32[256,1024]{1,0:T(8,128)S(1)}, u32[]{:S(2)}, u32[]{:S(2)}) collective-permute-start(f32[256,1024]{1,0:T(8,128)S(1)} %slice.78), channel_id=1, source_target_pairs={{0,8},{4,12},{24,16},{28,20},{1,9},{5,13},{25,17},{29,21},{2,10},{... | collective-permute-start | bytes 3145736 | tf_op jit(solution)/shard_map/ppermute | solution.py:267
  159.0 4.1 %collective-permute-done.11 = f32[256,1024]{1,0:T(8,128)S(1)} collective-permute-done((f32[256,1024]{1,0:T(8,128)S(1)}, f32[256,1024]{1,0:T(8,128)S(1)}, u32[]{:S(2)}, u32[]{:S(2)}) %collective-permute-start.11) | collective-permute-done | bytes 1048608 | tf_op jit(solution)/shard_map/ppermute | solution.py:267
  178.3 6.7 %collective-permute-done.16 = f32[4,1024]{1,0:T(4,128)S(1)} collective-permute-done((f32[4,1024]{1,0:T(4,128)S(1)}, f32[4,1024]{1,0:T(4,128)S(1)}, u32[]{:S(2)}, u32[]{:S(2)}) %collective-permute-start.16) | collective-permute-done | bytes 16416 | tf_op jit(solution)/shard_map/ppermute | solution.py:267
  199.6 8.2 %collective-permute-done.19 = f32[4,1024]{1,0:T(4,128)S(1)} collective-permute-done((f32[4,1024]{1,0:T(4,128)S(1)}, f32[4,1024]{1,0:T(4,128)S(1)}, u32[]{:S(2)}, u32[]{:S(2)}) %collective-permute-start.19) | collective-permute-done | bytes 16416 | tf_op jit(solution)/shard_map/ppermute | solution.py:267
  214.2 17.3 %collective-permute-done.25 = f32[256,1024]{1,0:T(8,128)S(1)} collective-permute-done((f32[256,1024]{1,0:T(8,128)S(1)}, f32[256,1024]{1,0:T(8,128)S(1)}, u32[]{:S(2)}, u32[]{:S(2)}) %collective-permute-start.25) | collective-permute-done | bytes 1048608 | tf_op jit(solution)/shard_map/ppermute | solution.py:267
  235.6 6.1 %collective-permute-start.33 = (f32[256,768]{1,0:T(8,128)S(1)}, f32[256,768]{1,0:T(8,128)S(1)}, u32[]{:S(2)}, u32[]{:S(2)}) collective-permute-start(f32[256,768]{1,0:T(8,128)S(1)} %slice.80), channel_id=1, source_target_pairs={{0,8},{4,12},{24,16},{28,20},{1,9},{5,13},{25,17},{29,21},{2,10},{... | collective-permute-start | bytes 2359304 | tf_op jit(solution)/shard_map/ppermute | solution.py:267
  246.0 4.4 %collective-permute-start.29 = (f32[6912]{0:T(1024)S(1)}, f32[6912]{0:T(1024)S(1)}, u32[]{:S(2)}, u32[]{:S(2)}) collective-permute-start(f32[6912]{0:T(1024)S(1)} %add.335), channel_id=1, source_target_pairs={{0,8},{4,12},{24,16},{28,20},{1,9},{5,13},{25,17},{29,21},{2,10},{... | collective-permute-start | bytes 82952 | tf_op jit(solution)/shard_map/ppermute | solution.py:267
  250.8 8.3 %collective-permute-done.29 = f32[6912]{0:T(1024)S(1)} collective-permute-done((f32[6912]{0:T(1024)S(1)}, f32[6912]{0:T(1024)S(1)}, u32[]{:S(2)}, u32[]{:S(2)}) %collective-permute-start.29) | collective-permute-done | bytes 27680 | tf_op jit(solution)/shard_map/ppermute | solution.py:267
  267.5 5.1 %collective-permute-done.35 = f32[128,1024]{1,0:T(8,128)S(1)} collective-permute-done((f32[128,1024]{1,0:T(8,128)S(1)}, f32[128,1024]{1,0:T(8,128)S(1)}, u32[]{:S(2)}, u32[]{:S(2)}) %collective-permute-start.35) | collective-permute-done | bytes 524320 | tf_op jit(solution)/shard_map/ppermute | solution.py:267
  272.7 8.0 %collective-permute-start.40 = (f32[256,768]{1,0:T(8,128)}, f32[256,768]{1,0:T(8,128)}, u32[]{:S(2)}, u32[]{:S(2)}) collective-permute-start(f32[256,768]{1,0:T(8,128)} %get-tuple-element.640), channel_id=1, source_target_pairs={{0,8},{4,12},{24,16},{28,20},{1,9},{5,13},{25,17},{29,21},{2,10},{... | collective-permute-start | bytes 2359304 | tf_op jit(solution)/shard_map/ppermute | solution.py:267
  287.7 7.1 %collective-permute-done.38 = f32[256,1024]{1,0:T(8,128)} collective-permute-done((f32[256,1024]{1,0:T(8,128)}, f32[256,1024]{1,0:T(8,128)}, u32[]{:S(2)}, u32[]{:S(2)}) %collective-permute-start.38) | collective-permute-done | bytes 1048608 | tf_op jit(solution)/shard_map/ppermute | solution.py:267
  315.0 5.9 %collective-permute-done.44 = f32[256,768]{1,0:T(8,128)S(1)} collective-permute-done((f32[256,768]{1,0:T(8,128)S(1)}, f32[256,768]{1,0:T(8,128)S(1)}, u32[]{:S(2)}, u32[]{:S(2)}) %collective-permute-start.44) | collective-permute-done | bytes 786464 | tf_op jit(solution)/shard_map/ppermute | solution.py:267
  334.5 15.4 %collective-permute-done.49 = f32[256,768]{1,0:T(8,128)S(1)} collective-permute-done((f32[256,768]{1,0:T(8,128)}, f32[256,768]{1,0:T(8,128)S(1)}, u32[]{:S(2)}, u32[]{:S(2)}) %collective-permute-start.49) | collective-permute-done | bytes 786464 | tf_op jit(solution)/shard_map/ppermute | solution.py:267
  352.8 14.0 %collective-permute-done.52 = f32[128,1024]{1,0:T(8,128)S(1)} collective-permute-done((f32[128,1024]{1,0:T(8,128)S(1)}, f32[128,1024]{1,0:T(8,128)S(1)}, u32[]{:S(2)}, u32[]{:S(2)}) %collective-permute-start.52) | collective-permute-done | bytes 524320 | tf_op jit(solution)/shard_map/ppermute | solution.py:267
  (347 shorter events, 172.5 us)
Async XLA Ops:
  66.0 40.8 %collective-permute-start.2 = (f32[512,1024]{1,0:T(8,128)}, f32[512,1024]{1,0:T(8,128)}, u32[]{:S(2)}, u32[]{:S(2)}) collective-permute-start(f32[512,1024]{1,0:T(8,128)} %constant_dynamic-slice_fusion.10), channel_id=1, source_target_pairs={{0,4},{4,0},{8,12},{12,8},{16,20},{20,16},{24,28},{28,24},{1,5},{5... | collective-permute-start | bytes 6291464 | tf_op jit(solution)/shard_map/ppermute | solution.py:267
  66.1 27.8 %collective-permute-start.1 = (f32[256,1024]{1,0:T(8,128)}, f32[256,1024]{1,0:T(8,128)}, u32[]{:S(2)}, u32[]{:S(2)}) collective-permute-start(f32[256,1024]{1,0:T(8,128)} %slice.76), channel_id=1, source_target_pairs={{0,8},{4,12},{24,16},{28,20},{1,9},{5,13},{25,17},{29,21},{2,10},{... | collective-permute-start | bytes 3145736 | tf_op jit(solution)/shard_map/ppermute | solution.py:267
  72.0 34.8 %collective-permute-start.3 = (f32[256,1024]{1,0:T(8,128)}, f32[256,1024]{1,0:T(8,128)}, u32[]{:S(2)}, u32[]{:S(2)}) collective-permute-start(f32[256,1024]{1,0:T(8,128)} %get-tuple-element.426), channel_id=1, source_target_pairs={{0,1},{1,0},{2,3},{3,2},{4,5},{5,4},{6,7},{7,6},{8,9},{9,8},{10,11... | collective-permute-start | bytes 3145736 | tf_op jit(solution)/shard_map/ppermute | solution.py:267
  73.5 34.9 %collective-permute-start.4 = (f32[256,1024]{1,0:T(8,128)}, f32[256,1024]{1,0:T(8,128)S(1)}, u32[]{:S(2)}, u32[]{:S(2)}) collective-permute-start(f32[256,1024]{1,0:T(8,128)} %get-tuple-element.430), channel_id=1, source_target_pairs={{0,2},{1,3},{2,0},{3,1},{4,6},{5,7},{6,4},{7,5},{8,10},{9,11},{10,... | collective-permute-start | bytes 3145736 | tf_op jit(solution)/shard_map/ppermute | solution.py:267
  98.5 23.9 %collective-permute-start.7 = (f32[256,1024]{1,0:T(8,128)S(1)}, f32[256,1024]{1,0:T(8,128)S(1)}, u32[]{:S(2)}, u32[]{:S(2)}) collective-permute-start(f32[256,1024]{1,0:T(8,128)S(1)} %get-tuple-element.455), channel_id=1, source_target_pairs={{8,16},{12,20},{16,8},{20,12},{9,17},{13,21},{17,9},{21,13},{10,18... | collective-permute-start | bytes 3145736 | tf_op jit(solution)/shard_map/ppermute | solution.py:267
  99.4 28.6 %collective-permute-start.8 = (f32[256,1024]{1,0:T(8,128)S(1)}, f32[256,1024]{1,0:T(8,128)S(1)}, u32[]{:S(2)}, u32[]{:S(2)}) collective-permute-start(f32[256,1024]{1,0:T(8,128)S(1)} %get-tuple-element.459), channel_id=1, source_target_pairs={{0,8},{4,12},{24,16},{28,20},{1,9},{5,13},{25,17},{29,21},{2,10},{... | collective-permute-start | bytes 3145736 | tf_op jit(solution)/shard_map/ppermute | solution.py:267
  138.6 24.5 %collective-permute-start.11 = (f32[256,1024]{1,0:T(8,128)S(1)}, f32[256,1024]{1,0:T(8,128)S(1)}, u32[]{:S(2)}, u32[]{:S(2)}) collective-permute-start(f32[256,1024]{1,0:T(8,128)S(1)} %add.318), channel_id=1, source_target_pairs={{8,0},{12,4},{16,24},{20,28},{9,1},{13,5},{17,25},{21,29},{10,2},{... | collective-permute-start | bytes 3145736 | tf_op jit(solution)/shard_map/ppermute | solution.py:267
  139.9 24.8 %collective-permute-start.12 = (f32[256,1024]{1,0:T(8,128)S(1)}, f32[256,1024]{1,0:T(8,128)S(1)}, u32[]{:S(2)}, u32[]{:S(2)}) collective-permute-start(f32[256,1024]{1,0:T(8,128)S(1)} %slice_add_fusion.4), channel_id=1, source_target_pairs={{8,16},{12,20},{16,8},{20,12},{9,17},{13,21},{17,9},{21,13},{10,18... | collective-permute-start | bytes 3145736 | tf_op jit(solution)/shard_map/ppermute | solution.py:267
  140.7 25.8 %collective-permute-start.13 = (f32[256,1024]{1,0:T(8,128)S(1)}, f32[256,1024]{1,0:T(8,128)S(1)}, u32[]{:S(2)}, u32[]{:S(2)}) collective-permute-start(f32[256,1024]{1,0:T(8,128)S(1)} %slice.78), channel_id=1, source_target_pairs={{0,8},{4,12},{24,16},{28,20},{1,9},{5,13},{25,17},{29,21},{2,10},{... | collective-permute-start | bytes 3145736 | tf_op jit(solution)/shard_map/ppermute | solution.py:267
  158.5 26.5 %collective-permute-start.17 = (f32[256,1024]{1,0:T(8,128)}, f32[256,1024]{1,0:T(8,128)S(1)}, u32[]{:S(2)}, u32[]{:S(2)}) collective-permute-start(f32[256,1024]{1,0:T(8,128)} %maximum_select_fusion.4), channel_id=1, source_target_pairs={{0,1},{1,0},{2,3},{3,2},{4,5},{5,4},{6,7},{7,6},{8,9},{9,8},{10,11... | collective-permute-start | bytes 3145736 | tf_op jit(solution)/shard_map/ppermute | solution.py:267
  163.2 26.4 %collective-permute-start.18 = (f32[256,1024]{1,0:T(8,128)}, f32[256,1024]{1,0:T(8,128)}, u32[]{:S(2)}, u32[]{:S(2)}) collective-permute-start(f32[256,1024]{1,0:T(8,128)} %maximum_select_fusion.5), channel_id=1, source_target_pairs={{0,2},{1,3},{2,0},{3,1},{4,6},{5,7},{6,4},{7,5},{8,10},{9,11},{10,... | collective-permute-start | bytes 3145736 | tf_op jit(solution)/shard_map/ppermute | solution.py:267
  174.8 33.8 %collective-permute-start.20 = (f32[256,1024]{1,0:T(8,128)S(1)}, f32[256,1024]{1,0:T(8,128)S(1)}, u32[]{:S(2)}, u32[]{:S(2)}) collective-permute-start(f32[256,1024]{1,0:T(8,128)S(1)} %copy-done.54), channel_id=1, source_target_pairs={{0,1},{1,0},{2,3},{3,2},{4,5},{5,4},{6,7},{7,6},{8,9},{9,8},{10,11... | collective-permute-start | bytes 3145736 | tf_op jit(solution)/shard_map/ppermute | solution.py:267
  176.4 36.5 %collective-permute-start.21 = (f32[256,1024]{1,0:T(8,128)S(1)}, f32[256,1024]{1,0:T(8,128)S(1)}, u32[]{:S(2)}, u32[]{:S(2)}) collective-permute-start(f32[256,1024]{1,0:T(8,128)S(1)} %copy-done.53), channel_id=1, source_target_pairs={{0,2},{1,3},{2,0},{3,1},{4,6},{5,7},{6,4},{7,5},{8,10},{9,11},{10,... | collective-permute-start | bytes 3145736 | tf_op jit(solution)/shard_map/ppermute | solution.py:267
  185.0 28.1 %collective-permute-start.22 = (f32[256,1024]{1,0:T(8,128)}, f32[256,1024]{1,0:T(8,128)S(1)}, u32[]{:S(2)}, u32[]{:S(2)}) collective-permute-start(f32[256,1024]{1,0:T(8,128)} %broadcast_select_fusion.11), channel_id=1, source_target_pairs={{0,4},{4,0},{8,12},{12,8},{16,20},{20,16},{24,28},{28,24},{1,5},{5... | collective-permute-start | bytes 3145736 | tf_op jit(solution)/shard_map/ppermute | solution.py:267
  185.1 28.1 %collective-permute-start.23 = (f32[256,1024]{1,0:T(8,128)}, f32[256,1024]{1,0:T(8,128)S(1)}, u32[]{:S(2)}, u32[]{:S(2)}) collective-permute-start(f32[256,1024]{1,0:T(8,128)} %add.322), channel_id=1, source_target_pairs={{8,0},{12,4},{16,24},{20,28},{9,1},{13,5},{17,25},{21,29},{10,2},{... | collective-permute-start | bytes 3145736 | tf_op jit(solution)/shard_map/ppermute | solution.py:267
  233.3 26.4 %collective-permute-start.30 = (f32[256,1024]{1,0:T(8,128)S(1)}, f32[256,1024]{1,0:T(8,128)S(1)}, u32[]{:S(2)}, u32[]{:S(2)}) collective-permute-start(f32[256,1024]{1,0:T(8,128)S(1)} %broadcast_select_fusion.10), channel_id=1, source_target_pairs={{0,4},{4,0},{8,12},{12,8},{16,20},{20,16},{24,28},{28,24},{1,5},{5... | collective-permute-start | bytes 3145736 | tf_op jit(solution)/shard_map/ppermute | solution.py:267
  233.6 27.4 %collective-permute-start.31 = (f32[256,1024]{1,0:T(8,128)S(1)}, f32[256,1024]{1,0:T(8,128)S(1)}, u32[]{:S(2)}, u32[]{:S(2)}) collective-permute-start(f32[256,1024]{1,0:T(8,128)S(1)} %add.332), channel_id=1, source_target_pairs={{8,0},{12,4},{16,24},{20,28},{9,1},{13,5},{17,25},{21,29},{10,2},{... | collective-permute-start | bytes 3145736 | tf_op jit(solution)/shard_map/ppermute | solution.py:267
  234.9 27.3 %collective-permute-start.32 = (f32[256,1024]{1,0:T(8,128)S(1)}, f32[256,1024]{1,0:T(8,128)S(1)}, u32[]{:S(2)}, u32[]{:S(2)}) collective-permute-start(f32[256,1024]{1,0:T(8,128)S(1)} %slice_add_fusion.2), channel_id=1, source_target_pairs={{8,16},{12,20},{16,8},{20,12},{9,17},{13,21},{17,9},{21,13},{10,18... | collective-permute-start | bytes 3145736 | tf_op jit(solution)/shard_map/ppermute | solution.py:267
  235.6 27.8 %collective-permute-start.33 = (f32[256,768]{1,0:T(8,128)S(1)}, f32[256,768]{1,0:T(8,128)S(1)}, u32[]{:S(2)}, u32[]{:S(2)}) collective-permute-start(f32[256,768]{1,0:T(8,128)S(1)} %slice.80), channel_id=1, source_target_pairs={{0,8},{4,12},{24,16},{28,20},{1,9},{5,13},{25,17},{29,21},{2,10},{... | collective-permute-start | bytes 2359304 | tf_op jit(solution)/shard_map/ppermute | solution.py:267
  264.7 30.1 %collective-permute-start.38 = (f32[256,1024]{1,0:T(8,128)}, f32[256,1024]{1,0:T(8,128)}, u32[]{:S(2)}, u32[]{:S(2)}) collective-permute-start(f32[256,1024]{1,0:T(8,128)} %add.346), channel_id=1, source_target_pairs={{8,0},{12,4},{16,24},{20,28},{9,1},{13,5},{17,25},{21,29},{10,2},{... | collective-permute-start | bytes 3145736 | tf_op jit(solution)/shard_map/ppermute | solution.py:267
  266.0 31.2 %collective-permute-start.39 = (f32[256,768]{1,0:T(8,128)}, f32[256,768]{1,0:T(8,128)}, u32[]{:S(2)}, u32[]{:S(2)}) collective-permute-start(f32[256,768]{1,0:T(8,128)} %get-tuple-element.636), channel_id=1, source_target_pairs={{8,16},{12,20},{16,8},{20,12},{9,17},{13,21},{17,9},{21,13},{10,18... | collective-permute-start | bytes 2359304 | tf_op jit(solution)/shard_map/ppermute | solution.py:267
  272.7 26.1 %collective-permute-start.40 = (f32[256,768]{1,0:T(8,128)}, f32[256,768]{1,0:T(8,128)}, u32[]{:S(2)}, u32[]{:S(2)}) collective-permute-start(f32[256,768]{1,0:T(8,128)} %get-tuple-element.640), channel_id=1, source_target_pairs={{0,8},{4,12},{24,16},{28,20},{1,9},{5,13},{25,17},{29,21},{2,10},{... | collective-permute-start | bytes 2359304 | tf_op jit(solution)/shard_map/ppermute | solution.py:267
  304.5 29.3 %collective-permute-start.47 = (f32[6912]{0:T(1024)S(1)}, f32[6912]{0:T(1024)S(1)}, u32[]{:S(2)}, u32[]{:S(2)}) collective-permute-start(f32[6912]{0:T(1024)S(1)} %add.348), channel_id=1, source_target_pairs={{8,0},{12,4},{16,24},{20,28},{9,1},{13,5},{17,25},{21,29},{10,2},{... | collective-permute-start | bytes 82952 | tf_op jit(solution)/shard_map/ppermute | solution.py:267
  326.5 23.3 %collective-permute-start.49 = (f32[256,768]{1,0:T(8,128)}, f32[256,768]{1,0:T(8,128)S(1)}, u32[]{:S(2)}, u32[]{:S(2)}) collective-permute-start(f32[256,768]{1,0:T(8,128)} %add.353), channel_id=1, source_target_pairs={{8,0},{12,4},{16,24},{20,28},{9,1},{13,5},{17,25},{21,29},{10,2},{... | collective-permute-start | bytes 2359304 | tf_op jit(solution)/shard_map/ppermute | solution.py:267
  (100 other events, 883.2 us)

commit v3 on v2

--- a/solution.py
+++ b/solution.py
@@ -193,7 +193,6 @@
 
 def attend(angles, projected, heads):
     seq_len = projected.shape[0]
-    pairs = heads * seq_len * seq_len // 2
     shape = jax.ShapeDtypeStruct
     return pl.pallas_call(
         functools.partial(attend_kernel, heads),
@@ -206,16 +205,12 @@
         out_specs=(VMEM,) * 5,
         scratch_shapes=[bias_held(min(256, seq_len))],
         compiler_params=pltpu.CompilerParams(vmem_limit_bytes=24 * 2**20),
-        cost_estimate=pl.CostEstimate(
-            flops=80 * pairs * HD, bytes_accessed=seq_len * seq_len * 8, transcendentals=pairs
-        ),
     )(angles, projected)
 
 
 def attend_back(angles, kept, d_attended, begin, heads, lanes):
     attended, sums, queries, keys, values = kept
     seq_len = attended.shape[0]
-    pairs = heads * seq_len * seq_len // 2
     cross = pltpu.VMEM((heads, HD, seq_len), jnp.float32)
     return pl.pallas_call(
         functools.partial(attend_back_kernel, begin, heads),
@@ -229,10 +224,263 @@
             bias_held(min(256, seq_len)),
         ],
         compiler_params=pltpu.CompilerParams(vmem_limit_bytes=24 * 2**20),
-        cost_estimate=pl.CostEstimate(
-            flops=160 * pairs * HD, bytes_accessed=seq_len * seq_len * 8, transcendentals=pairs
+    )(angles, queries, keys, values, sums, attended, d_attended)
+
+
+def normed_rows(tokens):
+    rows = tokens.astype(jnp.float32)
+    centred = rows - jnp.mean(rows, axis=-1, keepdims=True)
+    scale_inv = lax.rsqrt(jnp.mean(centred * centred, axis=-1, keepdims=True) + EPS)
+    return centred * scale_inv, scale_inv
+
+
+def tiled(width, tile, at=lambda i, *order: i):
+    return pl.BlockSpec((tile, width), lambda i, *order: (at(i, *order), 0))
+
+
+def whole(array):
+    return pl.BlockSpec(array.shape, lambda i, *order: (0,) * array.ndim)
+
+
+PARAMS = pltpu.CompilerParams(vmem_limit_bytes=40 * 2**20)
+
+
+def forward_kernel(
+    tokens,
+    cotangent,
+    attn_gain,
+    attn_shift,
+    mlp_gain,
+    mlp_shift,
+    w_qkv,
+    b_qkv,
+    w_out,
+    w_up,
+    b_up,
+    attn_low,
+    mlp_low,
+    projected,
+    d_attended,
+    hidden,
+    slope,
+):
+    normed, _ = normed_rows(tokens[...])
+    attn_in = (normed * attn_gain[...] + attn_shift[...]).astype(jnp.bfloat16)
+    mlp_in = (normed * mlp_gain[...] + mlp_shift[...]).astype(jnp.bfloat16)
+    attn_low[...] = attn_in
+    mlp_low[...] = mlp_in
+    count, lanes = w_qkv.shape[1], projected.shape[1]
+    if lanes > count:
+        projected[...] = jnp.zeros(projected.shape, jnp.float32)
+    projected[:, :count] = product(attn_in, w_qkv[...]) + b_qkv[...]
+    d_attended[...] = times_trans(cotangent[...], w_out[...]).astype(jnp.bfloat16)
+    pre_act = product(mlp_in, w_up[...]) + b_up[...]
+    below = 0.5 * (1.0 + lax.erf(pre_act * (0.5**0.5)))
+    bell = jnp.exp(-0.5 * pre_act * pre_act) * ((2.0 * math.pi) ** -0.5)
+    hidden[...] = (pre_act * below).astype(jnp.bfloat16)
+    slope[...] = (below + pre_act * bell).astype(slope.dtype)
+
+
+def forward(tokens, cotangent, vectors, w_qkv, b_qkv, w_out, w_up, b_up, lanes):
+    rows, width = tokens.shape
+    tile = rows // 4
+    fixed = (*vectors, w_qkv, b_qkv, w_out, w_up, b_up)
+    outs = (
+        (width, jnp.bfloat16),
+        (width, jnp.bfloat16),
+        (lanes, jnp.float32),
+        (w_out.shape[0], jnp.bfloat16),
+        (w_up.shape[1], jnp.bfloat16),
+        (w_up.shape[1], jnp.float32),
+    )
+    return pl.pallas_call(
+        forward_kernel,
+        grid=(4,),
+        in_specs=[tiled(width, tile)] * 2 + [whole(array) for array in fixed],
+        out_specs=tuple(tiled(wide, tile) for wide, _ in outs),
+        out_shape=tuple(jax.ShapeDtypeStruct((rows, wide), kind) for wide, kind in outs),
+        compiler_params=PARAMS,
+    )(tokens, cotangent, *fixed)
+
+
+def feed_back_kernel(
+    tokens, cotangent, slope, w_down, w_up, mlp_gain, d_pre, scaled, sums, bias_sum
+):
+    @pl.when(pl.program_id(0) == 0)
+    def _():
+        sums[...] = jnp.zeros(sums.shape, jnp.float32)
+        bias_sum[...] = jnp.zeros(bias_sum.shape, jnp.float32)
+
+    d_low = (times_trans(cotangent[...], w_down[...]) * slope[...]).astype(jnp.bfloat16)
+    d_pre[...] = d_low
+    d_in = times_trans(d_low, w_up[...])
+    scaled[...] = d_in * mlp_gain[...]
+    normed, _ = normed_rows(tokens[...])
+    sums[0:1, :] += jnp.sum(d_in * normed, axis=0, keepdims=True)
+    sums[1:2, :] += jnp.sum(d_in, axis=0, keepdims=True)
+    bias_sum[...] += jnp.sum(d_low.astype(jnp.float32), axis=0, keepdims=True)
+
+
+def feed_back(tokens, cotangent, slope, w_down, w_up, mlp_gain):
+    rows, width = tokens.shape
+    inner = w_up.shape[1]
+    tile = rows // 4
+    fixed = (w_down, w_up, mlp_gain)
+    shape = jax.ShapeDtypeStruct
+    out_shape = (
+        shape((rows, inner), jnp.bfloat16),
+        shape((rows, width), jnp.float32),
+        shape((2, width), jnp.float32),
+        shape((1, inner), jnp.float32),
+    )
+    return pl.pallas_call(
+        feed_back_kernel,
+        grid=(4,),
+        in_specs=[tiled(width, tile)] * 2 + [tiled(inner, tile)] + [whole(a) for a in fixed],
+        out_specs=(tiled(inner, tile), tiled(width, tile)) + tuple(whole(a) for a in out_shape[2:]),
+        out_shape=out_shape,
+        compiler_params=PARAMS,
+    )(tokens, cotangent, slope, *fixed)
+
+
+def quarter_outs(rows, width):
+    shape = jax.ShapeDtypeStruct((rows // 4, width), jnp.float32)
+    return (shape,) * 4
+
+
+def branches_kernel(tiles, attended, hidden, w_out, w_down, *outs):
+    total = product(attended[...], w_out[...]) + product(hidden[...], w_down[...])
+    for number, out in enumerate(outs):
+
+        @pl.when(pl.program_id(0) == number)
+        def _(out=out):
+            out[...] = total
+
+
+def picked(i, tiles):
+    return tiles[i]
+
+
+def branches(tiles, attended, hidden, w_out, w_down):
+    rows, width = hidden.shape[0], w_down.shape[1]
+    outs = quarter_outs(rows, width)
+    return pl.pallas_call(
+        branches_kernel,
+        grid_spec=pltpu.PrefetchScalarGridSpec(
+            num_scalar_prefetch=1,
+            grid=(4,),
+            in_specs=[
+                tiled(attended.shape[1], rows // 4, picked),
+                tiled(hidden.shape[1], rows // 4, picked),
+                whole(w_out),
+                whole(w_down),
+            ],
+            out_specs=tuple(whole(out) for out in outs),
         ),
-    )(angles, queries, keys, values, sums, attended, d_attended)
+        out_shape=outs,
+        compiler_params=PARAMS,
+    )(tiles, attended, hidden, w_out, w_down)
+
+
+def input_back_kernel(count, heads_wide, tiles, *refs):
+    d_heads, rest = refs[:count], refs[count:]
+    tokens, cotangent, before, w_qkv, attn_gain = rest[:5]
+    outs, (sums, bias_sum, branch_sum) = rest[5:9], rest[9:]
+
+    @pl.when(pl.program_id(0) == 0)
+    def _():
+        for held in (sums, bias_sum, branch_sum):
+            held[...] = jnp.zeros(held.shape, jnp.float32)
+
+    d_in = None
+    for number, part in enumerate(d_heads):
+        columns = slice(number * heads_wide, (number + 1) * heads_wide)
+        low = part[:, :heads_wide]
+        term = times_trans(low, w_qkv[:, columns])
+        d_in = term if d_in is None else d_in + term
+        bias_sum[:, columns] += jnp.sum(low.astype(jnp.float32), axis=0, keepdims=True)
+    normed, _ = normed_rows(tokens[...])
+    sums[0:1, :] += jnp.sum(d_in * normed, axis=0, keepdims=True)
+    sums[1:2, :] += jnp.sum(d_in, axis=0, keepdims=True)
+    branch_sum[...] += jnp.sum(cotangent[...].astype(jnp.float32), axis=0, keepdims=True)
+    total = d_in * attn_gain[...] + before[...]
+    for number, out in enumerate(outs):
+
+        @pl.when(pl.program_id(0) == number)
+        def _(out=out):
+            out[...] = total
+
+
+def input_back(tiles, d_heads, heads_wide, tokens, cotangent, before, w_qkv, attn_gain):
+    rows, width = tokens.shape
+    tile = rows // 4
+    shape = jax.ShapeDtypeStruct
+    outs = quarter_outs(rows, width) + (
+        shape((2, width), jnp.float32),
+        shape((1, w_qkv.shape[1]), jnp.float32),
+        shape((1, width), jnp.float32),
+    )
+    return pl.pallas_call(
+        functools.partial(input_back_kernel, len(d_heads), heads_wide),
+        grid_spec=pltpu.PrefetchScalarGridSpec(
+            num_scalar_prefetch=1,
+            grid=(4,),
+            in_specs=[tiled(part.shape[1], tile, picked) for part in d_heads]
+            + [tiled(width, tile, picked)] * 3
+            + [whole(w_qkv), whole(attn_gain)],
+            out_specs=tuple(whole(out) for out in outs),
+        ),
+        out_shape=outs,
+        compiler_params=PARAMS,
+    )(tiles, *d_heads, tokens, cotangent, before, w_qkv, attn_gain)
+
+
+def gradient_kernel(wide, tiles, first_mat, *refs):
+    parts, (away, keep) = refs[:-2], refs[-2:]
+    for number, part in enumerate(parts):
+        block = inner_rows(first_mat[...], part[:, :wide])
+        columns = slice(number * wide, (number + 1) * wide)
+
+        @pl.when(pl.program_id(0) < pl.num_programs(0) // 2)
+        def _(block=block, columns=columns):
+            away[:, columns] = block
+
+        @pl.when(pl.program_id(0) >= pl.num_programs(0) // 2)
+        def _(block=block, columns=columns):
+            keep[:, columns] = block
+
+
+def gradient(core, first_mat, parts, wide):
+    count, rows = first_mat.shape
+    steps = 4 if rows >= 1024 else 2
+    tile = rows // steps
+    if tile % 128:
+        full = inner_rows(
+            first_mat, jnp.concatenate([part[:, :wide] for part in parts], axis=1)
+        )
+        return tuple(
+            lax.dynamic_slice_in_dim(full, side * (rows // 2), rows // 2, 0)
+            for side in (1 - core, core)
+        )
+    half = steps // 2
+    tiles = (jnp.arange(steps, dtype=jnp.int32) + (1 - core) * half) % steps
+    out = jax.ShapeDtypeStruct((rows // 2, wide * len(parts)), jnp.float32)
+    columns = wide * len(parts)
+    return pl.pallas_call(
+        functools.partial(gradient_kernel, wide),
+        grid_spec=pltpu.PrefetchScalarGridSpec(
+            num_scalar_prefetch=1,
+            grid=(steps,),
+            in_specs=[pl.BlockSpec((count, tile), lambda i, tiles: (0, tiles[i]))]
+            + [whole(part) for part in parts],
+            out_specs=(
+                tiled(columns, tile, lambda i, tiles: jnp.minimum(i, half - 1)),
+                tiled(columns, tile, lambda i, tiles: jnp.maximum(i - half, 0)),
+            ),
+        ),
+        out_shape=(out, out),
+        compiler_params=PARAMS,
+    )(tiles, first_mat, *parts)
 
 
 class Order:
@@ -281,16 +529,18 @@
     return [(i, i ^ bit) for i in range(size)]
 
 
-def tensor_steps(array, size, order, between):
+def tensor_steps(away, keep, size, order, between):
     place = lax.axis_index("tensor")
     first = 0
-    for bit in order:
-        half = array.shape[0] // 2
+    rows = away.shape[0]
+    for number, bit in enumerate(order):
         mine = (place // bit) % 2
-        away = lax.dynamic_slice_in_dim(array, (1 - mine) * half, half, 0)
-        got = yield away, "tensor", swap_pairs(size, bit)
-        array = lax.dynamic_slice_in_dim(array, mine * half, half, 0) + got
-        first = first + mine * half
+        if number:
+            rows = rows // 2
+            away = lax.dynamic_slice_in_dim(array, (1 - mine) * rows, rows, 0)
+            keep = lax.dynamic_slice_in_dim(array, mine * rows, rows, 0)
+        array = keep + (yield away, "tensor", swap_pairs(size, bit))
+        first = first + mine * rows
     array = between(array, first)
     for bit in reversed(order):
         got = yield array, "tensor", swap_pairs(size, bit)
@@ -303,12 +553,13 @@
     return array
 
 
-def core_steps(array, size):
-    core = lax.axis_index("dp") % 2
-    half = array.shape[0] // 2
-    away = lax.dynamic_slice_in_dim(array, (1 - core) * half, half, 0)
+def core_steps(parts, size, chunks):
+    away, keep = parts
     got = yield away, "dp", swap_pairs(size, 1)
-    return lax.dynamic_slice_in_dim(array, core * half, half, 0) + got
+    rows = keep.shape[0] // chunks
+    return [
+        keep[c * rows : (c + 1) * rows] + got[c * rows : (c + 1) * rows] for c in range(chunks)
+    ]
 
 
 def line_steps(array, size, back=True):
@@ -348,11 +599,6 @@
     low = [jnp.where(core == 0, mine, other) for mine, other in parts]
     high = [jnp.where(core == 0, other, mine) for mine, other in parts]
     return jnp.concatenate(low + high, axis=0)
-
-
-def halves(array, chunks):
-    rows = array.shape[0] // chunks
-    return [array[c * rows : (c + 1) * rows] for c in range(chunks)]
 
 
 def shards(
@@ -376,97 +622,88 @@
     rows_here, width = tokens.shape
     heads = w_qkv.shape[1] // (3 * HD)
     group = 2 if heads % 2 == 0 else heads
-    lanes = -(-3 * HD * group // 128) * 128
+    wide = 3 * HD * group
+    lanes = -(-wide // 128) * 128
+    groups = heads // group
     bits = [1 << k for k in range(tensor_size.bit_length() - 1)]
     orders = (bits, bits[::-1])
     split = rows_here // 2
-    order = Order(lax.axis_index("dp") % 2)
+    core = lax.axis_index("dp") % 2
+    place = lax.axis_index("tensor")
+    order = Order(core)
     run = order.run
+    mine = [(place // its[0]) % 2 for its in orders]
+    tiles = jnp.stack([1 - mine[0], 3 - mine[1], mine[0], 2 + mine[1]]).astype(jnp.int32)
 
     def chain(steps):
         return Chain(order, steps)
 
-    def norm(tokens):
-        rows = tokens.astype(jnp.float32)
-        centred = rows - jnp.mean(rows, axis=-1, keepdims=True)
-        scale_inv = lax.rsqrt(jnp.mean(centred * centred, axis=-1, keepdims=True) + EPS)
-        normed = centred * scale_inv
-        return (
-            (normed * attn_gain + attn_shift).astype(jnp.bfloat16),
-            (normed * mlp_gain + mlp_shift).astype(jnp.bfloat16),
-            normed,
-            scale_inv,
-        )
-
-    def feed(mlp_low, w_up):
-        pre_act = product(mlp_low, w_up) + b_up
-        below = 0.5 * (1.0 + lax.erf(pre_act * (0.5**0.5)))
-        bell = jnp.exp(-0.5 * pre_act * pre_act) * ((2.0 * math.pi) ** -0.5)
-        return (pre_act * below).astype(jnp.bfloat16), below + pre_act * bell
-
-    def project(attn_low, w_qkv):
-        projected = product(attn_low, w_qkv) + b_qkv
-        if group * 3 * HD != lanes:
-            projected = jnp.pad(projected, ((0, 0), (0, lanes - group * 3 * HD)))
-        return projected
-
-    attn_low, mlp_low, normed, scale_inv = run(norm, tokens)
-    hidden, slope = run(feed, mlp_low, w_up)
-    core_down = chain(core_steps(run(inner_rows, hidden, cotangent), dp_size))
-    projected = run(project, attn_low, w_qkv)
+    def lines(core_chain):
+        return [line_steps(part, dp_size) for part in core_chain.end()]
+
+    def grads(chunks, first_mat, *parts, wide=None):
+        def step(first_mat, *parts):
+            return gradient(core, first_mat, parts, wide or parts[0].shape[1])
+
+        return chain(core_steps(run(step, first_mat, *parts), dp_size, chunks))
+
+    vectors = [v[None, :] for v in (attn_gain, attn_shift, mlp_gain, mlp_shift)]
+    attn_low, mlp_low, projected, d_attended, hidden, slope = run(
+        lambda *a: forward(a[0], a[1], vectors, *a[2:], lanes=lanes * groups),
+        tokens,
+        cotangent,
+        w_qkv,
+        b_qkv[None, :],
+        w_out,
+        w_up,
+        b_up[None, :],
+    )
+    core_down = grads(2, hidden, cotangent)
+    d_pre, scaled_mlp, sums_mlp, up_bias = run(
+        feed_back, tokens, cotangent, slope, w_down, w_up, mlp_gain[None, :]
+    )
+    down = lines(core_down)
+    down[0] = chain(down[0])
+    core_up = grads(2, mlp_low, d_pre)
     angles = run(turn_angles, segment[0])
-    d_attended = run(
-        lambda dy, w: times_trans(dy, w).astype(jnp.bfloat16), cotangent, w_out
-    )
-    down = [line_steps(part, dp_size) for part in halves(core_down.end(), 2)]
-    down[0] = chain(down[0])
     kept = run(functools.partial(attend, heads=heads), angles, projected)
     attended = kept[0]
-
-    def branches(attended, hidden):
-        return tuple(
-            product(attended[rows], w_out) + product(hidden[rows], w_down)
-            for rows in (slice(0, split), slice(split, None))
-        )
-
-    partial = run(branches, attended, hidden)
+    partial = run(branches, tiles, attended, hidden, w_out, w_down)
     result = [
-        chain(tensor_steps(part, tensor_size, its, lambda rows, first: rows))
-        for part, its in zip(partial, orders, strict=True)
+        chain(tensor_steps(partial[p], partial[2 + p], tensor_size, orders[p], lambda rows, first: rows))
+        for p in range(2)
     ]
-    d_pre = run(
-        lambda dy, w, slope: (times_trans(dy, w) * slope).astype(jnp.bfloat16),
-        cotangent,
-        w_down,
-        slope,
-    )
-    core_up = chain(core_steps(run(inner_rows, mlp_low, d_pre), dp_size))
+    up = lines(core_up)
     down[0].on()
     down[1] = chain(down[1])
-    d_mlp_in = run(times_trans, d_pre, w_up)
-    up = [line_steps(part, dp_size) for part in halves(core_up.end(), 2)]
-    result[0].on()
-    result[1].on()
 
     back = []
     for begin in range(0, heads, group):
         def step(angles, d_attended, *kept, begin=begin):
             return attend_back(angles, kept, d_attended, begin, group, lanes)
 
-        back.append(run(step, angles, d_attended, *kept)[:, : group * 3 * HD])
-        result[0].on()
-        result[1].on()
-        if begin == 0:
-            down[0].on()
-            down[1].on()
-            up[0] = chain(up[0])
-
-    def backward(w_qkv, d_mlp_in, *back):
-        d_projected = jnp.concatenate(back, axis=1)
-        d_attn_in = times_trans(d_projected, w_qkv)
-        return d_projected, d_attn_in, d_attn_in * attn_gain + d_mlp_in * mlp_gain
-
-    d_projected, d_attn_in, scaled = run(backward, w_qkv, d_mlp_in, *back)
+        back.append(run(step, angles, d_attended, *kept))
+    *scaled, sums_attn, qkv_bias, branch_sum = run(
+        lambda tiles, *a: input_back(tiles, a[:-5], wide, *a[-5:]),
+        tiles,
+        *back,
+        tokens,
+        cotangent,
+        scaled_mlp,
+        w_qkv,
+        attn_gain[None, :],
+    )
+    for part in result:
+        part.on()
+    core_qkv = grads(2, attn_low, *back, wide=wide)
+    down[0].on()
+    down[1].on()
+    up[0] = chain(up[0])
+    core_out = grads(1, attended, cotangent)
+    qkv = lines(core_qkv)
+    for part in result:
+        part.on()
+    out = lines(core_out)[0]
 
     def norm_back(part):
         def between(rows, first):
@@ -475,85 +712,74 @@
             def here(whole):
                 return lax.dynamic_slice_in_dim(whole, at, rows.shape[0], 0)
 
-            normed_here = here(normed)
-            return here(cotangent).astype(jnp.float32) + here(scale_inv) * (
+            normed, scale_inv = normed_rows(here(tokens))
+            return here(cotangent).astype(jnp.float32) + scale_inv * (
                 rows
                 - jnp.mean(rows, axis=-1, keepdims=True)
-                - normed_here * jnp.mean(rows * normed_here, axis=-1, keepdims=True)
+                - normed * jnp.mean(rows * normed, axis=-1, keepdims=True)
             )
 
         return between
 
-    d_tokens = [
-        chain(tensor_steps(scaled[p * split : (p + 1) * split], tensor_size, its, norm_back(p)))
-        for p, its in enumerate(orders)
-    ]
-    core_qkv = chain(core_steps(run(inner_rows, attn_low, d_projected), dp_size))
-    down[0].on()
-    down[1].on()
-    up[0].on()
+    for part in result:
+        part.on()
+    for part in (down[0], down[1], up[0]):
+        part.on()
     up[1] = chain(up[1])
-    core_out = chain(core_steps(run(inner_rows, attended, cotangent), dp_size))
-
-    def sums(d_attn_in, d_mlp_in, normed):
-        return jnp.stack(
-            [
-                jnp.sum(d_attn_in * normed, axis=0),
-                jnp.sum(d_attn_in, axis=0),
-                jnp.sum(d_mlp_in * normed, axis=0),
-                jnp.sum(d_mlp_in, axis=0),
-            ]
+    small = chain(
+        small_steps(
+            jnp.concatenate([sums_attn, sums_mlp], axis=0),
+            [v[0] for v in (qkv_bias, up_bias, branch_sum)],
+            tensor_size,
+            dp_size,
         )
-
-    def columns(*arrays):
-        return tuple(jnp.sum(array.astype(jnp.float32), axis=0) for array in arrays)
-
-    stats = run(sums, d_attn_in, d_mlp_in, normed)
-    rest = run(columns, d_projected, d_pre, cotangent)
-    small = chain(small_steps(stats, rest, tensor_size, dp_size))
-    qkv = [line_steps(part, dp_size) for part in halves(core_qkv.end(), 2)]
-    out = line_steps(core_out.end(), dp_size)
+    )
+    down[0].end()
     small.on()
 
     def finish(tokens, *parts):
         summed = jnp.concatenate(parts, axis=0)
         return (tokens.astype(jnp.float32) + summed + b_branch).astype(jnp.bfloat16)
 
-    result = run(finish, tokens, *(part.end() for part in result))
+    ended = [part.end() for part in result]
+    d_tokens = [
+        chain(tensor_steps(scaled[p], scaled[2 + p], tensor_size, orders[p], norm_back(p)))
+        for p in range(2)
+    ]
+    result = run(finish, tokens, *ended)
+    for part in (down[1], up[0], up[1]):
+        part.on()
+    qkv[0] = chain(qkv[0])
+    small.on()
     small.on()
     for part in d_tokens:
         part.on()
-    for part in (down[0], down[1], up[0], up[1]):
-        part.on()
-    qkv[0] = chain(qkv[0])
+    down[1].end()
+    grad_down = run(lambda *p: assemble(p[0], (p[1:3], p[3:5])), core, *down[0].end(), *down[1].end())
+    for part in (up[0], up[1], qkv[0]):
+        part.on()
+    qkv[1] = chain(qkv[1])
+    for part in d_tokens:
+        part.on()
     small.on()
-    for part in d_tokens:
-        part.on()
-    small.on()
-    for part in (down[1], up[0], up[1], qkv[0]):
-        part.on()
-    qkv[1] = chain(qkv[1])
-    small.on()
-    for part in d_tokens:
-        part.on()
-    grad_down = run(lambda *p: assemble(p[0], (p[1:3], p[3:5])), order.token, *down[0].end(), *down[1].end())
-    for part in (up[0], up[1], qkv[0], qkv[1]):
+    up[0].end()
+    for part in (up[1], qkv[0], qkv[1]):
         part.on()
     out = chain(out)
     for part in d_tokens:
         part.on()
-    for part in (up[1], qkv[0], qkv[1], out):
+    up[1].end()
+    grad_up = run(lambda *p: assemble(p[0], (p[1:3], p[3:5])), core, *up[0].end(), *up[1].end())
+    for part in (out, qkv[0], qkv[1]):
+        part.on()
+    vectors = small.end()
+    qkv[0].end()
+    for part in (out, qkv[1]):
         part.on()
     d_tokens = run(lambda *p: jnp.concatenate(p, axis=0), *(part.end() for part in d_tokens))
-    grad_up = run(lambda *p: assemble(p[0], (p[1:3], p[3:5])), order.token, *up[0].end(), *up[1].end())
-    vectors = small.end()
-    for part in (qkv[0], qkv[1], out):
-        part.on()
-    qkv[0].end(), qkv[1].end()
-    out.on()
-    grad_qkv = run(lambda *p: assemble(p[0], (p[1:3], p[3:5])), order.token, *qkv[0].end(), *qkv[1].end())
-    grad_out = out.end()
-    grad_out = assemble(order.token, (grad_out,))
+    qkv[1].end()
+    grad_qkv = run(lambda *p: assemble(p[0], (p[1:3], p[3:5])), core, *qkv[0].end(), *qkv[1].end())
+    grad_out = assemble(order.token, (out.end(),))
 
     sizes = (width,) * 4 + (w_qkv.shape[1], w_up.shape[1], width)
     ends = [sum(sizes[: k + 1]) for k in range(len(sizes))]

time: 377 us -> 396 us (1.050)
  Pallas kernels: 27.7 us -> 75.3 us
  matrix products: 31.3 us -> 0 us
  other arithmetic: 74 us -> 88.5 us
  starting transfers between devices: 82.5 us -> 69.7 us
  waiting for transfers between devices: 130 us -> 122 us
  local copies, waits for them, and re-layouts: 25 us -> 31.9 us
    pallas_call x0 -> x8, Pallas kernels: none -> 48.1 us  [the longest x4 17.4 us: gradient(): pl.pallas_call(functools.partial(gradient_kernel, wide), grid_spec=pltpu....]
    dot_general x14 -> x0, matrix products: 31.3 us -> none  [the longest x6 14.5 us: product(): return jnp.dot(first_mat, second_mat, preferred_element_type=jnp.float32)]
    add x13 -> x16, other arithmetic: 7.78 us -> 25 us  [line_steps(): array = array + got]
    unnamed x144 -> x161, local copies, waits for them, and re-layouts: 11.8 us -> 26.6 us
    ppermute x54, starting transfers between devices: 82.5 us -> 69.7 us  [_go(): self.held = lax.ppermute(array, axis, pairs)]
    add x10, other arithmetic: 8.76 us -> 16.6 us  [the longest x4 10.4 us: core_steps(): keep[c * rows:(c + 1) * rows] + got[c * rows:(c + 1) * rows]]
    ppermute x54, waiting for transfers between devices: 130 us -> 122 us  [_go(): self.held = lax.ppermute(array, axis, pairs)]
    dynamic_slice x11 -> x4, local copies, waits for them, and re-layouts: 10.1 us -> 3.45 us  [tensor_steps(): away = lax.dynamic_slice_in_dim(array, (1 - mine) * rows, rows, 0)]
  transfers between devices with their start and end apart: 54 -> 54, of which waited for: 19 -> 16; matrix products, arithmetic and copies ran while one was open for 22% -> 22% of each run, Pallas kernels for 4% -> 13%
where the time goes in v3:
time: 396 us; the launch traced here: 390 us
  waiting for transfers between devices  122 us (31%)
  other arithmetic  88.5 us (22%)
  Pallas kernels  75.3 us (19%)
  starting transfers between devices  69.7 us (18%)
  local copies, waits for them, and re-layouts  31.9 us (8%)
    ppermute x54, waiting for transfers between devices, _go(): self.held = lax.ppermute(array, axis, pairs)  122 us
    ppermute x54, starting transfers between devices, _go(): self.held = lax.ppermute(array, axis, pairs)  69.7 us
    unnamed x161, local copies, waits for them, and re-layouts  26.6 us
    add x16, other arithmetic, line_steps(): array = array + got  25 us
    pallas_call x4, Pallas kernels, gradient(): pl.pallas_call(functools.partial(gradient_kernel, wide), grid_spec=pltpu....  17.4 us
    pallas_call x2, Pallas kernels, attend_back(): pl.pallas_call(functools.partial(attend_back_kernel, begin, heads), out_s...  14.5 us
    pallas_call x1, Pallas kernels, attend(): pl.pallas_call(functools.partial(attend_kernel, heads), out_shape=(shape(...  12.7 us
    select_n x8, other arithmetic, tensor_steps(): jnp.where(mine == 0, jnp.concatenate([array, got], axis=0), jnp.concatena...  11.1 us
  transfers between devices with their start and end apart: 54, of which 16 were waited for; matrix products, arithmetic and copies ran while one was open for 22% of the time, Pallas kernels for 13%

profile of v3, /device:TPU:0, one launch (start us, length us, event | category | flops | bytes accessed | tf_op | source)
XLA Modules:
  0.0 389.9 jit_solution(10065399072203365909)
XLA Ops:
  10.4 10.5 %shard_map.237 = (bf16[1024,1024]{1,0:T(8,128)(2,1)S(1)}, bf16[1024,1024]{1,0:T(8,128)(2,1)S(1)}, f32[1024,768]{1,0:T(8,128)}, bf16[1024,256]{1,0:T(8,128)(2,1)S...) custom-call(bf16[1024,1024]{1,0:T(8,128)(2,1)S(1)} %copy-done.2, bf16[1024,1024]{1,0:T(8,128)(2,1)S(1)} %copy-done, ...), custom_call_target="tpu_custom_call" | custom-call | tf_op jit(solution)/shard_map/pallas_call | solution.py:296
  32.8 8.3 %shard_map.239 = (bf16[1024,1024]{1,0:T(8,128)(2,1)S(1)}, f32[1024,1024]{1,0:T(8,128)}, f32[2,1024]{1,0:T(2,128)S(1)}, f32[1,1024]{1,0:T(1,128)S(1)}) custom-call(bf16[1024,1024]{1,0:T(8,128)(2,1)S(1)} %copy-done.3, bf16[1024,1024]{1,0:T(8,128)(2,1)S(1)} %copy-done.1, f32[1024,1024]{1,0:T(8,128)} %get-tuple-element.414.slope, ...), custom_call_target="tpu_custom_call" | custom-call | tf_op jit(solution)/shard_map/pallas_call | solution.py:336
  43.1 5.1 %shard_map.240 = (f32[512,1024]{1,0:T(8,128)}, f32[512,1024]{1,0:T(8,128)S(1)}) custom-call(s32[4]{0:T(128)S(1)} %get-tuple-element.808.tiles, bf16[1024,1024]{1,0:T(8,128)(2,1)S(1)} %copy-done.26, bf16[1024,1024]{1,0:T(8,128)(2,1)S(1)} %get-tuple-element.431.refs_0_), custom_call_target="tpu_custom_call" | custom-call | tf_op jit(solution)/shard_map/pallas_call | solution.py:469
  48.3 6.6 %collective-permute-start.2 = (f32[256,1024]{1,0:T(8,128)}, f32[256,1024]{1,0:T(8,128)}, u32[]{:S(2)}, u32[]{:S(2)}) collective-permute-start(f32[256,1024]{1,0:T(8,128)} %get-tuple-element.466), channel_id=1, source_target_pairs={{0,8},{4,12},{24,16},{28,20},{1,9},{5,13},{25,17},{29,21},{2,10},{... | collective-permute-start | bytes 3145736 | tf_op jit(solution)/shard_map/ppermute | solution.py:515
  57.7 12.7 %shard_map.241 = (bf16[1024,256]{1,0:T(8,128)(2,1)S(1)}, f32[1024,128]{1,0:T(8,128)S(1)}, bf16[4,1024,64]{2,1,0:T(8,128)(2,1)S(1)}, bf16[4,1024,64]{2,1,0:T(8,128)(2,1)S(1)}, bf16[4,1024,64]{2,1,0:T(8,128)(2,1)S(1)}) custom-call(f32[24,1024]{1,0:T(8,128)S(1)} %pad_maximum_fusion.5.angles, f32[1024,768]{1,0:T(8,128)S(1)} %copy-done.21), custom_call_target="tpu_custom_call" | custom-call | tf_op jit(solution)/shard_map/pallas_call | solution.py:197
  73.5 5.7 %shard_map.242 = (f32[256,1024]{1,0:T(8,128)}, f32[256,1024]{1,0:T(8,128)}, f32[256,1024]{1,0:T(8,128)S(1)}, f32[256,1024]{1,0:T(8,128)S(1)}) custom-call(s32[4]{0:T(128)S(1)} %get-tuple-element.495.tiles, bf16[1024,256]{1,0:T(8,128)(2,1)S(1)} %get-tuple-element.541.attended.first_mat, bf16[1024,1024]{1,0:T(8,128)(2,1)S(1)} %copy-done.10, ...), custom_call_target="tpu_custom_call" | custom-call | tf_op jit(solution)/shard_map/pallas_call | solution.py:367
  88.1 7.1 %shard_map.243.refs_0_ = bf16[1024,384]{1,0:T(8,128)(2,1)S(1)} custom-call(f32[24,1024]{1,0:T(8,128)S(1)} %pad_maximum_fusion.5.angles, bf16[4,1024,64]{2,1,0:T(8,128)(2,1)S(1)} %copy-done.16, bf16[4,1024,64]{2,1,0:T(8,128)(2,1)S(1)} %copy-done.18, bf16[4,1024,64]{2,1,0:T(8,128)(2,1)S(1)} %copy-done.20, f32[1024,128]{1,0:T(8,128)S(1)} %copy-done.30, ...), custom_call_target="tpu_custom_call" | custom-call | tf_op jit(solution)/shard_map/pallas_call | solution.py:215
  95.3 7.4 %shard_map.244.refs_1_ = bf16[1024,384]{1,0:T(8,128)(2,1)S(1)} custom-call(f32[24,1024]{1,0:T(8,128)S(1)} %pad_maximum_fusion.5.angles, bf16[4,1024,64]{2,1,0:T(8,128)(2,1)S(1)} %copy-done.16, bf16[4,1024,64]{2,1,0:T(8,128)(2,1)S(1)} %copy-done.18, bf16[4,1024,64]{2,1,0:T(8,128)(2,1)S(1)} %copy-done.20, f32[1024,128]{1,0:T(8,128)S(1)} %copy-done.30, ...), custom_call_target="tpu_custom_call" | custom-call | tf_op jit(solution)/shard_map/pallas_call | solution.py:215
  102.8 6.1 %shard_map.245 = (f32[256,1024]{1,0:T(8,128)S(1)}, f32[256,1024]{1,0:T(8,128)S(1)}, f32[256,1024]{1,0:T(8,128)S(1)}, f32[256,1024]{1,0:T(8,128)S(1)}, f32[2,1024...) custom-call(s32[4]{0:T(128)S(1)} %get-tuple-element.495.tiles, ...), custom_call_target="tpu_custom_call" | custom-call | tf_op jit(solution)/shard_map/pallas_call | solution.py:423
  116.6 5.8 %shard_map.246 = (f32[512,768]{1,0:T(8,128)}, f32[512,768]{1,0:T(8,128)S(1)}) custom-call(s32[4]{0:T(128)S(1)} %get-tuple-element.808.tiles, bf16[1024,1024]{1,0:T(8,128)(2,1)S(1)} %copy-done.24, bf16[1024,384]{1,0:T(8,128)(2,1)S(1)} %shard_map.243.refs_0_, bf16[1024,384]{1,0:T(8,128)(2,1)S(1)} %shard_map.244.refs_1_), custom_call_target="tpu_custom_call" | custom-call | tf_op jit(solution)/shard_map/pallas_call | solution.py:469
  136.1 14.3 %collective-permute-done.6 = f32[256,1024]{1,0:T(8,128)} collective-permute-done((f32[256,1024]{1,0:T(8,128)}, f32[256,1024]{1,0:T(8,128)}, u32[]{:S(2)}, u32[]{:S(2)}) %collective-permute-start.6) | collective-permute-done | bytes 1048608 | tf_op jit(solution)/shard_map/ppermute | solution.py:515
  161.6 8.1 %collective-permute-start.15 = (f32[256,1024]{1,0:T(8,128)}, f32[256,1024]{1,0:T(8,128)}, u32[]{:S(2)}, u32[]{:S(2)}) collective-permute-start(f32[256,1024]{1,0:T(8,128)} %get-tuple-element.576), channel_id=1, source_target_pairs={{0,8},{4,12},{24,16},{28,20},{1,9},{5,13},{25,17},{29,21},{2,10},{... | collective-permute-start | bytes 3145736 | tf_op jit(solution)/shard_map/ppermute | solution.py:515
  177.6 5.8 %collective-permute-done.13 = f32[256,1024]{1,0:T(8,128)} collective-permute-done((f32[256,1024]{1,0:T(8,128)}, f32[256,1024]{1,0:T(8,128)}, u32[]{:S(2)}, u32[]{:S(2)}) %collective-permute-start.13) | collective-permute-done | bytes 1048608 | tf_op jit(solution)/shard_map/ppermute | solution.py:515
  198.2 13.8 %collective-permute-done.17 = f32[4,1024]{1,0:T(4,128)S(1)} collective-permute-done((f32[4,1024]{1,0:T(4,128)S(1)}, f32[4,1024]{1,0:T(4,128)S(1)}, u32[]{:S(2)}, u32[]{:S(2)}) %collective-permute-start.17) | collective-permute-done | bytes 16416 | tf_op jit(solution)/shard_map/ppermute | solution.py:515
  229.1 7.2 %collective-permute-done.22 = f32[256,1024]{1,0:T(8,128)S(1)} collective-permute-done((f32[256,1024]{1,0:T(8,128)}, f32[256,1024]{1,0:T(8,128)S(1)}, u32[]{:S(2)}, u32[]{:S(2)}) %collective-permute-start.22) | collective-permute-done | bytes 1048608 | tf_op jit(solution)/shard_map/ppermute | solution.py:515
  240.5 7.4 %collective-permute-done.25 = f32[256,1024]{1,0:T(8,128)S(1)} collective-permute-done((f32[256,1024]{1,0:T(8,128)S(1)}, f32[256,1024]{1,0:T(8,128)S(1)}, u32[]{:S(2)}, u32[]{:S(2)}) %collective-permute-start.25) | collective-permute-done | bytes 1048608 | tf_op jit(solution)/shard_map/ppermute | solution.py:515
  273.4 10.5 %collective-permute-done.32 = f32[128,1024]{1,0:T(8,128)S(1)} collective-permute-done((f32[128,1024]{1,0:T(8,128)S(1)}, f32[128,1024]{1,0:T(8,128)S(1)}, u32[]{:S(2)}, u32[]{:S(2)}) %collective-permute-start.32) | collective-permute-done | bytes 524320 | tf_op jit(solution)/shard_map/ppermute | solution.py:515
  283.9 4.4 %collective-permute-start.37 = (f32[256,768]{1,0:T(8,128)S(1)}, f32[256,768]{1,0:T(8,128)S(1)}, u32[]{:S(2)}, u32[]{:S(2)}) collective-permute-start(f32[256,768]{1,0:T(8,128)S(1)} %get-tuple-element.686), channel_id=1, source_target_pairs={{0,8},{4,12},{24,16},{28,20},{1,9},{5,13},{25,17},{29,21},{2,10},{... | collective-permute-start | bytes 2359304 | tf_op jit(solution)/shard_map/ppermute | solution.py:515
  288.9 9.8 %collective-permute-done.35 = f32[256,1024]{1,0:T(8,128)S(1)} collective-permute-done((f32[256,1024]{1,0:T(8,128)S(1)}, f32[256,1024]{1,0:T(8,128)S(1)}, u32[]{:S(2)}, u32[]{:S(2)}) %collective-permute-start.35) | collective-permute-done | bytes 1048608 | tf_op jit(solution)/shard_map/ppermute | solution.py:515
  305.1 5.0 %collective-permute-start.41 = (f32[128,1024]{1,0:T(8,128)}, f32[128,1024]{1,0:T(8,128)}, u32[]{:S(2)}, u32[]{:S(2)}) collective-permute-start(f32[128,1024]{1,0:T(8,128)} %add.295), channel_id=1, source_target_pairs={{0,8},{4,12},{24,16},{28,20},{1,9},{5,13},{25,17},{29,21},{2,10},{... | collective-permute-start | bytes 1572872 | tf_op jit(solution)/shard_map/ppermute | solution.py:515
  322.5 6.5 %collective-permute-done.42 = f32[256,768]{1,0:T(8,128)} collective-permute-done((f32[256,768]{1,0:T(8,128)}, f32[256,768]{1,0:T(8,128)}, u32[]{:S(2)}, u32[]{:S(2)}) %collective-permute-start.42) | collective-permute-done | bytes 786464 | tf_op jit(solution)/shard_map/ppermute | solution.py:515
  337.2 17.0 %collective-permute-done.45 = f32[6912]{0:T(1024)S(1)} collective-permute-done((f32[6912]{0:T(1024)S(1)}, f32[6912]{0:T(1024)S(1)}, u32[]{:S(2)}, u32[]{:S(2)}) %collective-permute-start.45) | collective-permute-done | bytes 27680 | tf_op jit(solution)/shard_map/ppermute | solution.py:515
  356.1 4.6 %collective-permute-done.49 = f32[256,1024]{1,0:T(8,128)S(1)} collective-permute-done((f32[256,1024]{1,0:T(8,128)S(1)}, f32[256,1024]{1,0:T(8,128)S(1)}, u32[]{:S(2)}, u32[]{:S(2)}) %collective-permute-start.49) | collective-permute-done | bytes 1048608 | tf_op jit(solution)/shard_map/ppermute | solution.py:515
  369.9 16.3 %collective-permute-done.52 = f32[128,1024]{1,0:T(8,128)S(1)} collective-permute-done((f32[128,1024]{1,0:T(8,128)}, f32[128,1024]{1,0:T(8,128)S(1)}, u32[]{:S(2)}, u32[]{:S(2)}) %collective-permute-start.52) | collective-permute-done | bytes 524320 | tf_op jit(solution)/shard_map/ppermute | solution.py:515
  (345 shorter events, 181.4 us)
Async XLA Ops:
  48.2 36.0 %collective-permute-start.1 = (f32[512,1024]{1,0:T(8,128)}, f32[512,1024]{1,0:T(8,128)}, u32[]{:S(2)}, u32[]{:S(2)}) collective-permute-start(f32[512,1024]{1,0:T(8,128)} %get-tuple-element.464), channel_id=1, source_target_pairs={{0,4},{4,0},{8,12},{12,8},{16,20},{20,16},{24,28},{28,24},{1,5},{5... | collective-permute-start | bytes 6291464 | tf_op jit(solution)/shard_map/ppermute | solution.py:515
  48.3 35.9 %collective-permute-start.2 = (f32[256,1024]{1,0:T(8,128)}, f32[256,1024]{1,0:T(8,128)}, u32[]{:S(2)}, u32[]{:S(2)}) collective-permute-start(f32[256,1024]{1,0:T(8,128)} %get-tuple-element.466), channel_id=1, source_target_pairs={{0,8},{4,12},{24,16},{28,20},{1,9},{5,13},{25,17},{29,21},{2,10},{... | collective-permute-start | bytes 3145736 | tf_op jit(solution)/shard_map/ppermute | solution.py:515
  81.1 27.9 %collective-permute-start.3 = (f32[256,1024]{1,0:T(8,128)}, f32[256,1024]{1,0:T(8,128)}, u32[]{:S(2)}, u32[]{:S(2)}) collective-permute-start(f32[256,1024]{1,0:T(8,128)} %get-tuple-element.511), channel_id=1, source_target_pairs={{0,1},{1,0},{2,3},{3,2},{4,5},{5,4},{6,7},{7,6},{8,9},{9,8},{10,11... | collective-permute-start | bytes 3145736 | tf_op jit(solution)/shard_map/ppermute | solution.py:515
  82.6 30.5 %collective-permute-start.4 = (f32[256,1024]{1,0:T(8,128)}, f32[256,1024]{1,0:T(8,128)}, u32[]{:S(2)}, u32[]{:S(2)}) collective-permute-start(f32[256,1024]{1,0:T(8,128)} %get-tuple-element.516), channel_id=1, source_target_pairs={{0,2},{1,3},{2,0},{3,1},{4,6},{5,7},{6,4},{7,5},{8,10},{9,11},{10,... | collective-permute-start | bytes 3145736 | tf_op jit(solution)/shard_map/ppermute | solution.py:515
  123.5 33.4 %collective-permute-start.7 = (f32[512,768]{1,0:T(8,128)}, f32[512,768]{1,0:T(8,128)}, u32[]{:S(2)}, u32[]{:S(2)}) collective-permute-start(f32[512,768]{1,0:T(8,128)} %get-tuple-element.548), channel_id=1, source_target_pairs={{0,4},{4,0},{8,12},{12,8},{16,20},{20,16},{24,28},{28,24},{1,5},{5... | collective-permute-start | bytes 4718600 | tf_op jit(solution)/shard_map/ppermute | solution.py:515
  125.1 25.2 %collective-permute-start.6 = (f32[256,1024]{1,0:T(8,128)}, f32[256,1024]{1,0:T(8,128)}, u32[]{:S(2)}, u32[]{:S(2)}) collective-permute-start(f32[256,1024]{1,0:T(8,128)} %get-tuple-element.534), channel_id=1, source_target_pairs={{0,8},{4,12},{24,16},{28,20},{1,9},{5,13},{25,17},{29,21},{2,10},{... | collective-permute-start | bytes 3145736 | tf_op jit(solution)/shard_map/ppermute | solution.py:515
  128.2 28.6 %collective-permute-start.8 = (f32[128,1024]{1,0:T(8,128)}, f32[128,1024]{1,0:T(8,128)}, u32[]{:S(2)}, u32[]{:S(2)}) collective-permute-start(f32[128,1024]{1,0:T(8,128)} %constant_dynamic-slice_fusion.3), channel_id=1, source_target_pairs={{0,2},{1,3},{2,0},{3,1},{4,6},{5,7},{6,4},{7,5},{8,10},{9,11},{10,... | collective-permute-start | bytes 1572872 | tf_op jit(solution)/shard_map/ppermute | solution.py:515
  128.8 29.2 %collective-permute-start.9 = (f32[128,1024]{1,0:T(8,128)}, f32[128,1024]{1,0:T(8,128)S(1)}, u32[]{:S(2)}, u32[]{:S(2)}) collective-permute-start(f32[128,1024]{1,0:T(8,128)} %constant_dynamic-slice_fusion.2), channel_id=1, source_target_pairs={{0,1},{1,0},{2,3},{3,2},{4,5},{5,4},{6,7},{7,6},{8,9},{9,8},{10,11... | collective-permute-start | bytes 1572872 | tf_op jit(solution)/shard_map/ppermute | solution.py:515
  155.5 27.9 %collective-permute-start.13 = (f32[256,1024]{1,0:T(8,128)}, f32[256,1024]{1,0:T(8,128)}, u32[]{:S(2)}, u32[]{:S(2)}) collective-permute-start(f32[256,1024]{1,0:T(8,128)} %add.254), channel_id=1, source_target_pairs={{8,0},{12,4},{16,24},{20,28},{9,1},{13,5},{17,25},{21,29},{10,2},{... | collective-permute-start | bytes 3145736 | tf_op jit(solution)/shard_map/ppermute | solution.py:515
  160.0 28.2 %collective-permute-start.14 = (f32[256,1024]{1,0:T(8,128)}, f32[256,1024]{1,0:T(8,128)}, u32[]{:S(2)}, u32[]{:S(2)}) collective-permute-start(f32[256,1024]{1,0:T(8,128)} %add.255), channel_id=1, source_target_pairs={{8,16},{12,20},{16,8},{20,12},{9,17},{13,21},{17,9},{21,13},{10,18... | collective-permute-start | bytes 3145736 | tf_op jit(solution)/shard_map/ppermute | solution.py:515
  161.6 30.6 %collective-permute-start.15 = (f32[256,1024]{1,0:T(8,128)}, f32[256,1024]{1,0:T(8,128)}, u32[]{:S(2)}, u32[]{:S(2)}) collective-permute-start(f32[256,1024]{1,0:T(8,128)} %get-tuple-element.576), channel_id=1, source_target_pairs={{0,8},{4,12},{24,16},{28,20},{1,9},{5,13},{25,17},{29,21},{2,10},{... | collective-permute-start | bytes 3145736 | tf_op jit(solution)/shard_map/ppermute | solution.py:515
  185.9 27.7 %collective-permute-start.18 = (f32[256,1024]{1,0:T(8,128)}, f32[256,1024]{1,0:T(8,128)}, u32[]{:S(2)}, u32[]{:S(2)}) collective-permute-start(f32[256,1024]{1,0:T(8,128)} %maximum_select_fusion.4), channel_id=1, source_target_pairs={{0,1},{1,0},{2,3},{3,2},{4,5},{5,4},{6,7},{7,6},{8,9},{9,8},{10,11... | collective-permute-start | bytes 3145736 | tf_op jit(solution)/shard_map/ppermute | solution.py:515
  186.4 27.2 %collective-permute-start.19 = (f32[256,1024]{1,0:T(8,128)}, f32[256,1024]{1,0:T(8,128)}, u32[]{:S(2)}, u32[]{:S(2)}) collective-permute-start(f32[256,1024]{1,0:T(8,128)} %maximum_select_fusion.5), channel_id=1, source_target_pairs={{0,2},{1,3},{2,0},{3,1},{4,6},{5,7},{6,4},{7,5},{8,10},{9,11},{10,... | collective-permute-start | bytes 3145736 | tf_op jit(solution)/shard_map/ppermute | solution.py:515
  190.9 30.4 %collective-permute-start.20 = (f32[256,1024]{1,0:T(8,128)}, f32[256,1024]{1,0:T(8,128)}, u32[]{:S(2)}, u32[]{:S(2)}) collective-permute-start(f32[256,1024]{1,0:T(8,128)} %add.264), channel_id=1, source_target_pairs={{8,0},{12,4},{16,24},{20,28},{9,1},{13,5},{17,25},{21,29},{10,2},{... | collective-permute-start | bytes 3145736 | tf_op jit(solution)/shard_map/ppermute | solution.py:515
  197.4 28.0 %collective-permute-start.21 = (f32[256,1024]{1,0:T(8,128)}, f32[256,1024]{1,0:T(8,128)S(1)}, u32[]{:S(2)}, u32[]{:S(2)}) collective-permute-start(f32[256,1024]{1,0:T(8,128)} %add.265), channel_id=1, source_target_pairs={{8,16},{12,20},{16,8},{20,12},{9,17},{13,21},{17,9},{21,13},{10,18... | collective-permute-start | bytes 3145736 | tf_op jit(solution)/shard_map/ppermute | solution.py:515
  224.0 27.3 %collective-permute-start.26 = (f32[256,1024]{1,0:T(8,128)S(1)}, f32[256,1024]{1,0:T(8,128)S(1)}, u32[]{:S(2)}, u32[]{:S(2)}) collective-permute-start(f32[256,1024]{1,0:T(8,128)S(1)} %copy-done.49), channel_id=1, source_target_pairs={{0,2},{1,3},{2,0},{3,1},{4,6},{5,7},{6,4},{7,5},{8,10},{9,11},{10,... | collective-permute-start | bytes 3145736 | tf_op jit(solution)/shard_map/ppermute | solution.py:515
  225.5 29.4 %collective-permute-start.27 = (f32[256,1024]{1,0:T(8,128)S(1)}, f32[256,1024]{1,0:T(8,128)}, u32[]{:S(2)}, u32[]{:S(2)}) collective-permute-start(f32[256,1024]{1,0:T(8,128)S(1)} %broadcast_select_fusion.10), channel_id=1, source_target_pairs={{0,4},{4,0},{8,12},{12,8},{16,20},{20,16},{24,28},{28,24},{1,5},{5... | collective-permute-start | bytes 3145736 | tf_op jit(solution)/shard_map/ppermute | solution.py:515
  237.5 27.8 %collective-permute-start.28 = (f32[256,1024]{1,0:T(8,128)}, f32[256,1024]{1,0:T(8,128)}, u32[]{:S(2)}, u32[]{:S(2)}) collective-permute-start(f32[256,1024]{1,0:T(8,128)} %add.271), channel_id=1, source_target_pairs={{8,0},{12,4},{16,24},{20,28},{9,1},{13,5},{17,25},{21,29},{10,2},{... | collective-permute-start | bytes 3145736 | tf_op jit(solution)/shard_map/ppermute | solution.py:515
  238.8 27.9 %collective-permute-start.29 = (f32[256,1024]{1,0:T(8,128)}, f32[256,1024]{1,0:T(8,128)}, u32[]{:S(2)}, u32[]{:S(2)}) collective-permute-start(f32[256,1024]{1,0:T(8,128)} %add.272), channel_id=1, source_target_pairs={{8,16},{12,20},{16,8},{20,12},{9,17},{13,21},{17,9},{21,13},{10,18... | collective-permute-start | bytes 3145736 | tf_op jit(solution)/shard_map/ppermute | solution.py:515
  251.3 37.6 %collective-permute-start.33 = (f32[6912]{0:T(1024)S(1)}, f32[6912]{0:T(1024)S(1)}, u32[]{:S(2)}, u32[]{:S(2)}) collective-permute-start(f32[6912]{0:T(1024)S(1)} %fusion.23), channel_id=1, source_target_pairs={{0,8},{4,12},{24,16},{28,20},{1,9},{5,13},{25,17},{29,21},{2,10},{... | collective-permute-start | bytes 82952 | tf_op jit(solution)/shard_map/ppermute | solution.py:515
  270.9 27.9 %collective-permute-start.35 = (f32[256,1024]{1,0:T(8,128)S(1)}, f32[256,1024]{1,0:T(8,128)S(1)}, u32[]{:S(2)}, u32[]{:S(2)}) collective-permute-start(f32[256,1024]{1,0:T(8,128)S(1)} %add.278), channel_id=1, source_target_pairs={{8,0},{12,4},{16,24},{20,28},{9,1},{13,5},{17,25},{21,29},{10,2},{... | collective-permute-start | bytes 3145736 | tf_op jit(solution)/shard_map/ppermute | solution.py:515
  272.2 30.9 %collective-permute-start.36 = (f32[256,768]{1,0:T(8,128)S(1)}, f32[256,768]{1,0:T(8,128)S(1)}, u32[]{:S(2)}, u32[]{:S(2)}) collective-permute-start(f32[256,768]{1,0:T(8,128)S(1)} %add.279), channel_id=1, source_target_pairs={{8,16},{12,20},{16,8},{20,12},{9,17},{13,21},{17,9},{21,13},{10,18... | collective-permute-start | bytes 2359304 | tf_op jit(solution)/shard_map/ppermute | solution.py:515
  335.2 25.4 %collective-permute-start.49 = (f32[256,1024]{1,0:T(8,128)S(1)}, f32[256,1024]{1,0:T(8,128)S(1)}, u32[]{:S(2)}, u32[]{:S(2)}) collective-permute-start(f32[256,1024]{1,0:T(8,128)S(1)} %maximum_select_fusion.6), channel_id=1, source_target_pairs={{0,1},{1,0},{2,3},{3,2},{4,5},{5,4},{6,7},{7,6},{8,9},{9,8},{10,11... | collective-permute-start | bytes 3145736 | tf_op jit(solution)/shard_map/ppermute | solution.py:515
  335.8 25.1 %collective-permute-start.50 = (f32[256,1024]{1,0:T(8,128)S(1)}, f32[256,1024]{1,0:T(8,128)S(1)}, u32[]{:S(2)}, u32[]{:S(2)}) collective-permute-start(f32[256,1024]{1,0:T(8,128)S(1)} %maximum_select_fusion.7), channel_id=1, source_target_pairs={{0,2},{1,3},{2,0},{3,1},{4,6},{5,7},{6,4},{7,5},{8,10},{9,11},{10,... | collective-permute-start | bytes 3145736 | tf_op jit(solution)/shard_map/ppermute | solution.py:515
  (110 other events, 961.0 us)

commit v4 on v3

--- a/solution.py
+++ b/solution.py
@@ -204,7 +204,7 @@
         in_specs=[VMEM] * 2,
         out_specs=(VMEM,) * 5,
         scratch_shapes=[bias_held(min(256, seq_len))],
-        compiler_params=pltpu.CompilerParams(vmem_limit_bytes=24 * 2**20),
+        compiler_params=pltpu.CompilerParams(vmem_limit_bytes=56 * 2**20),
     )(angles, projected)
 
 
@@ -223,7 +223,7 @@
             cross,
             bias_held(min(256, seq_len)),
         ],
-        compiler_params=pltpu.CompilerParams(vmem_limit_bytes=24 * 2**20),
+        compiler_params=pltpu.CompilerParams(vmem_limit_bytes=56 * 2**20),
     )(angles, queries, keys, values, sums, attended, d_attended)
 
 
@@ -242,7 +242,7 @@
     return pl.BlockSpec(array.shape, lambda i, *order: (0,) * array.ndim)
 
 
-PARAMS = pltpu.CompilerParams(vmem_limit_bytes=40 * 2**20)
+PARAMS = pltpu.CompilerParams(vmem_limit_bytes=56 * 2**20)
 
 
 def forward_kernel(
@@ -436,36 +436,35 @@
 
 
 def gradient_kernel(wide, tiles, first_mat, *refs):
-    parts, (away, keep) = refs[:-2], refs[-2:]
+    parts, outs = refs[:-2], refs[-2:]
     for number, part in enumerate(parts):
         block = inner_rows(first_mat[...], part[:, :wide])
         columns = slice(number * wide, (number + 1) * wide)
-
-        @pl.when(pl.program_id(0) < pl.num_programs(0) // 2)
-        def _(block=block, columns=columns):
-            away[:, columns] = block
-
-        @pl.when(pl.program_id(0) >= pl.num_programs(0) // 2)
-        def _(block=block, columns=columns):
-            keep[:, columns] = block
-
-
-def gradient(core, first_mat, parts, wide):
-    count, rows = first_mat.shape
+        for side, out in enumerate(outs):
+
+            @pl.when(pl.program_id(0) // (pl.num_programs(0) // 2) == side)
+            def _(out=out, block=block, columns=columns):
+                out[:, columns] = block
+
+
+def gradient(swapped, first_mat, parts, wide, begin=0, rows=None):
+    count = first_mat.shape[0]
+    rows = rows or first_mat.shape[1]
     steps = 4 if rows >= 1024 else 2
     tile = rows // steps
+    half = steps // 2
+    columns = wide * len(parts)
     if tile % 128:
         full = inner_rows(
-            first_mat, jnp.concatenate([part[:, :wide] for part in parts], axis=1)
+            first_mat[:, begin : begin + rows],
+            jnp.concatenate([part[:, :wide] for part in parts], axis=1),
         )
         return tuple(
             lax.dynamic_slice_in_dim(full, side * (rows // 2), rows // 2, 0)
-            for side in (1 - core, core)
+            for side in (swapped, 1 - swapped)
         )
-    half = steps // 2
-    tiles = (jnp.arange(steps, dtype=jnp.int32) + (1 - core) * half) % steps
-    out = jax.ShapeDtypeStruct((rows // 2, wide * len(parts)), jnp.float32)
-    columns = wide * len(parts)
+    tiles = (jnp.arange(steps, dtype=jnp.int32) + swapped * half) % steps + begin // tile
+    out = jax.ShapeDtypeStruct((rows // 2, columns), jnp.float32)
     return pl.pallas_call(
         functools.partial(gradient_kernel, wide),
         grid_spec=pltpu.PrefetchScalarGridSpec(
@@ -483,6 +482,199 @@
     )(tiles, first_mat, *parts)
 
 
+def float_shape(rows, width):
+    return jax.ShapeDtypeStruct((rows, width), jnp.float32)
+
+
+def steps_for(rows):
+    return 2 if rows % 16 == 0 else 1
+
+
+def scalars(*values):
+    return jnp.stack([jnp.asarray(value, jnp.int32) for value in values])
+
+
+def add_kernel(first, second, out):
+    out[...] = first[...] + second[...]
+
+
+def add(first, second):
+    rows, width = first.shape
+    steps = steps_for(rows)
+    spec = tiled(width, rows // steps)
+    return pl.pallas_call(
+        add_kernel,
+        grid=(steps,),
+        in_specs=[spec] * 2,
+        out_specs=spec,
+        out_shape=float_shape(rows, width),
+        compiler_params=PARAMS,
+    )(first, second)
+
+
+def choose_kernel(flag, first, second, out):
+    @pl.when(flag[0] == 1)
+    def _():
+        out[...] = first[...]
+
+    @pl.when(flag[0] == 0)
+    def _():
+        out[...] = second[...]
+
+
+def choose(flag, first, second):
+    rows, width = first.shape
+    steps = steps_for(rows)
+    spec = tiled(width, rows // steps)
+    return pl.pallas_call(
+        choose_kernel,
+        grid_spec=pltpu.PrefetchScalarGridSpec(
+            num_scalar_prefetch=1, grid=(steps,), in_specs=[spec] * 2, out_specs=spec
+        ),
+        out_shape=float_shape(rows, width),
+        compiler_params=PARAMS,
+    )(scalars(flag), first, second)
+
+
+def add_parts_kernel(first, second, *outs):
+    total = first[...] + second[...]
+    for number, out in enumerate(outs):
+
+        @pl.when(pl.program_id(0) == number)
+        def _(out=out):
+            out[...] = total
+
+
+def add_parts(first, second, parts):
+    rows, width = first.shape
+    outs = (float_shape(rows // parts, width),) * parts
+    spec = tiled(width, rows // parts)
+    return pl.pallas_call(
+        add_parts_kernel,
+        grid=(parts,),
+        in_specs=[spec] * 2,
+        out_specs=tuple(whole(out) for out in outs),
+        out_shape=outs,
+        compiler_params=PARAMS,
+    )(first, second)
+
+
+def add_split_kernel(mine, first, second, away, keep):
+    total = first[...] + second[...]
+
+    @pl.when(pl.program_id(0) == 0)
+    def _():
+        away[...] = total
+
+    @pl.when(pl.program_id(0) == 1)
+    def _():
+        keep[...] = total
+
+
+def add_split(mine, first, second):
+    rows, width = first.shape
+    outs = (float_shape(rows // 2, width),) * 2
+    spec = tiled(width, rows // 2, lambda i, mine: (i + 1 + mine[0]) % 2)
+    return pl.pallas_call(
+        add_split_kernel,
+        grid_spec=pltpu.PrefetchScalarGridSpec(
+            num_scalar_prefetch=1,
+            grid=(2,),
+            in_specs=[spec] * 2,
+            out_specs=tuple(whole(out) for out in outs),
+        ),
+        out_shape=outs,
+        compiler_params=PARAMS,
+    )(scalars(mine), first, second)
+
+
+def norm_back_kernel(at, first, second, tokens, cotangent, out):
+    rows = first[...] + second[...]
+    normed, scale_inv = normed_rows(tokens[...])
+    out[...] = cotangent[...].astype(jnp.float32) + scale_inv * (
+        rows
+        - jnp.mean(rows, axis=-1, keepdims=True)
+        - normed * jnp.mean(rows * normed, axis=-1, keepdims=True)
+    )
+
+
+def norm_back(first, second, at, tokens, cotangent):
+    rows, width = first.shape
+    spec = pl.BlockSpec((rows, width), lambda i, at: (0, 0))
+    moved = pl.BlockSpec((rows, width), lambda i, at: (at[0], 0))
+    return pl.pallas_call(
+        norm_back_kernel,
+        grid_spec=pltpu.PrefetchScalarGridSpec(
+            num_scalar_prefetch=1,
+            grid=(1,),
+            in_specs=[spec, spec, moved, moved],
+            out_specs=spec,
+        ),
+        out_shape=float_shape(rows, width),
+        compiler_params=PARAMS,
+    )(scalars(at // rows), first, second, tokens, cotangent)
+
+
+def join_kernel(mine, own, other, out):
+    @pl.when(pl.program_id(0) == mine[0])
+    def _():
+        out[...] = own[...]
+
+    @pl.when(pl.program_id(0) != mine[0])
+    def _():
+        out[...] = other[...]
+
+
+def join(mine, own, other):
+    rows, width = own.shape
+    return pl.pallas_call(
+        join_kernel,
+        grid_spec=pltpu.PrefetchScalarGridSpec(
+            num_scalar_prefetch=1,
+            grid=(2,),
+            in_specs=[pl.BlockSpec((rows, width), lambda i, mine: (0, 0))] * 2,
+            out_specs=tiled(width, rows, lambda i, mine: i),
+        ),
+        out_shape=float_shape(2 * rows, width),
+        compiler_params=PARAMS,
+    )(scalars(mine), own, other)
+
+
+def collect_kernel(order, *refs):
+    parts, out = refs[:4], refs[-1]
+    extra = refs[4:-1]
+    for number, part in enumerate(parts):
+
+        @pl.when(order[pl.program_id(0)] == number)
+        def _(part=part):
+            if extra:
+                tokens, bias = extra
+                total = tokens[...].astype(jnp.float32) + part[...] + bias[...]
+                out[...] = total.astype(out.dtype)
+            else:
+                out[...] = part[...]
+
+
+def collect(order, parts, *extra):
+    rows, width = parts[0].shape
+    specs = [pl.BlockSpec((rows, width), lambda i, order: (0, 0))] * 4
+    if extra:
+        specs = specs + [tiled(width, rows, lambda i, order: i), whole(extra[1])]
+    return pl.pallas_call(
+        collect_kernel,
+        grid_spec=pltpu.PrefetchScalarGridSpec(
+            num_scalar_prefetch=1,
+            grid=(4,),
+            in_specs=specs,
+            out_specs=tiled(width, rows, lambda i, order: i),
+        ),
+        out_shape=jax.ShapeDtypeStruct(
+            (4 * rows, width), extra[0].dtype if extra else jnp.float32
+        ),
+        compiler_params=PARAMS,
+    )(order, *parts, *extra)
+
+
 class Order:
     def __init__(self, token):
         self.token = token
@@ -495,6 +687,7 @@
     def run(self, step, *arrays):
         tied = lax.optimization_barrier((self.token, *arrays))
         out = step(*tied[1:])
+        out = tuple(out) if isinstance(out, list) else out
         if isinstance(out, tuple):
             return self.tie(*out)
         return self.tie(out)
@@ -529,40 +722,31 @@
     return [(i, i ^ bit) for i in range(size)]
 
 
-def tensor_steps(away, keep, size, order, between):
+def tensor_steps(away, keep, size, order, finish):
     place = lax.axis_index("tensor")
     first = 0
     rows = away.shape[0]
     for number, bit in enumerate(order):
-        mine = (place // bit) % 2
-        if number:
+        got = yield away, "tensor", swap_pairs(size, bit)
+        first = first + (place // bit) % 2 * rows
+        if number + 1 < len(order):
+            away, keep = add_split((place // order[number + 1]) % 2, keep, got)
             rows = rows // 2
-            away = lax.dynamic_slice_in_dim(array, (1 - mine) * rows, rows, 0)
-            keep = lax.dynamic_slice_in_dim(array, mine * rows, rows, 0)
-        array = keep + (yield away, "tensor", swap_pairs(size, bit))
-        first = first + mine * rows
-    array = between(array, first)
-    for bit in reversed(order):
+    array = finish(keep, got, first)
+    for number, bit in enumerate(reversed(order)):
         got = yield array, "tensor", swap_pairs(size, bit)
-        mine = (place // bit) % 2
-        array = jnp.where(
-            mine == 0,
-            jnp.concatenate([array, got], axis=0),
-            jnp.concatenate([got, array], axis=0),
-        )
-    return array
+        if number + 1 < len(order):
+            array = join((place // bit) % 2, array, got)
+    return array, got
 
 
 def core_steps(parts, size, chunks):
     away, keep = parts
     got = yield away, "dp", swap_pairs(size, 1)
-    rows = keep.shape[0] // chunks
-    return [
-        keep[c * rows : (c + 1) * rows] + got[c * rows : (c + 1) * rows] for c in range(chunks)
-    ]
-
-
-def line_steps(array, size, back=True):
+    return add_parts(keep, got, chunks)
+
+
+def line_steps(array, size):
     chips = size // 2
     place = lax.axis_index("dp") // 2
 
@@ -573,26 +757,22 @@
         steps = range(chips // 2 - 1)
         for s in steps:
             got = yield array, "dp", pairs([(s, s + 1), (chips - 1 - s, chips - 2 - s)])
-            array = array + got
+            array = add(array, got)
         middle = chips // 2
         got = yield array, "dp", pairs([(middle - 1, middle), (middle, middle - 1)])
-        array = array + got
+        array = add(array, got)
         for s in reversed(steps):
             got = yield array, "dp", pairs([(s + 1, s), (chips - 2 - s, chips - 1 - s)])
-            array = jnp.where((place == s) | (place == chips - 1 - s), got, array)
-    if not back:
-        return array
+            array = choose((place == s) | (place == chips - 1 - s), got, array)
     got = yield array, "dp", swap_pairs(size, 1)
     return array, got
 
 
-def small_steps(stats, rest, tensor_size, dp_size):
-    for bit in (1 << k for k in range(tensor_size.bit_length() - 1)):
-        got = yield stats, "tensor", swap_pairs(tensor_size, bit)
+def small_steps(stats, size):
+    for bit in (1 << k for k in range(size.bit_length() - 1)):
+        got = yield stats, "tensor", swap_pairs(size, bit)
         stats = stats + got
-    vectors = jnp.concatenate([stats.reshape(-1), *rest])
-    got = yield vectors, "dp", swap_pairs(dp_size, 1)
-    return (yield from line_steps(vectors + got, dp_size, back=False))
+    return stats
 
 
 def assemble(core, parts):
@@ -641,9 +821,9 @@
     def lines(core_chain):
         return [line_steps(part, dp_size) for part in core_chain.end()]
 
-    def grads(chunks, first_mat, *parts, wide=None):
+    def grads(chunks, first_mat, *parts, wide=None, begin=0, rows=None):
         def step(first_mat, *parts):
-            return gradient(core, first_mat, parts, wide or parts[0].shape[1])
+            return gradient(1 - core, first_mat, parts, wide or parts[0].shape[1], begin, rows)
 
         return chain(core_steps(run(step, first_mat, *parts), dp_size, chunks))
 
@@ -658,31 +838,45 @@
         w_up,
         b_up[None, :],
     )
-    core_down = grads(2, hidden, cotangent)
+    inner = hidden.shape[1]
+    core_down = grads(1, hidden, cotangent, begin=inner // 2, rows=inner // 2)
+    top = run(
+        lambda h, dy: gradient(0, h, [dy], width, 0, inner // 2), hidden, cotangent
+    )
+    top = lax.psum(top, "dp")
+    angles = run(turn_angles, segment[0])
+    down = chain(lines(core_down)[0])
     d_pre, scaled_mlp, sums_mlp, up_bias = run(
         feed_back, tokens, cotangent, slope, w_down, w_up, mlp_gain[None, :]
     )
-    down = lines(core_down)
-    down[0] = chain(down[0])
     core_up = grads(2, mlp_low, d_pre)
-    angles = run(turn_angles, segment[0])
     kept = run(functools.partial(attend, heads=heads), angles, projected)
     attended = kept[0]
+    up = lines(core_up)
+    down.on()
+    up[0] = chain(up[0])
     partial = run(branches, tiles, attended, hidden, w_out, w_down)
     result = [
-        chain(tensor_steps(partial[p], partial[2 + p], tensor_size, orders[p], lambda rows, first: rows))
+        chain(
+            tensor_steps(
+                partial[p],
+                partial[2 + p],
+                tensor_size,
+                orders[p],
+                lambda keep, got, first: add(keep, got),
+            )
+        )
         for p in range(2)
     ]
-    up = lines(core_up)
-    down[0].on()
-    down[1] = chain(down[1])
-
     back = []
     for begin in range(0, heads, group):
         def step(angles, d_attended, *kept, begin=begin):
             return attend_back(angles, kept, d_attended, begin, group, lanes)
 
         back.append(run(step, angles, d_attended, *kept))
+    down.on()
+    up[0].on()
+    up[1] = chain(up[1])
     *scaled, sums_attn, qkv_bias, branch_sum = run(
         lambda tiles, *a: input_back(tiles, a[:-5], wide, *a[-5:]),
         tiles,
@@ -693,96 +887,83 @@
         w_qkv,
         attn_gain[None, :],
     )
+    top = order.tie(*top)
     for part in result:
         part.on()
+    small = chain(small_steps(jnp.concatenate([sums_attn, sums_mlp], axis=0), tensor_size))
     core_qkv = grads(2, attn_low, *back, wide=wide)
-    down[0].on()
-    down[1].on()
-    up[0] = chain(up[0])
-    core_out = grads(1, attended, cotangent)
+    small.on()
+    grad_out = run(inner_rows, attended, cotangent)
     qkv = lines(core_qkv)
+    stats = small.end()
     for part in result:
         part.on()
+    for part in (down, up[0], up[1]):
+        part.on()
+    qkv[0] = chain(qkv[0])
+
+    sizes = (width,) * 4 + (w_qkv.shape[1], w_up.shape[1], width)
+    ends = [sum(sizes[: k + 1]) for k in range(len(sizes))]
+    flat = jnp.concatenate([stats.reshape(-1), qkv_bias[0], up_bias[0], branch_sum[0]])
+    spare = -(-flat.shape[0] // width // 16) * 16
+    flat = jnp.pad(flat, (0, spare * width - flat.shape[0])).reshape(spare, width)
+
+    def pack(grad_out, flat):
+        packed = jnp.concatenate([grad_out, flat], axis=0)
+        rows = packed.shape[0] // 2
+        return tuple(
+            lax.dynamic_slice_in_dim(packed, side * rows, rows, 0) for side in (1 - core, core)
+        )
+
+    core_out = chain(core_steps(run(pack, grad_out, flat), dp_size, 1))
+
+    def back_end(part):
+        def finish(keep, got, first):
+            return norm_back(keep, got, first + part * split, tokens, cotangent)
+
+        return finish
+
     out = lines(core_out)[0]
-
-    def norm_back(part):
-        def between(rows, first):
-            at = first + part * split
-
-            def here(whole):
-                return lax.dynamic_slice_in_dim(whole, at, rows.shape[0], 0)
-
-            normed, scale_inv = normed_rows(here(tokens))
-            return here(cotangent).astype(jnp.float32) + scale_inv * (
-                rows
-                - jnp.mean(rows, axis=-1, keepdims=True)
-                - normed * jnp.mean(rows * normed, axis=-1, keepdims=True)
-            )
-
-        return between
-
     for part in result:
         part.on()
-    for part in (down[0], down[1], up[0]):
-        part.on()
-    up[1] = chain(up[1])
-    small = chain(
-        small_steps(
-            jnp.concatenate([sums_attn, sums_mlp], axis=0),
-            [v[0] for v in (qkv_bias, up_bias, branch_sum)],
-            tensor_size,
-            dp_size,
-        )
-    )
-    down[0].end()
-    small.on()
-
-    def finish(tokens, *parts):
-        summed = jnp.concatenate(parts, axis=0)
-        return (tokens.astype(jnp.float32) + summed + b_branch).astype(jnp.bfloat16)
-
-    ended = [part.end() for part in result]
+    down.end()
     d_tokens = [
-        chain(tensor_steps(scaled[p], scaled[2 + p], tensor_size, orders[p], norm_back(p)))
+        chain(tensor_steps(scaled[p], scaled[2 + p], tensor_size, orders[p], back_end(p)))
         for p in range(2)
     ]
-    result = run(finish, tokens, *ended)
-    for part in (down[1], up[0], up[1]):
-        part.on()
-    qkv[0] = chain(qkv[0])
-    small.on()
-    small.on()
-    for part in d_tokens:
-        part.on()
-    down[1].end()
-    grad_down = run(lambda *p: assemble(p[0], (p[1:3], p[3:5])), core, *down[0].end(), *down[1].end())
     for part in (up[0], up[1], qkv[0]):
         part.on()
     qkv[1] = chain(qkv[1])
+    grad_down = run(collect, scalars(0, 1, 2 + core, 3 - core), [*top, *down.end()])
+    spots = scalars(mine[0], 1 - mine[0], 2 + mine[1], 3 - mine[1])
+    up[0].end()
+    ended = [part.end() for part in result]
     for part in d_tokens:
         part.on()
-    small.on()
-    up[0].end()
+    result = run(collect, spots, [*ended[0], *ended[1]], tokens, b_branch[None, :])
     for part in (up[1], qkv[0], qkv[1]):
         part.on()
     out = chain(out)
+    up[1].end()
     for part in d_tokens:
         part.on()
-    up[1].end()
-    grad_up = run(lambda *p: assemble(p[0], (p[1:3], p[3:5])), core, *up[0].end(), *up[1].end())
-    for part in (out, qkv[0], qkv[1]):
+    core_spots = jnp.where(core == 0, scalars(0, 2, 1, 3), scalars(1, 3, 0, 2))
+    grad_up = run(collect, core_spots, [*up[0].end(), *up[1].end()])
+    for part in (qkv[0], qkv[1], out):
         part.on()
-    vectors = small.end()
+    for part in d_tokens:
+        part.on()
     qkv[0].end()
-    for part in (out, qkv[1]):
+    for part in (qkv[1], out):
         part.on()
-    d_tokens = run(lambda *p: jnp.concatenate(p, axis=0), *(part.end() for part in d_tokens))
     qkv[1].end()
-    grad_qkv = run(lambda *p: assemble(p[0], (p[1:3], p[3:5])), core, *qkv[0].end(), *qkv[1].end())
-    grad_out = assemble(order.token, (out.end(),))
-
-    sizes = (width,) * 4 + (w_qkv.shape[1], w_up.shape[1], width)
-    ends = [sum(sizes[: k + 1]) for k in range(len(sizes))]
+    grad_qkv = run(collect, core_spots, [*qkv[0].end(), *qkv[1].end()])
+    ended = [part.end() for part in d_tokens]
+    out.on()
+    d_tokens = run(collect, spots, [*ended[0], *ended[1]])
+    packed = order.tie(assemble(core, (out.end(),)))
+    grad_out = packed[: w_out.shape[0]]
+    vectors = packed[w_out.shape[0] :].reshape(-1)
     a_gain, a_shift, m_gain, m_shift, qkv_bias, up_bias, branch = (
         vectors[end - size : end] for end, size in zip(ends, sizes, strict=True)
     )

time: 396 us -> 428 us (1.081)
  Pallas kernels: 75.3 us -> 213 us
  other arithmetic: 88.5 us -> 6.46 us
  waiting for transfers between devices: 122 us -> 91.7 us
  between operations: 2.43 us -> 14.8 us
  local copies, waits for them, and re-layouts: 31.9 us -> 22.1 us
    pallas_call x0 -> x39, Pallas kernels: none -> 107 us  [the longest x14 31 us: add(): pl.pallas_call(add_kernel, grid=(steps,), in_specs=[spec] * 2, out_specs=...]
    add x29 -> x0, other arithmetic: 42.1 us -> none  [the longest x16 25 us: line_steps(): array = array + got]
    ppermute x54 -> x46, waiting for transfers between devices: 122 us -> 91.7 us  [_go(): self.held = lax.ppermute(array, axis, pairs)]
    select_n x18 -> x3, other arithmetic: 18.1 us -> 1.55 us  [the longest x2 1.04 us: gradient(): (jnp.arange(steps, dtype=jnp.int32) + swapped * half) % steps]
    unnamed x161 -> x106, local copies, waits for them, and re-layouts: 26.6 us -> 16.9 us
    pallas_call x4, Pallas kernels: 17.4 us -> 26.7 us  [gradient(): pl.pallas_call(functools.partial(gradient_kernel, wide), grid_spec=pltpu....]
    select_n x7 -> x1, other arithmetic: 9.22 us -> 0.08 us  [assemble(): low = [jnp.where(core == 0, mine, other) for mine, other in parts]]
    concatenate x4 -> x1, other arithmetic: 8.16 us -> 0.11 us  [assemble(): return jnp.concatenate(low + high, axis=0)]
  transfers between devices with their start and end apart: 54 -> 47, of which waited for: 16 -> 17; matrix products, arithmetic and copies ran while one was open for 22% -> 2% of each run, Pallas kernels for 13% -> 37%
where the time goes in v4:
time: 428 us; the launch traced here: 420 us
  Pallas kernels  213 us (50%)
  waiting for transfers between devices  91.7 us (21%)
  starting transfers between devices  70.6 us (16%)
  local copies, waits for them, and re-layouts  22.1 us (5%)
  between operations  14.8 us (3%)
  other arithmetic  6.46 us (2%)
    ppermute x46, waiting for transfers between devices, _go(): self.held = lax.ppermute(array, axis, pairs)  91.7 us
    ppermute x46, starting transfers between devices, _go(): self.held = lax.ppermute(array, axis, pairs)  70.5 us
    pallas_call x14, Pallas kernels, add(): pl.pallas_call(add_kernel, grid=(steps,), in_specs=[spec] * 2, out_specs=...  31 us
    pallas_call x4, Pallas kernels, gradient(): pl.pallas_call(functools.partial(gradient_kernel, wide), grid_spec=pltpu....  26.7 us
    pallas_call x5, Pallas kernels, collect(): pl.pallas_call(collect_kernel, grid_spec=pltpu.PrefetchScalarGridSpec(num...  26.7 us
    pallas_call x2, Pallas kernels, attend_back(): pl.pallas_call(functools.partial(attend_back_kernel, begin, heads), out_s...  21.1 us
    unnamed x106, local copies, waits for them, and re-layouts  16.9 us
    pallas_call x1, Pallas kernels, attend(): pl.pallas_call(functools.partial(attend_kernel, heads), out_shape=(shape(...  16.4 us
  transfers between devices with their start and end apart: 47, of which 17 were waited for; matrix products, arithmetic and copies ran while one was open for 2% of the time, Pallas kernels for 37%

profile of v4, /device:TPU:0, one launch (start us, length us, event | category | flops | bytes accessed | tf_op | source)
XLA Modules:
  0.0 420.1 jit_solution(3231137575959544801)
XLA Ops:
  8.5 11.5 %shard_map.237 = (bf16[1024,1024]{1,0:T(8,128)(2,1)}, bf16[1024,1024]{1,0:T(8,128)(2,1)}, f32[1024,768]{1,0:T(8,128)}, bf16[1024,256]{1,0:T(8,128)(2,1)}, bf16[1...) custom-call(bf16[1024,1024]{1,0:T(8,128)(2,1)} %tokens.5, bf16[1024,1024]{1,0:T(8,128)(2,1)} %cotangent.5, f32[1,1024]{1,0:T(1,128)} %bitcast.38, ...), custom_call_target="tpu_custom_call" | custom-call | tf_op jit(solution)/shard_map/pallas_call | solution.py:296
  20.6 5.4 %shard_map.238 = (f32[256,1024]{1,0:T(8,128)}, f32[256,1024]{1,0:T(8,128)}) custom-call(s32[2]{0:T(128)} %get-tuple-element.787.tiles, bf16[1024,1024]{1,0:T(8,128)(2,1)} %get-tuple-element.468.first_mat.hidden, bf16[1024,1024]{1,0:T(8,128)(2,1)} %cotangent.5), custom_call_target="tpu_custom_call" | custom-call | tf_op jit(solution)/shard_map/pallas_call | solution.py:468
  26.4 5.6 %shard_map.239 = (f32[256,1024]{1,0:T(8,128)}, f32[256,1024]{1,0:T(8,128)}) custom-call(s32[2]{0:T(128)} %get-tuple-element.786.tiles, bf16[1024,1024]{1,0:T(8,128)(2,1)} %get-tuple-element.468.first_mat.hidden, bf16[1024,1024]{1,0:T(8,128)(2,1)} %cotangent.5), custom_call_target="tpu_custom_call" | custom-call | tf_op jit(solution)/shard_map/pallas_call | solution.py:468
  39.7 10.6 %shard_map.241 = (bf16[1024,1024]{1,0:T(8,128)(2,1)}, f32[1024,1024]{1,0:T(8,128)}, f32[2,1024]{1,0:T(2,128)}, f32[1,1024]{1,0:T(1,128)}) custom-call(bf16[1024,1024]{1,0:T(8,128)(2,1)} %tokens.5, bf16[1024,1024]{1,0:T(8,128)(2,1)} %cotangent.5, f32[1024,1024]{1,0:T(8,128)} %get-tuple-element.427.slope, bf16[1024,1024]{1,0:T(8,128)(2,1)} %w_down.1, ...), custom_call_target="tpu_custom_call" | custom-call | tf_op jit(solution)/shard_map/pallas_call | solution.py:336
  50.3 7.8 %shard_map.242 = (f32[512,1024]{1,0:T(8,128)}, f32[512,1024]{1,0:T(8,128)}) custom-call(s32[4]{0:T(128)} %and_select_fusion.tiles, bf16[1024,1024]{1,0:T(8,128)(2,1)} %get-tuple-element.438.first_mat, bf16[1024,1024]{1,0:T(8,128)(2,1)} %get-tuple-element.439.refs_0_), custom_call_target="tpu_custom_call" | custom-call | tf_op jit(solution)/shard_map/pallas_call | solution.py:468
  58.2 6.0 %collective-permute-start.2 = (f32[256,1024]{1,0:T(8,128)S(1)}, f32[256,1024]{1,0:T(8,128)}, u32[]{:S(2)}, u32[]{:S(2)}) collective-permute-start(f32[256,1024]{1,0:T(8,128)S(1)} %copy-done.2), channel_id=1, source_target_pairs={{0,8},{4,12},{24,16},{28,20},{1,9},{5,13},{25,17},{29,21},{2,10},{... | collective-permute-start | bytes 3145736 | tf_op jit(solution)/shard_map/ppermute | solution.py:708
  64.3 16.4 %shard_map.243 = (bf16[1024,256]{1,0:T(8,128)(2,1)}, f32[1024,128]{1,0:T(8,128)}, bf16[4,1024,64]{2,1,0:T(8,128)(2,1)}, bf16[4,1024,64]{2,1,0:T(8,128)(2,1)}, bf16[4,1024,64]{2,1,0:T(8,128)(2,1)}) custom-call(f32[24,1024]{1,0:T(8,128)} %pad_maximum_fusion.1.angles, f32[1024,768]{1,0:T(8,128)} %get-tuple-element.448.projected), custom_call_target="tpu_custom_call" | custom-call | tf_op jit(solution)/shard_map/pallas_call | solution.py:197
  80.7 21.7 %collective-permute-done.2.second = f32[256,1024]{1,0:T(8,128)} collective-permute-done((f32[256,1024]{1,0:T(8,128)S(1)}, f32[256,1024]{1,0:T(8,128)}, u32[]{:S(2)}, u32[]{:S(2)}) %collective-permute-start.2) | collective-permute-done | bytes 1048608 | tf_op jit(solution)/shard_map/ppermute | solution.py:708
  109.4 6.3 %collective-permute-start.4 = (f32[256,1024]{1,0:T(8,128)}, f32[256,1024]{1,0:T(8,128)S(1)}, u32[]{:S(2)}, u32[]{:S(2)}) collective-permute-start(f32[256,1024]{1,0:T(8,128)} %get-tuple-element.505.first), channel_id=1, source_target_pairs={{0,8},{4,12},{24,16},{28,20},{1,9},{5,13},{25,17},{29,21},{2,10},{... | collective-permute-start | bytes 3145736 | tf_op jit(solution)/shard_map/ppermute | solution.py:708
  116.2 9.0 %shard_map.246 = (f32[256,1024]{1,0:T(8,128)}, f32[256,1024]{1,0:T(8,128)}, f32[256,1024]{1,0:T(8,128)}, f32[256,1024]{1,0:T(8,128)}) custom-call(s32[4]{0:T(128)} %get-tuple-element.514.tiles, bf16[1024,256]{1,0:T(8,128)(2,1)} %get-tuple-element.561.attended, bf16[1024,1024]{1,0:T(8,128)(2,1)} %get-tuple-element.468.first_mat.hidden, ...), custom_call_target="tpu_custom_call" | custom-call | tf_op jit(solution)/shard_map/pallas_call | solution.py:367
  128.4 10.5 %shard_map.247.refs_0_ = bf16[1024,384]{1,0:T(8,128)(2,1)} custom-call(f32[24,1024]{1,0:T(8,128)} %pad_maximum_fusion.1.angles, bf16[4,1024,64]{2,1,0:T(8,128)(2,1)} %get-tuple-element.494.q_s, bf16[4,1024,64]{2,1,0:T(8,128)(2,1)} %get-tuple-element.495.k_s, bf16[4,1024,64]{2,1,0:T(8,128)(2,1)} %get-tuple-element.496.v_s, ...), custom_call_target="tpu_custom_call" | custom-call | tf_op jit(solution)/shard_map/pallas_call | solution.py:215
  138.9 10.6 %shard_map.248.refs_1_ = bf16[1024,384]{1,0:T(8,128)(2,1)} custom-call(f32[24,1024]{1,0:T(8,128)} %pad_maximum_fusion.1.angles, bf16[4,1024,64]{2,1,0:T(8,128)(2,1)} %get-tuple-element.494.q_s, bf16[4,1024,64]{2,1,0:T(8,128)(2,1)} %get-tuple-element.495.k_s, bf16[4,1024,64]{2,1,0:T(8,128)(2,1)} %get-tuple-element.496.v_s, ...), custom_call_target="tpu_custom_call" | custom-call | tf_op jit(solution)/shard_map/pallas_call | solution.py:215
  158.7 10.0 %shard_map.251 = (f32[256,1024]{1,0:T(8,128)}, f32[256,1024]{1,0:T(8,128)}, f32[256,1024]{1,0:T(8,128)}, f32[256,1024]{1,0:T(8,128)}, f32[2,1024]{1,0:T(2,128)}, /*index=5*/f32[1,768]{1,0:T(1,128)}, f32[1,1024]{1,0:T(1,128)}) custom-call(s32[4]{0:T(128)} %get-tuple-element.514.tiles, bf16[1024,384]{1,0:T(8,128)(2,1)} %shard_map.247.refs_0_, ...), custom_call_target="tpu_custom_call" | custom-call | tf_op jit(solution)/shard_map/pallas_call | solution.py:423
  176.0 7.9 %shard_map.254 = (f32[512,768]{1,0:T(8,128)}, f32[512,768]{1,0:T(8,128)}) custom-call(s32[4]{0:T(128)} %and_select_fusion.tiles, bf16[1024,1024]{1,0:T(8,128)(2,1)} %get-tuple-element.549.first_mat, bf16[1024,384]{1,0:T(8,128)(2,1)} %shard_map.247.refs_0_, bf16[1024,384]{1,0:T(8,128)(2,1)} %shard_map.248.refs_1_), custom_call_target="tpu_custom_call" | custom-call | tf_op jit(solution)/shard_map/pallas_call | solution.py:468
  187.0 8.3 %collective-permute-start.14 = (f32[256,1024]{1,0:T(8,128)}, f32[256,1024]{1,0:T(8,128)}, u32[]{:S(2)}, u32[]{:S(2)}) collective-permute-start(f32[256,1024]{1,0:T(8,128)} %get-tuple-element.586.first), channel_id=1, source_target_pairs={{0,8},{4,12},{24,16},{28,20},{1,9},{5,13},{25,17},{29,21},{2,10},{... | collective-permute-start | bytes 3145736 | tf_op jit(solution)/shard_map/ppermute | solution.py:708
  207.5 7.6 %collective-permute-done.10.second = f32[128,1024]{1,0:T(8,128)S(1)} collective-permute-done((f32[128,1024]{1,0:T(8,128)}, f32[128,1024]{1,0:T(8,128)S(1)}, u32[]{:S(2)}, u32[]{:S(2)}) %collective-permute-start.10) | collective-permute-done | bytes 524320 | tf_op jit(solution)/shard_map/ppermute | solution.py:708
  236.7 9.1 %collective-permute-done.16.other = f32[128,1024]{1,0:T(8,128)} collective-permute-done((f32[128,1024]{1,0:T(8,128)S(1)}, f32[128,1024]{1,0:T(8,128)}, u32[]{:S(2)}, u32[]{:S(2)}) %collective-permute-start.16) | collective-permute-done | bytes 524320 | tf_op jit(solution)/shard_map/ppermute | solution.py:708
  263.6 5.8 %collective-permute-done.21.second = f32[256,768]{1,0:T(8,128)} collective-permute-done((f32[256,768]{1,0:T(8,128)}, f32[256,768]{1,0:T(8,128)}, u32[]{:S(2)}, u32[]{:S(2)}) %collective-permute-start.21) | collective-permute-done | bytes 786464 | tf_op jit(solution)/shard_map/ppermute | solution.py:708
  277.8 5.6 %collective-permute-done.24.refs_3_ = f32[256,1024]{1,0:T(8,128)S(1)} collective-permute-done((f32[256,1024]{1,0:T(8,128)}, f32[256,1024]{1,0:T(8,128)S(1)}, u32[]{:S(2)}, u32[]{:S(2)}) %collective-permute-start.24) | collective-permute-done | bytes 1048608 | tf_op jit(solution)/shard_map/ppermute | solution.py:708
  306.3 6.0 %shard_map.269 = bf16[1024,1024]{1,0:T(8,128)(2,1)} custom-call(s32[4]{0:T(128)} %get-tuple-element.757.order, f32[256,1024]{1,0:T(8,128)} %shard_map.261.refs_0_, f32[256,1024]{1,0:T(8,128)} %collective-permute-done.23.refs_1_, f32[256,1024]{1,0:T(8,128)} %shard_map.262.refs_2_, f32[256,1024]{1,0:T(8,128)} %copy-done.30, bf16[1024,1024]{1,0:T(8,128)(2,1)} %tokens.5, ...), custom_call_target="tpu_custom_call" | custom-call | tf_op jit(solution)/shard_map/pallas_call | solution.py:663
  326.1 6.3 %collective-permute-start.35 = (f32[136,1024]{1,0:T(8,128)}, f32[136,1024]{1,0:T(8,128)S(1)}, u32[]{:S(2)}, u32[]{:S(2)}) collective-permute-start(f32[136,1024]{1,0:T(8,128)} %shard_map.273.first), channel_id=1, source_target_pairs={{0,8},{4,12},{24,16},{28,20},{1,9},{5,13},{25,17},{29,21},{2,10},{... | collective-permute-start | bytes 1671176 | tf_op jit(solution)/shard_map/ppermute | solution.py:708
  360.2 8.8 %collective-permute-done.36.other = f32[128,1024]{1,0:T(8,128)S(1)} collective-permute-done((f32[128,1024]{1,0:T(8,128)S(1)}, f32[128,1024]{1,0:T(8,128)S(1)}, u32[]{:S(2)}, u32[]{:S(2)}) %collective-permute-start.36) | collective-permute-done | bytes 524320 | tf_op jit(solution)/shard_map/ppermute | solution.py:708
  389.8 10.0 %collective-permute-done.42.refs_1_ = f32[256,1024]{1,0:T(8,128)S(1)} collective-permute-done((f32[256,1024]{1,0:T(8,128)S(1)}, f32[256,1024]{1,0:T(8,128)S(1)}, u32[]{:S(2)}, u32[]{:S(2)}) %collective-permute-start.42) | collective-permute-done | bytes 1048608 | tf_op jit(solution)/shard_map/ppermute | solution.py:708
  404.5 5.4 %shard_map.286 = f32[1024,1024]{1,0:T(8,128)} custom-call(s32[4]{0:T(128)} %get-tuple-element.757.order, f32[256,1024]{1,0:T(8,128)} %shard_map.280.refs_0_, f32[256,1024]{1,0:T(8,128)} %copy-done.19, f32[256,1024]{1,0:T(8,128)} %shard_map.281.refs_2_, f32[256,1024]{1,0:T(8,128)} %copy-done.20), custom_call_target="tpu_custom_call" | custom-call | tf_op jit(solution)/shard_map/pallas_call | solution.py:663
  (254 shorter events, 192.9 us)
Async XLA Ops:
  7.2 161.6 %all-reduce.4.cloned.1.call-start = ((), (), s32[]{:S(2)}) async-start(), calls=%async_computation | async-start | bytes 4194304 | tf_op jit(solution)/shard_map/psum | solution.py:846
  58.2 44.3 %collective-permute-start.2 = (f32[256,1024]{1,0:T(8,128)S(1)}, f32[256,1024]{1,0:T(8,128)}, u32[]{:S(2)}, u32[]{:S(2)}) collective-permute-start(f32[256,1024]{1,0:T(8,128)S(1)} %copy-done.2), channel_id=1, source_target_pairs={{0,8},{4,12},{24,16},{28,20},{1,9},{5,13},{25,17},{29,21},{2,10},{... | collective-permute-start | bytes 3145736 | tf_op jit(solution)/shard_map/ppermute | solution.py:708
  108.6 40.8 %collective-permute-start.3 = (f32[256,1024]{1,0:T(8,128)S(1)}, f32[256,1024]{1,0:T(8,128)S(1)}, u32[]{:S(2)}, u32[]{:S(2)}) collective-permute-start(f32[256,1024]{1,0:T(8,128)S(1)} %copy-done.4), channel_id=1, source_target_pairs={{8,16},{12,20},{16,8},{20,12},{9,17},{13,21},{17,9},{21,13},{10,18... | collective-permute-start | bytes 3145736 | tf_op jit(solution)/shard_map/ppermute | solution.py:708
  109.4 46.0 %collective-permute-start.4 = (f32[256,1024]{1,0:T(8,128)}, f32[256,1024]{1,0:T(8,128)S(1)}, u32[]{:S(2)}, u32[]{:S(2)}) collective-permute-start(f32[256,1024]{1,0:T(8,128)} %get-tuple-element.505.first), channel_id=1, source_target_pairs={{0,8},{4,12},{24,16},{28,20},{1,9},{5,13},{25,17},{29,21},{2,10},{... | collective-permute-start | bytes 3145736 | tf_op jit(solution)/shard_map/ppermute | solution.py:708
  125.3 43.6 %collective-permute-start.5 = (f32[256,1024]{1,0:T(8,128)}, f32[256,1024]{1,0:T(8,128)S(1)}, u32[]{:S(2)}, u32[]{:S(2)}) collective-permute-start(f32[256,1024]{1,0:T(8,128)} %get-tuple-element.533), channel_id=1, source_target_pairs={{0,1},{1,0},{2,3},{3,2},{4,5},{5,4},{6,7},{7,6},{8,9},{9,8},{10,11... | collective-permute-start | bytes 3145736 | tf_op jit(solution)/shard_map/ppermute | solution.py:708
  126.8 45.6 %collective-permute-start.6 = (f32[256,1024]{1,0:T(8,128)}, f32[256,1024]{1,0:T(8,128)S(1)}, u32[]{:S(2)}, u32[]{:S(2)}) collective-permute-start(f32[256,1024]{1,0:T(8,128)} %get-tuple-element.539), channel_id=1, source_target_pairs={{0,2},{1,3},{2,0},{3,1},{4,6},{5,7},{6,4},{7,5},{8,10},{9,11},{10,... | collective-permute-start | bytes 3145736 | tf_op jit(solution)/shard_map/ppermute | solution.py:708
  184.0 35.7 %collective-permute-start.12 = (f32[256,1024]{1,0:T(8,128)}, f32[256,1024]{1,0:T(8,128)}, u32[]{:S(2)}, u32[]{:S(2)}) collective-permute-start(f32[256,1024]{1,0:T(8,128)} %shard_map.249.second), channel_id=1, source_target_pairs={{8,0},{12,4},{16,24},{20,28},{9,1},{13,5},{17,25},{21,29},{10,2},{... | collective-permute-start | bytes 3145736 | tf_op jit(solution)/shard_map/ppermute | solution.py:708
  185.3 36.8 %collective-permute-start.13 = (f32[256,1024]{1,0:T(8,128)}, f32[256,1024]{1,0:T(8,128)}, u32[]{:S(2)}, u32[]{:S(2)}) collective-permute-start(f32[256,1024]{1,0:T(8,128)} %shard_map.250.first), channel_id=1, source_target_pairs={{8,16},{12,20},{16,8},{20,12},{9,17},{13,21},{17,9},{21,13},{10,18... | collective-permute-start | bytes 3145736 | tf_op jit(solution)/shard_map/ppermute | solution.py:708
  187.0 37.5 %collective-permute-start.14 = (f32[256,1024]{1,0:T(8,128)}, f32[256,1024]{1,0:T(8,128)}, u32[]{:S(2)}, u32[]{:S(2)}) collective-permute-start(f32[256,1024]{1,0:T(8,128)} %get-tuple-element.586.first), channel_id=1, source_target_pairs={{0,8},{4,12},{24,16},{28,20},{1,9},{5,13},{25,17},{29,21},{2,10},{... | collective-permute-start | bytes 3145736 | tf_op jit(solution)/shard_map/ppermute | solution.py:708
  232.8 24.2 %collective-permute-start.18 = (f32[256,1024]{1,0:T(8,128)S(1)}, f32[256,1024]{1,0:T(8,128)S(1)}, u32[]{:S(2)}, u32[]{:S(2)}) collective-permute-start(f32[256,1024]{1,0:T(8,128)S(1)} %copy-done.6), channel_id=1, source_target_pairs={{0,4},{4,0},{8,12},{12,8},{16,20},{20,16},{24,28},{28,24},{1,5},{5... | collective-permute-start | bytes 3145736 | tf_op jit(solution)/shard_map/ppermute | solution.py:708
  233.1 27.2 %collective-permute-start.19 = (f32[256,1024]{1,0:T(8,128)S(1)}, f32[256,1024]{1,0:T(8,128)S(1)}, u32[]{:S(2)}, u32[]{:S(2)}) collective-permute-start(f32[256,1024]{1,0:T(8,128)S(1)} %copy-done.7), channel_id=1, source_target_pairs={{8,0},{12,4},{16,24},{20,28},{9,1},{13,5},{17,25},{21,29},{10,2},{... | collective-permute-start | bytes 3145736 | tf_op jit(solution)/shard_map/ppermute | solution.py:708
  235.9 35.0 %collective-permute-start.20 = (f32[256,1024]{1,0:T(8,128)S(1)}, f32[256,1024]{1,0:T(8,128)S(1)}, u32[]{:S(2)}, u32[]{:S(2)}) collective-permute-start(f32[256,1024]{1,0:T(8,128)S(1)} %copy-done.3), channel_id=1, source_target_pairs={{8,16},{12,20},{16,8},{20,12},{9,17},{13,21},{17,9},{21,13},{10,18... | collective-permute-start | bytes 3145736 | tf_op jit(solution)/shard_map/ppermute | solution.py:708
  247.9 26.4 %collective-permute-start.23 = (f32[256,1024]{1,0:T(8,128)}, f32[256,1024]{1,0:T(8,128)}, u32[]{:S(2)}, u32[]{:S(2)}) collective-permute-start(f32[256,1024]{1,0:T(8,128)} %shard_map.261.refs_0_), channel_id=1, source_target_pairs={{0,1},{1,0},{2,3},{3,2},{4,5},{5,4},{6,7},{7,6},{8,9},{9,8},{10,11... | collective-permute-start | bytes 3145736 | tf_op jit(solution)/shard_map/ppermute | solution.py:708
  257.0 26.4 %collective-permute-start.24 = (f32[256,1024]{1,0:T(8,128)}, f32[256,1024]{1,0:T(8,128)S(1)}, u32[]{:S(2)}, u32[]{:S(2)}) collective-permute-start(f32[256,1024]{1,0:T(8,128)} %shard_map.262.refs_2_), channel_id=1, source_target_pairs={{0,2},{1,3},{2,0},{3,1},{4,6},{5,7},{6,4},{7,5},{8,10},{9,11},{10,... | collective-permute-start | bytes 3145736 | tf_op jit(solution)/shard_map/ppermute | solution.py:708
  269.4 26.1 %collective-permute-start.25 = (f32[256,1024]{1,0:T(8,128)}, f32[256,1024]{1,0:T(8,128)}, u32[]{:S(2)}, u32[]{:S(2)}) collective-permute-start(f32[256,1024]{1,0:T(8,128)} %get-tuple-element.649), channel_id=1, source_target_pairs={{0,1},{1,0},{2,3},{3,2},{4,5},{5,4},{6,7},{7,6},{8,9},{9,8},{10,11... | collective-permute-start | bytes 3145736 | tf_op jit(solution)/shard_map/ppermute | solution.py:708
  270.9 31.9 %collective-permute-start.26 = (f32[256,1024]{1,0:T(8,128)}, f32[256,1024]{1,0:T(8,128)S(1)}, u32[]{:S(2)}, u32[]{:S(2)}) collective-permute-start(f32[256,1024]{1,0:T(8,128)} %get-tuple-element.655), channel_id=1, source_target_pairs={{0,2},{1,3},{2,0},{3,1},{4,6},{5,7},{6,4},{7,5},{8,10},{9,11},{10,... | collective-permute-start | bytes 3145736 | tf_op jit(solution)/shard_map/ppermute | solution.py:708
  274.3 38.0 %collective-permute-start.27 = (f32[256,1024]{1,0:T(8,128)}, f32[256,1024]{1,0:T(8,128)S(1)}, u32[]{:S(2)}, u32[]{:S(2)}) collective-permute-start(f32[256,1024]{1,0:T(8,128)} %shard_map.264.second), channel_id=1, source_target_pairs={{8,0},{12,4},{16,24},{20,28},{9,1},{13,5},{17,25},{21,29},{10,2},{... | collective-permute-start | bytes 3145736 | tf_op jit(solution)/shard_map/ppermute | solution.py:708
  283.4 32.2 %collective-permute-start.28 = (f32[256,768]{1,0:T(8,128)}, f32[256,768]{1,0:T(8,128)}, u32[]{:S(2)}, u32[]{:S(2)}) collective-permute-start(f32[256,768]{1,0:T(8,128)} %shard_map.265.first), channel_id=1, source_target_pairs={{8,16},{12,20},{16,8},{20,12},{9,17},{13,21},{17,9},{21,13},{10,18... | collective-permute-start | bytes 2359304 | tf_op jit(solution)/shard_map/ppermute | solution.py:708
  285.0 34.2 %collective-permute-start.29 = (f32[256,768]{1,0:T(8,128)}, f32[256,768]{1,0:T(8,128)}, u32[]{:S(2)}, u32[]{:S(2)}) collective-permute-start(f32[256,768]{1,0:T(8,128)} %get-tuple-element.680.first), channel_id=1, source_target_pairs={{0,8},{4,12},{24,16},{28,20},{1,9},{5,13},{25,17},{29,21},{2,10},{... | collective-permute-start | bytes 2359304 | tf_op jit(solution)/shard_map/ppermute | solution.py:708
  317.7 29.5 %collective-permute-start.33 = (f32[256,768]{1,0:T(8,128)}, f32[256,768]{1,0:T(8,128)S(1)}, u32[]{:S(2)}, u32[]{:S(2)}) collective-permute-start(f32[256,768]{1,0:T(8,128)} %shard_map.271.second), channel_id=1, source_target_pairs={{8,0},{12,4},{16,24},{20,28},{9,1},{13,5},{17,25},{21,29},{10,2},{... | collective-permute-start | bytes 2359304 | tf_op jit(solution)/shard_map/ppermute | solution.py:708
  321.3 28.9 %collective-permute-start.34 = (f32[256,768]{1,0:T(8,128)}, f32[256,768]{1,0:T(8,128)S(1)}, u32[]{:S(2)}, u32[]{:S(2)}) collective-permute-start(f32[256,768]{1,0:T(8,128)} %shard_map.272.first), channel_id=1, source_target_pairs={{8,16},{12,20},{16,8},{20,12},{9,17},{13,21},{17,9},{21,13},{10,18... | collective-permute-start | bytes 2359304 | tf_op jit(solution)/shard_map/ppermute | solution.py:708
  326.1 30.4 %collective-permute-start.35 = (f32[136,1024]{1,0:T(8,128)}, f32[136,1024]{1,0:T(8,128)S(1)}, u32[]{:S(2)}, u32[]{:S(2)}) collective-permute-start(f32[136,1024]{1,0:T(8,128)} %shard_map.273.first), channel_id=1, source_target_pairs={{0,8},{4,12},{24,16},{28,20},{1,9},{5,13},{25,17},{29,21},{2,10},{... | collective-permute-start | bytes 1671176 | tf_op jit(solution)/shard_map/ppermute | solution.py:708
  375.0 24.8 %collective-permute-start.42 = (f32[256,1024]{1,0:T(8,128)S(1)}, f32[256,1024]{1,0:T(8,128)S(1)}, u32[]{:S(2)}, u32[]{:S(2)}) collective-permute-start(f32[256,1024]{1,0:T(8,128)S(1)} %copy-done.5), channel_id=1, source_target_pairs={{0,1},{1,0},{2,3},{3,2},{4,5},{5,4},{6,7},{7,6},{8,9},{9,8},{10,11... | collective-permute-start | bytes 3145736 | tf_op jit(solution)/shard_map/ppermute | solution.py:708
  376.5 24.7 %collective-permute-start.43 = (f32[256,1024]{1,0:T(8,128)}, f32[256,1024]{1,0:T(8,128)S(1)}, u32[]{:S(2)}, u32[]{:S(2)}) collective-permute-start(f32[256,1024]{1,0:T(8,128)} %shard_map.281.refs_2_), channel_id=1, source_target_pairs={{0,2},{1,3},{2,0},{3,1},{4,6},{5,7},{6,4},{7,5},{8,10},{9,11},{10,... | collective-permute-start | bytes 3145736 | tf_op jit(solution)/shard_map/ppermute | solution.py:708
  (74 other events, 685.7 us)
Sparse Core Ops, SparseCore 0:
  64.4 89.3 all-reduce.3

commit v5 on v4

--- a/solution.py
+++ b/solution.py
@@ -204,7 +204,7 @@
         in_specs=[VMEM] * 2,
         out_specs=(VMEM,) * 5,
         scratch_shapes=[bias_held(min(256, seq_len))],
-        compiler_params=pltpu.CompilerParams(vmem_limit_bytes=56 * 2**20),
+        compiler_params=pltpu.CompilerParams(vmem_limit_bytes=24 * 2**20),
     )(angles, projected)
 
 
@@ -223,7 +223,7 @@
             cross,
             bias_held(min(256, seq_len)),
         ],
-        compiler_params=pltpu.CompilerParams(vmem_limit_bytes=56 * 2**20),
+        compiler_params=pltpu.CompilerParams(vmem_limit_bytes=24 * 2**20),
     )(angles, queries, keys, values, sums, attended, d_attended)
 
 
@@ -242,7 +242,8 @@
     return pl.BlockSpec(array.shape, lambda i, *order: (0,) * array.ndim)
 
 
-PARAMS = pltpu.CompilerParams(vmem_limit_bytes=56 * 2**20)
+PARAMS = pltpu.CompilerParams(vmem_limit_bytes=40 * 2**20)
+SMALL = pltpu.CompilerParams(vmem_limit_bytes=48 * 2**20)
 
 
 def forward_kernel(
@@ -487,7 +488,7 @@
 
 
 def steps_for(rows):
-    return 2 if rows % 16 == 0 else 1
+    return 4 if rows % 512 == 0 else 2 if rows % 16 == 0 else 1
 
 
 def scalars(*values):
@@ -508,7 +509,7 @@
         in_specs=[spec] * 2,
         out_specs=spec,
         out_shape=float_shape(rows, width),
-        compiler_params=PARAMS,
+        compiler_params=SMALL,
     )(first, second)
 
 
@@ -532,7 +533,7 @@
             num_scalar_prefetch=1, grid=(steps,), in_specs=[spec] * 2, out_specs=spec
         ),
         out_shape=float_shape(rows, width),
-        compiler_params=PARAMS,
+        compiler_params=SMALL,
     )(scalars(flag), first, second)
 
 
@@ -555,7 +556,7 @@
         in_specs=[spec] * 2,
         out_specs=tuple(whole(out) for out in outs),
         out_shape=outs,
-        compiler_params=PARAMS,
+        compiler_params=SMALL,
     )(first, second)
 
 
@@ -584,7 +585,7 @@
             out_specs=tuple(whole(out) for out in outs),
         ),
         out_shape=outs,
-        compiler_params=PARAMS,
+        compiler_params=SMALL,
     )(scalars(mine), first, second)
 
 
@@ -611,7 +612,7 @@
             out_specs=spec,
         ),
         out_shape=float_shape(rows, width),
-        compiler_params=PARAMS,
+        compiler_params=SMALL,
     )(scalars(at // rows), first, second, tokens, cotangent)
 
 
@@ -636,13 +637,13 @@
             out_specs=tiled(width, rows, lambda i, mine: i),
         ),
         out_shape=float_shape(2 * rows, width),
-        compiler_params=PARAMS,
+        compiler_params=SMALL,
     )(scalars(mine), own, other)
 
 
-def collect_kernel(order, *refs):
-    parts, out = refs[:4], refs[-1]
-    extra = refs[4:-1]
+def collect_kernel(count, order, *refs):
+    parts, out = refs[:count], refs[-1]
+    extra = refs[count:-1]
     for number, part in enumerate(parts):
 
         @pl.when(order[pl.program_id(0)] == number)
@@ -657,21 +658,22 @@
 
 def collect(order, parts, *extra):
     rows, width = parts[0].shape
-    specs = [pl.BlockSpec((rows, width), lambda i, order: (0, 0))] * 4
+    count = len(parts)
+    specs = [pl.BlockSpec((rows, width), lambda i, order: (0, 0))] * count
     if extra:
         specs = specs + [tiled(width, rows, lambda i, order: i), whole(extra[1])]
     return pl.pallas_call(
-        collect_kernel,
+        functools.partial(collect_kernel, count),
         grid_spec=pltpu.PrefetchScalarGridSpec(
             num_scalar_prefetch=1,
-            grid=(4,),
+            grid=(count,),
             in_specs=specs,
             out_specs=tiled(width, rows, lambda i, order: i),
         ),
         out_shape=jax.ShapeDtypeStruct(
-            (4 * rows, width), extra[0].dtype if extra else jnp.float32
+            (count * rows, width), extra[0].dtype if extra else jnp.float32
         ),
-        compiler_params=PARAMS,
+        compiler_params=SMALL,
     )(order, *parts, *extra)
 
 
@@ -766,6 +768,10 @@
             array = choose((place == s) | (place == chips - 1 - s), got, array)
     got = yield array, "dp", swap_pairs(size, 1)
     return array, got
+
+
+def add_end(keep, got, first):
+    return add(keep, got)
 
 
 def small_steps(stats, size):
@@ -828,6 +834,7 @@
         return chain(core_steps(run(step, first_mat, *parts), dp_size, chunks))
 
     vectors = [v[None, :] for v in (attn_gain, attn_shift, mlp_gain, mlp_shift)]
+    angles = run(turn_angles, segment[0])
     attn_low, mlp_low, projected, d_attended, hidden, slope = run(
         lambda *a: forward(a[0], a[1], vectors, *a[2:], lanes=lanes * groups),
         tokens,
@@ -838,36 +845,20 @@
         w_up,
         b_up[None, :],
     )
-    inner = hidden.shape[1]
-    core_down = grads(1, hidden, cotangent, begin=inner // 2, rows=inner // 2)
-    top = run(
-        lambda h, dy: gradient(0, h, [dy], width, 0, inner // 2), hidden, cotangent
-    )
-    top = lax.psum(top, "dp")
-    angles = run(turn_angles, segment[0])
-    down = chain(lines(core_down)[0])
+    core_down = grads(1, hidden, cotangent)
     d_pre, scaled_mlp, sums_mlp, up_bias = run(
         feed_back, tokens, cotangent, slope, w_down, w_up, mlp_gain[None, :]
     )
-    core_up = grads(2, mlp_low, d_pre)
+    down = chain(lines(core_down)[0])
+    core_up = grads(1, mlp_low, d_pre)
     kept = run(functools.partial(attend, heads=heads), angles, projected)
     attended = kept[0]
-    up = lines(core_up)
-    down.on()
-    up[0] = chain(up[0])
     partial = run(branches, tiles, attended, hidden, w_out, w_down)
     result = [
-        chain(
-            tensor_steps(
-                partial[p],
-                partial[2 + p],
-                tensor_size,
-                orders[p],
-                lambda keep, got, first: add(keep, got),
-            )
-        )
+        chain(tensor_steps(partial[p], partial[2 + p], tensor_size, orders[p], add_end))
         for p in range(2)
     ]
+    up = lines(core_up)[0]
     back = []
     for begin in range(0, heads, group):
         def step(angles, d_attended, *kept, begin=begin):
@@ -875,8 +866,7 @@
 
         back.append(run(step, angles, d_attended, *kept))
     down.on()
-    up[0].on()
-    up[1] = chain(up[1])
+    up = chain(up)
     *scaled, sums_attn, qkv_bias, branch_sum = run(
         lambda tiles, *a: input_back(tiles, a[:-5], wide, *a[-5:]),
         tiles,
@@ -887,20 +877,16 @@
         w_qkv,
         attn_gain[None, :],
     )
-    top = order.tie(*top)
     for part in result:
         part.on()
     small = chain(small_steps(jnp.concatenate([sums_attn, sums_mlp], axis=0), tensor_size))
-    core_qkv = grads(2, attn_low, *back, wide=wide)
+    core_qkv = grads(1, attn_low, *back, wide=wide)
     small.on()
-    grad_out = run(inner_rows, attended, cotangent)
-    qkv = lines(core_qkv)
-    stats = small.end()
     for part in result:
         part.on()
-    for part in (down, up[0], up[1]):
-        part.on()
-    qkv[0] = chain(qkv[0])
+    grad_out = run(inner_rows, attended, cotangent)
+    qkv = lines(core_qkv)[0]
+    stats = small.end()
 
     sizes = (width,) * 4 + (w_qkv.shape[1], w_up.shape[1], width)
     ends = [sum(sizes[: k + 1]) for k in range(len(sizes))]
@@ -923,44 +909,42 @@
 
         return finish
 
-    out = lines(core_out)[0]
     for part in result:
         part.on()
-    down.end()
     d_tokens = [
         chain(tensor_steps(scaled[p], scaled[2 + p], tensor_size, orders[p], back_end(p)))
         for p in range(2)
     ]
-    for part in (up[0], up[1], qkv[0]):
-        part.on()
-    qkv[1] = chain(qkv[1])
-    grad_down = run(collect, scalars(0, 1, 2 + core, 3 - core), [*top, *down.end()])
+    out = lines(core_out)[0]
+    down.on()
+    up.on()
+    qkv = chain(qkv)
     spots = scalars(mine[0], 1 - mine[0], 2 + mine[1], 3 - mine[1])
-    up[0].end()
     ended = [part.end() for part in result]
     for part in d_tokens:
         part.on()
     result = run(collect, spots, [*ended[0], *ended[1]], tokens, b_branch[None, :])
-    for part in (up[1], qkv[0], qkv[1]):
+    for part in d_tokens:
+        part.on()
+    for part in (down, up, qkv):
         part.on()
     out = chain(out)
-    up[1].end()
+    down.end()
     for part in d_tokens:
         part.on()
-    core_spots = jnp.where(core == 0, scalars(0, 2, 1, 3), scalars(1, 3, 0, 2))
-    grad_up = run(collect, core_spots, [*up[0].end(), *up[1].end()])
-    for part in (qkv[0], qkv[1], out):
+    core_spots = scalars(core, 1 - core)
+    grad_down = run(collect, core_spots, [*down.end()])
+    for part in (out, qkv, up):
         part.on()
-    for part in d_tokens:
-        part.on()
-    qkv[0].end()
-    for part in (qkv[1], out):
-        part.on()
-    qkv[1].end()
-    grad_qkv = run(collect, core_spots, [*qkv[0].end(), *qkv[1].end()])
     ended = [part.end() for part in d_tokens]
+    d_tokens = run(collect, spots, [*ended[0], *ended[1]])
+    up.end()
+    grad_up = run(collect, core_spots, [*up.end()])
     out.on()
-    d_tokens = run(collect, spots, [*ended[0], *ended[1]])
+    qkv.on()
+    out.on()
+    qkv.end()
+    grad_qkv = run(collect, core_spots, [*qkv.end()])
     packed = order.tie(assemble(core, (out.end(),)))
     grad_out = packed[: w_out.shape[0]]
     vectors = packed[w_out.shape[0] :].reshape(-1)

time: 428 us -> 392 us (0.916)
  Pallas kernels: 213 us -> 143 us
  waiting for transfers between devices: 91.7 us -> 129 us
  local copies, waits for them, and re-layouts: 22.1 us -> 46 us
  between operations: 14.8 us -> 1.58 us
  starting transfers between devices: 70.6 us -> 59.6 us
    ppermute x46 -> x38, waiting for transfers between devices: 91.7 us -> 129 us  [_go(): self.held = lax.ppermute(array, axis, pairs)]
    unnamed x106 -> x144, local copies, waits for them, and re-layouts: 16.9 us -> 41.5 us
    pallas_call x4 -> x3, Pallas kernels: 26.7 us -> 15 us  [gradient(): pl.pallas_call(functools.partial(gradient_kernel, wide), grid_spec=pltpu....]
    ppermute x46 -> x38, starting transfers between devices: 70.5 us -> 59.6 us  [_go(): self.held = lax.ppermute(array, axis, pairs)]
    pallas_call x14 -> x10, Pallas kernels: 31 us -> 22.7 us  [add(): pl.pallas_call(add_kernel, grid=(steps,), in_specs=[spec] * 2, out_specs=...]
    pallas_call x5, Pallas kernels: 26.7 us -> 19.1 us  [collect(): pl.pallas_call(functools.partial(collect_kernel, count), grid_spec=pltpu....]
    pallas_call x4, Pallas kernels: 8.86 us -> 1.48 us  [join(): pl.pallas_call(join_kernel, grid_spec=pltpu.PrefetchScalarGridSpec(num_sc...]
    pallas_call x2, Pallas kernels: 21.1 us -> 14.6 us  [attend_back(): pl.pallas_call(functools.partial(attend_back_kernel, begin, heads), out_s...]
  transfers between devices with their start and end apart: 47 -> 38, of which waited for: 17 -> 18; matrix products, arithmetic and copies ran while one was open for 2% -> 2% of each run, Pallas kernels for 37% -> 27%
where the time goes in v5:
time: 392 us; the launch traced here: 385 us
  Pallas kernels  143 us (36%)
  waiting for transfers between devices  129 us (33%)
  starting transfers between devices  59.6 us (15%)
  local copies, waits for them, and re-layouts  46 us (12%)
  other arithmetic  4.69 us (1%)
    ppermute x38, waiting for transfers between devices, _go(): self.held = lax.ppermute(array, axis, pairs)  129 us
    ppermute x38, starting transfers between devices, _go(): self.held = lax.ppermute(array, axis, pairs)  59.6 us
    unnamed x144, local copies, waits for them, and re-layouts  41.5 us
    pallas_call x10, Pallas kernels, add(): pl.pallas_call(add_kernel, grid=(steps,), in_specs=[spec] * 2, out_specs=...  22.7 us
    pallas_call x5, Pallas kernels, collect(): pl.pallas_call(functools.partial(collect_kernel, count), grid_spec=pltpu....  19.1 us
    pallas_call x3, Pallas kernels, gradient(): pl.pallas_call(functools.partial(gradient_kernel, wide), grid_spec=pltpu....  15 us
    pallas_call x2, Pallas kernels, attend_back(): pl.pallas_call(functools.partial(attend_back_kernel, begin, heads), out_s...  14.6 us
    pallas_call x1, Pallas kernels, attend(): pl.pallas_call(functools.partial(attend_kernel, heads), out_shape=(shape(...  12.8 us
  transfers between devices with their start and end apart: 38, of which 18 were waited for; matrix products, arithmetic and copies ran while one was open for 2% of the time, Pallas kernels for 27%

profile of v5, /device:TPU:0, one launch (start us, length us, event | category | flops | bytes accessed | tf_op | source)
XLA Modules:
  0.0 385.3 jit_solution(1215495813750861598)
XLA Ops:
  14.7 10.6 %shard_map.237 = (bf16[1024,1024]{1,0:T(8,128)(2,1)S(1)}, bf16[1024,1024]{1,0:T(8,128)(2,1)S(1)}, f32[1024,768]{1,0:T(8,128)}, bf16[1024,256]{1,0:T(8,128)(2,1)S...) custom-call(bf16[1024,1024]{1,0:T(8,128)(2,1)S(1)} %copy-done.2, bf16[1024,1024]{1,0:T(8,128)(2,1)S(1)} %copy-done, ...), custom_call_target="tpu_custom_call" | custom-call | tf_op jit(solution)/shard_map/pallas_call | solution.py:297
  37.9 8.4 %shard_map.239 = (bf16[1024,1024]{1,0:T(8,128)(2,1)S(1)}, f32[1024,1024]{1,0:T(8,128)}, f32[2,1024]{1,0:T(2,128)S(1)}, f32[1,1024]{1,0:T(1,128)S(1)}) custom-call(bf16[1024,1024]{1,0:T(8,128)(2,1)S(1)} %copy-done.3, bf16[1024,1024]{1,0:T(8,128)(2,1)S(1)} %copy-done.1, f32[1024,1024]{1,0:T(8,128)} %get-tuple-element.365.slope, ...), custom_call_target="tpu_custom_call" | custom-call | tf_op jit(solution)/shard_map/pallas_call | solution.py:337
  57.4 6.4 %collective-permute-start.2 = (f32[512,1024]{1,0:T(8,128)}, f32[512,1024]{1,0:T(8,128)}, u32[]{:S(2)}, u32[]{:S(2)}) collective-permute-start(f32[512,1024]{1,0:T(8,128)} %shard_map.240.first), channel_id=1, source_target_pairs={{0,8},{4,12},{24,16},{28,20},{1,9},{5,13},{25,17},{29,21},{2,10},{... | collective-permute-start | bytes 6291464 | tf_op jit(solution)/shard_map/ppermute | solution.py:710
  65.9 12.8 %shard_map.242 = (bf16[1024,256]{1,0:T(8,128)(2,1)S(1)}, f32[1024,128]{1,0:T(8,128)S(1)}, bf16[4,1024,64]{2,1,0:T(8,128)(2,1)S(1)}, bf16[4,1024,64]{2,1,0:T(8,128)(2,1)S(1)}, bf16[4,1024,64]{2,1,0:T(8,128)(2,1)S(1)}) custom-call(f32[24,1024]{1,0:T(8,128)S(1)} %pad_maximum_fusion.1.angles, f32[1024,768]{1,0:T(8,128)S(1)} %copy-done.19), custom_call_target="tpu_custom_call" | custom-call | tf_op jit(solution)/shard_map/pallas_call | solution.py:197
  80.3 6.0 %shard_map.243 = (f32[256,1024]{1,0:T(8,128)}, f32[256,1024]{1,0:T(8,128)}, f32[256,1024]{1,0:T(8,128)S(1)}, f32[256,1024]{1,0:T(8,128)S(1)}) custom-call(s32[4]{0:T(128)S(1)} %get-tuple-element.446.tiles, bf16[1024,256]{1,0:T(8,128)(2,1)S(1)} %get-tuple-element.500.attended, bf16[1024,1024]{1,0:T(8,128)(2,1)S(1)} %copy-done.12, ...), custom_call_target="tpu_custom_call" | custom-call | tf_op jit(solution)/shard_map/pallas_call | solution.py:368
  89.4 7.2 %shard_map.244.refs_0_ = bf16[1024,384]{1,0:T(8,128)(2,1)S(1)} custom-call(f32[24,1024]{1,0:T(8,128)S(1)} %pad_maximum_fusion.1.angles, bf16[4,1024,64]{2,1,0:T(8,128)(2,1)S(1)} %get-tuple-element.429.q_s, bf16[4,1024,64]{2,1,0:T(8,128)(2,1)S(1)} %get-tuple-element.430.k_s, bf16[4,1024,64]{2,1,0:T(8,128)(2,1)S(1)} %get-tuple-element.431.v_s, ...), custom_call_target="tpu_custom_call" | custom-call | tf_op jit(solution)/shard_map/pallas_call | solution.py:215
  96.6 7.4 %shard_map.245.refs_1_ = bf16[1024,384]{1,0:T(8,128)(2,1)S(1)} custom-call(f32[24,1024]{1,0:T(8,128)S(1)} %pad_maximum_fusion.1.angles, bf16[4,1024,64]{2,1,0:T(8,128)(2,1)S(1)} %get-tuple-element.429.q_s, bf16[4,1024,64]{2,1,0:T(8,128)(2,1)S(1)} %get-tuple-element.430.k_s, bf16[4,1024,64]{2,1,0:T(8,128)(2,1)S(1)} %get-tuple-element.431.v_s, ...), custom_call_target="tpu_custom_call" | custom-call | tf_op jit(solution)/shard_map/pallas_call | solution.py:215
  114.6 7.7 %shard_map.248 = (f32[256,1024]{1,0:T(8,128)}, f32[256,1024]{1,0:T(8,128)S(1)}, f32[256,1024]{1,0:T(8,128)S(1)}, f32[256,1024]{1,0:T(8,128)S(1)}, f32[2,1024]{1,...) custom-call(s32[4]{0:T(128)S(1)} %get-tuple-element.446.tiles, bf16[1024,384]{1,0:T(8,128)(2,1)S(1)} %shard_map.244.refs_0_, ...), custom_call_target="tpu_custom_call" | custom-call | tf_op jit(solution)/shard_map/pallas_call | solution.py:424
  130.4 5.9 %shard_map.251 = (f32[512,768]{1,0:T(8,128)}, f32[512,768]{1,0:T(8,128)S(1)}) custom-call(s32[4]{0:T(128)S(1)} %and_select_fusion.tiles, bf16[1024,1024]{1,0:T(8,128)(2,1)S(1)} %copy-done.26, bf16[1024,384]{1,0:T(8,128)(2,1)S(1)} %shard_map.244.refs_0_, bf16[1024,384]{1,0:T(8,128)(2,1)S(1)} %shard_map.245.refs_1_), custom_call_target="tpu_custom_call" | custom-call | tf_op jit(solution)/shard_map/pallas_call | solution.py:469
  143.0 10.5 %collective-permute-done.5 = f32[4,1024]{1,0:T(4,128)S(1)} collective-permute-done((f32[4,1024]{1,0:T(4,128)S(1)}, f32[4,1024]{1,0:T(4,128)S(1)}, u32[]{:S(2)}, u32[]{:S(2)}) %collective-permute-start.5) | collective-permute-done | bytes 16416 | tf_op jit(solution)/shard_map/ppermute | solution.py:710
  153.5 5.7 %collective-permute-start.14 = (f32[512,1024]{1,0:T(8,128)}, f32[512,1024]{1,0:T(8,128)}, u32[]{:S(2)}, u32[]{:S(2)}) collective-permute-start(f32[512,1024]{1,0:T(8,128)} %copy-done.6), channel_id=1, source_target_pairs={{0,8},{4,12},{24,16},{28,20},{1,9},{5,13},{25,17},{29,21},{2,10},{... | collective-permute-start | bytes 6291464 | tf_op jit(solution)/shard_map/ppermute | solution.py:710
  173.0 7.3 %collective-permute-done.10.other = f32[128,1024]{1,0:T(8,128)S(1)} collective-permute-done((f32[128,1024]{1,0:T(8,128)S(1)}, f32[128,1024]{1,0:T(8,128)S(1)}, u32[]{:S(2)}, u32[]{:S(2)}) %collective-permute-start.10) | collective-permute-done | bytes 524320 | tf_op jit(solution)/shard_map/ppermute | solution.py:710
  196.0 6.8 %collective-permute-done.14.second = f32[512,1024]{1,0:T(8,128)} collective-permute-done((f32[512,1024]{1,0:T(8,128)}, f32[512,1024]{1,0:T(8,128)}, u32[]{:S(2)}, u32[]{:S(2)}) %collective-permute-start.14) | collective-permute-done | bytes 2097184 | tf_op jit(solution)/shard_map/ppermute | solution.py:710
  213.7 6.5 %collective-permute-done.16.refs_3_ = f32[256,1024]{1,0:T(8,128)S(1)} collective-permute-done((f32[256,1024]{1,0:T(8,128)S(1)}, f32[256,1024]{1,0:T(8,128)S(1)}, u32[]{:S(2)}, u32[]{:S(2)}) %collective-permute-start.16) | collective-permute-done | bytes 1048608 | tf_op jit(solution)/shard_map/ppermute | solution.py:710
  220.1 10.9 %collective-permute-done.17.second = f32[256,1024]{1,0:T(8,128)S(1)} collective-permute-done((f32[256,1024]{1,0:T(8,128)}, f32[256,1024]{1,0:T(8,128)S(1)}, u32[]{:S(2)}, u32[]{:S(2)}) %collective-permute-start.17) | collective-permute-done | bytes 1048608 | tf_op jit(solution)/shard_map/ppermute | solution.py:710
  233.3 9.3 %collective-permute-done.18.second = f32[256,1024]{1,0:T(8,128)S(1)} collective-permute-done((f32[256,1024]{1,0:T(8,128)S(1)}, f32[256,1024]{1,0:T(8,128)S(1)}, u32[]{:S(2)}, u32[]{:S(2)}) %collective-permute-start.18) | collective-permute-done | bytes 1048608 | tf_op jit(solution)/shard_map/ppermute | solution.py:710
  245.9 7.6 %collective-permute-start.23 = (f32[512,768]{1,0:T(8,128)}, f32[512,768]{1,0:T(8,128)}, u32[]{:S(2)}, u32[]{:S(2)}) collective-permute-start(f32[512,768]{1,0:T(8,128)} %shard_map.258.first), channel_id=1, source_target_pairs={{0,8},{4,12},{24,16},{28,20},{1,9},{5,13},{25,17},{29,21},{2,10},{... | collective-permute-start | bytes 4718600 | tf_op jit(solution)/shard_map/ppermute | solution.py:710
  272.6 9.9 %collective-permute-done.23.second = f32[512,768]{1,0:T(8,128)} collective-permute-done((f32[512,768]{1,0:T(8,128)}, f32[512,768]{1,0:T(8,128)}, u32[]{:S(2)}, u32[]{:S(2)}) %collective-permute-start.23) | collective-permute-done | bytes 1572896 | tf_op jit(solution)/shard_map/ppermute | solution.py:710
  287.1 6.1 %collective-permute-start.27 = (f32[136,1024]{1,0:T(8,128)S(1)}, f32[136,1024]{1,0:T(8,128)S(1)}, u32[]{:S(2)}, u32[]{:S(2)}) collective-permute-start(f32[136,1024]{1,0:T(8,128)S(1)} %shard_map.267.first), channel_id=1, source_target_pairs={{0,8},{4,12},{24,16},{28,20},{1,9},{5,13},{25,17},{29,21},{2,10},{... | collective-permute-start | bytes 1671176 | tf_op jit(solution)/shard_map/ppermute | solution.py:710
  295.3 7.1 %collective-permute-done.25.other = f32[128,1024]{1,0:T(8,128)S(1)} collective-permute-done((f32[128,1024]{1,0:T(8,128)S(1)}, f32[128,1024]{1,0:T(8,128)S(1)}, u32[]{:S(2)}, u32[]{:S(2)}) %collective-permute-start.25) | collective-permute-done | bytes 524320 | tf_op jit(solution)/shard_map/ppermute | solution.py:710
  309.7 11.5 %collective-permute-done.29.first = f32[512,1024]{1,0:T(8,128)S(1)} collective-permute-done((f32[512,1024]{1,0:T(8,128)S(1)}, f32[512,1024]{1,0:T(8,128)S(1)}, u32[]{:S(2)}, u32[]{:S(2)}) %collective-permute-start.29) | collective-permute-done | bytes 2097184 | tf_op jit(solution)/shard_map/ppermute | solution.py:710
  327.7 21.5 %collective-permute-done.30.refs_1_ = f32[256,1024]{1,0:T(8,128)S(1)} collective-permute-done((f32[256,1024]{1,0:T(8,128)S(1)}, f32[256,1024]{1,0:T(8,128)S(1)}, u32[]{:S(2)}, u32[]{:S(2)}) %collective-permute-start.30) | collective-permute-done | bytes 1048608 | tf_op jit(solution)/shard_map/ppermute | solution.py:710
  357.6 7.3 %collective-permute-done.34.first = f32[512,768]{1,0:T(8,128)S(1)} collective-permute-done((f32[512,768]{1,0:T(8,128)S(1)}, f32[512,768]{1,0:T(8,128)S(1)}, u32[]{:S(2)}, u32[]{:S(2)}) %collective-permute-start.34) | collective-permute-done | bytes 1572896 | tf_op jit(solution)/shard_map/ppermute | solution.py:710
  366.6 9.1 %collective-permute-done.35.first = f32[136,1024]{1,0:T(8,128)S(1)} collective-permute-done((f32[136,1024]{1,0:T(8,128)S(1)}, f32[136,1024]{1,0:T(8,128)S(1)}, u32[]{:S(2)}, u32[]{:S(2)}) %collective-permute-start.35) | collective-permute-done | bytes 557088 | tf_op jit(solution)/shard_map/ppermute | solution.py:710
  (264 shorter events, 174.3 us)
Async XLA Ops:
  57.3 32.1 %collective-permute-start.1 = (f32[512,1024]{1,0:T(8,128)}, f32[512,1024]{1,0:T(8,128)}, u32[]{:S(2)}, u32[]{:S(2)}) collective-permute-start(f32[512,1024]{1,0:T(8,128)} %get-tuple-element.413), channel_id=1, source_target_pairs={{0,4},{4,0},{8,12},{12,8},{16,20},{20,16},{24,28},{28,24},{1,5},{5... | collective-permute-start | bytes 6291464 | tf_op jit(solution)/shard_map/ppermute | solution.py:710
  57.4 50.3 %collective-permute-start.2 = (f32[512,1024]{1,0:T(8,128)}, f32[512,1024]{1,0:T(8,128)}, u32[]{:S(2)}, u32[]{:S(2)}) collective-permute-start(f32[512,1024]{1,0:T(8,128)} %shard_map.240.first), channel_id=1, source_target_pairs={{0,8},{4,12},{24,16},{28,20},{1,9},{5,13},{25,17},{29,21},{2,10},{... | collective-permute-start | bytes 6291464 | tf_op jit(solution)/shard_map/ppermute | solution.py:710
  86.4 38.9 %collective-permute-start.3 = (f32[256,1024]{1,0:T(8,128)}, f32[256,1024]{1,0:T(8,128)}, u32[]{:S(2)}, u32[]{:S(2)}) collective-permute-start(f32[256,1024]{1,0:T(8,128)} %get-tuple-element.462), channel_id=1, source_target_pairs={{0,1},{1,0},{2,3},{3,2},{4,5},{5,4},{6,7},{7,6},{8,9},{9,8},{10,11... | collective-permute-start | bytes 3145736 | tf_op jit(solution)/shard_map/ppermute | solution.py:710
  87.9 40.3 %collective-permute-start.4 = (f32[256,1024]{1,0:T(8,128)}, f32[256,1024]{1,0:T(8,128)}, u32[]{:S(2)}, u32[]{:S(2)}) collective-permute-start(f32[256,1024]{1,0:T(8,128)} %get-tuple-element.468), channel_id=1, source_target_pairs={{0,2},{1,3},{2,0},{3,1},{4,6},{5,7},{6,4},{7,5},{8,10},{9,11},{10,... | collective-permute-start | bytes 3145736 | tf_op jit(solution)/shard_map/ppermute | solution.py:710
  137.4 31.7 %collective-permute-start.8 = (f32[512,768]{1,0:T(8,128)}, f32[512,768]{1,0:T(8,128)}, u32[]{:S(2)}, u32[]{:S(2)}) collective-permute-start(f32[512,768]{1,0:T(8,128)} %get-tuple-element.503), channel_id=1, source_target_pairs={{0,4},{4,0},{8,12},{12,8},{16,20},{20,16},{24,28},{28,24},{1,5},{5... | collective-permute-start | bytes 4718600 | tf_op jit(solution)/shard_map/ppermute | solution.py:710
  138.9 23.9 %collective-permute-start.7 = (f32[128,1024]{1,0:T(8,128)}, f32[128,1024]{1,0:T(8,128)}, u32[]{:S(2)}, u32[]{:S(2)}) collective-permute-start(f32[128,1024]{1,0:T(8,128)} %get-tuple-element.495), channel_id=1, source_target_pairs={{0,1},{1,0},{2,3},{3,2},{4,5},{5,4},{6,7},{7,6},{8,9},{9,8},{10,11... | collective-permute-start | bytes 1572872 | tf_op jit(solution)/shard_map/ppermute | solution.py:710
  140.4 47.2 %collective-permute-start.13 = (f32[512,1024]{1,0:T(8,128)}, f32[512,1024]{1,0:T(8,128)}, u32[]{:S(2)}, u32[]{:S(2)}) collective-permute-start(f32[512,1024]{1,0:T(8,128)} %shard_map.246.first), channel_id=1, source_target_pairs={{8,16},{12,20},{16,8},{20,12},{9,17},{13,21},{17,9},{21,13},{10,18... | collective-permute-start | bytes 6291464 | tf_op jit(solution)/shard_map/ppermute | solution.py:710
  153.5 49.3 %collective-permute-start.14 = (f32[512,1024]{1,0:T(8,128)}, f32[512,1024]{1,0:T(8,128)}, u32[]{:S(2)}, u32[]{:S(2)}) collective-permute-start(f32[512,1024]{1,0:T(8,128)} %copy-done.6), channel_id=1, source_target_pairs={{0,8},{4,12},{24,16},{28,20},{1,9},{5,13},{25,17},{29,21},{2,10},{... | collective-permute-start | bytes 6291464 | tf_op jit(solution)/shard_map/ppermute | solution.py:710
  182.3 26.6 %collective-permute-start.15 = (f32[256,1024]{1,0:T(8,128)S(1)}, f32[256,1024]{1,0:T(8,128)S(1)}, u32[]{:S(2)}, u32[]{:S(2)}) collective-permute-start(f32[256,1024]{1,0:T(8,128)S(1)} %shard_map.254.refs_0_), channel_id=1, source_target_pairs={{0,1},{1,0},{2,3},{3,2},{4,5},{5,4},{6,7},{7,6},{8,9},{9,8},{10,11... | collective-permute-start | bytes 3145736 | tf_op jit(solution)/shard_map/ppermute | solution.py:710
  192.5 72.5 %collective-permute-start.21 = (f32[512,1024]{1,0:T(8,128)}, f32[512,1024]{1,0:T(8,128)}, u32[]{:S(2)}, u32[]{:S(2)}) collective-permute-start(f32[512,1024]{1,0:T(8,128)} %shard_map.256.second), channel_id=1, source_target_pairs={{8,0},{12,4},{16,24},{20,28},{9,1},{13,5},{17,25},{21,29},{10,2},{... | collective-permute-start | bytes 6291464 | tf_op jit(solution)/shard_map/ppermute | solution.py:710
  194.0 26.2 %collective-permute-start.16 = (f32[256,1024]{1,0:T(8,128)S(1)}, f32[256,1024]{1,0:T(8,128)S(1)}, u32[]{:S(2)}, u32[]{:S(2)}) collective-permute-start(f32[256,1024]{1,0:T(8,128)S(1)} %shard_map.255.refs_2_), channel_id=1, source_target_pairs={{0,2},{1,3},{2,0},{3,1},{4,6},{5,7},{6,4},{7,5},{8,10},{9,11},{10,... | collective-permute-start | bytes 3145736 | tf_op jit(solution)/shard_map/ppermute | solution.py:710
  194.5 36.4 %collective-permute-start.17 = (f32[256,1024]{1,0:T(8,128)}, f32[256,1024]{1,0:T(8,128)S(1)}, u32[]{:S(2)}, u32[]{:S(2)}) collective-permute-start(f32[256,1024]{1,0:T(8,128)} %get-tuple-element.546), channel_id=1, source_target_pairs={{0,1},{1,0},{2,3},{3,2},{4,5},{5,4},{6,7},{7,6},{8,9},{9,8},{10,11... | collective-permute-start | bytes 3145736 | tf_op jit(solution)/shard_map/ppermute | solution.py:710
  202.8 39.8 %collective-permute-start.18 = (f32[256,1024]{1,0:T(8,128)S(1)}, f32[256,1024]{1,0:T(8,128)S(1)}, u32[]{:S(2)}, u32[]{:S(2)}) collective-permute-start(f32[256,1024]{1,0:T(8,128)S(1)} %copy-done.68), channel_id=1, source_target_pairs={{0,2},{1,3},{2,0},{3,1},{4,6},{5,7},{6,4},{7,5},{8,10},{9,11},{10,... | collective-permute-start | bytes 3145736 | tf_op jit(solution)/shard_map/ppermute | solution.py:710
  208.9 59.2 %collective-permute-start.22 = (f32[512,1024]{1,0:T(8,128)}, f32[512,1024]{1,0:T(8,128)}, u32[]{:S(2)}, u32[]{:S(2)}) collective-permute-start(f32[512,1024]{1,0:T(8,128)} %shard_map.257.first), channel_id=1, source_target_pairs={{8,16},{12,20},{16,8},{20,12},{9,17},{13,21},{17,9},{21,13},{10,18... | collective-permute-start | bytes 6291464 | tf_op jit(solution)/shard_map/ppermute | solution.py:710
  232.8 29.3 %collective-permute-start.19 = (f32[128,1024]{1,0:T(8,128)}, f32[128,1024]{1,0:T(8,128)}, u32[]{:S(2)}, u32[]{:S(2)}) collective-permute-start(f32[128,1024]{1,0:T(8,128)} %get-tuple-element.569), channel_id=1, source_target_pairs={{0,2},{1,3},{2,0},{3,1},{4,6},{5,7},{6,4},{7,5},{8,10},{9,11},{10,... | collective-permute-start | bytes 1572872 | tf_op jit(solution)/shard_map/ppermute | solution.py:710
  245.9 36.6 %collective-permute-start.23 = (f32[512,768]{1,0:T(8,128)}, f32[512,768]{1,0:T(8,128)}, u32[]{:S(2)}, u32[]{:S(2)}) collective-permute-start(f32[512,768]{1,0:T(8,128)} %shard_map.258.first), channel_id=1, source_target_pairs={{0,8},{4,12},{24,16},{28,20},{1,9},{5,13},{25,17},{29,21},{2,10},{... | collective-permute-start | bytes 4718600 | tf_op jit(solution)/shard_map/ppermute | solution.py:710
  268.0 25.8 %collective-permute-start.24 = (f32[512,1024]{1,0:T(8,128)S(1)}, f32[512,1024]{1,0:T(8,128)}, u32[]{:S(2)}, u32[]{:S(2)}) collective-permute-start(f32[512,1024]{1,0:T(8,128)S(1)} %shard_map.264.refs_0_), channel_id=1, source_target_pairs={{0,4},{4,0},{8,12},{12,8},{16,20},{20,16},{24,28},{28,24},{1,5},{5... | collective-permute-start | bytes 6291464 | tf_op jit(solution)/shard_map/ppermute | solution.py:710
  271.0 50.2 %collective-permute-start.29 = (f32[512,1024]{1,0:T(8,128)S(1)}, f32[512,1024]{1,0:T(8,128)S(1)}, u32[]{:S(2)}, u32[]{:S(2)}) collective-permute-start(f32[512,1024]{1,0:T(8,128)S(1)} %shard_map.265.second), channel_id=1, source_target_pairs={{8,0},{12,4},{16,24},{20,28},{9,1},{13,5},{17,25},{21,29},{10,2},{... | collective-permute-start | bytes 6291464 | tf_op jit(solution)/shard_map/ppermute | solution.py:710
  285.2 22.3 %collective-permute-start.28 = (f32[512,768]{1,0:T(8,128)S(1)}, f32[512,768]{1,0:T(8,128)}, u32[]{:S(2)}, u32[]{:S(2)}) collective-permute-start(f32[512,768]{1,0:T(8,128)S(1)} %shard_map.266.first), channel_id=1, source_target_pairs={{8,16},{12,20},{16,8},{20,12},{9,17},{13,21},{17,9},{21,13},{10,18... | collective-permute-start | bytes 4718600 | tf_op jit(solution)/shard_map/ppermute | solution.py:710
  323.6 29.9 %collective-permute-start.32 = (f32[512,1024]{1,0:T(8,128)S(1)}, f32[512,1024]{1,0:T(8,128)S(1)}, u32[]{:S(2)}, u32[]{:S(2)}) collective-permute-start(f32[512,1024]{1,0:T(8,128)S(1)} %shard_map.273.refs_0_), channel_id=1, source_target_pairs={{0,4},{4,0},{8,12},{12,8},{16,20},{20,16},{24,28},{28,24},{1,5},{5... | collective-permute-start | bytes 6291464 | tf_op jit(solution)/shard_map/ppermute | solution.py:710
  323.7 25.6 %collective-permute-start.30 = (f32[256,1024]{1,0:T(8,128)S(1)}, f32[256,1024]{1,0:T(8,128)S(1)}, u32[]{:S(2)}, u32[]{:S(2)}) collective-permute-start(f32[256,1024]{1,0:T(8,128)S(1)} %shard_map.268.refs_0_), channel_id=1, source_target_pairs={{0,1},{1,0},{2,3},{3,2},{4,5},{5,4},{6,7},{7,6},{8,9},{9,8},{10,11... | collective-permute-start | bytes 3145736 | tf_op jit(solution)/shard_map/ppermute | solution.py:710
  325.2 25.2 %collective-permute-start.31 = (f32[256,1024]{1,0:T(8,128)S(1)}, f32[256,1024]{1,0:T(8,128)S(1)}, u32[]{:S(2)}, u32[]{:S(2)}) collective-permute-start(f32[256,1024]{1,0:T(8,128)S(1)} %shard_map.269.refs_2_), channel_id=1, source_target_pairs={{0,2},{1,3},{2,0},{3,1},{4,6},{5,7},{6,4},{7,5},{8,10},{9,11},{10,... | collective-permute-start | bytes 3145736 | tf_op jit(solution)/shard_map/ppermute | solution.py:710
  325.7 39.2 %collective-permute-start.34 = (f32[512,768]{1,0:T(8,128)S(1)}, f32[512,768]{1,0:T(8,128)S(1)}, u32[]{:S(2)}, u32[]{:S(2)}) collective-permute-start(f32[512,768]{1,0:T(8,128)S(1)} %shard_map.272.second), channel_id=1, source_target_pairs={{8,0},{12,4},{16,24},{20,28},{9,1},{13,5},{17,25},{21,29},{10,2},{... | collective-permute-start | bytes 4718600 | tf_op jit(solution)/shard_map/ppermute | solution.py:710
  327.0 29.2 %collective-permute-start.33 = (f32[136,1024]{1,0:T(8,128)S(1)}, f32[136,1024]{1,0:T(8,128)S(1)}, u32[]{:S(2)}, u32[]{:S(2)}) collective-permute-start(f32[136,1024]{1,0:T(8,128)S(1)} %shard_map.271.first), channel_id=1, source_target_pairs={{8,16},{12,20},{16,8},{20,12},{9,17},{13,21},{17,9},{21,13},{10,18... | collective-permute-start | bytes 1671176 | tf_op jit(solution)/shard_map/ppermute | solution.py:710
  (84 other events, 616.2 us)

commit v6 on v5

--- a/solution.py
+++ b/solution.py
@@ -865,6 +865,8 @@
             return attend_back(angles, kept, d_attended, begin, group, lanes)
 
         back.append(run(step, angles, d_attended, *kept))
+    for part in result:
+        part.on()
     down.on()
     up = chain(up)
     *scaled, sums_attn, qkv_bias, branch_sum = run(
@@ -877,15 +879,18 @@
         w_qkv,
         attn_gain[None, :],
     )
-    for part in result:
-        part.on()
-    small = chain(small_steps(jnp.concatenate([sums_attn, sums_mlp], axis=0), tensor_size))
     core_qkv = grads(1, attn_low, *back, wide=wide)
-    small.on()
     for part in result:
         part.on()
     grad_out = run(inner_rows, attended, cotangent)
     qkv = lines(core_qkv)[0]
+    down.on()
+    up.on()
+    qkv = chain(qkv)
+    for part in result:
+        part.on()
+    small = chain(small_steps(jnp.concatenate([sums_attn, sums_mlp], axis=0), tensor_size))
+    small.on()
     stats = small.end()
 
     sizes = (width,) * 4 + (w_qkv.shape[1], w_up.shape[1], width)
@@ -909,18 +914,13 @@
 
         return finish
 
-    for part in result:
-        part.on()
+    out = lines(core_out)[0]
+    spots = scalars(mine[0], 1 - mine[0], 2 + mine[1], 3 - mine[1])
+    ended = [part.end() for part in result]
     d_tokens = [
         chain(tensor_steps(scaled[p], scaled[2 + p], tensor_size, orders[p], back_end(p)))
         for p in range(2)
     ]
-    out = lines(core_out)[0]
-    down.on()
-    up.on()
-    qkv = chain(qkv)
-    spots = scalars(mine[0], 1 - mine[0], 2 + mine[1], 3 - mine[1])
-    ended = [part.end() for part in result]
     for part in d_tokens:
         part.on()
     result = run(collect, spots, [*ended[0], *ended[1]], tokens, b_branch[None, :])

time: 392 us -> 366 us (0.934)
  Pallas kernels: 143 us -> 125 us
  local copies, waits for them, and re-layouts: 46 us -> 36.4 us
  waiting for transfers between devices: 129 us -> 137 us
  starting transfers between devices: 59.6 us -> 54 us
    unnamed x144 -> x116, local copies, waits for them, and re-layouts: 41.5 us -> 31.9 us
    ppermute x38, waiting for transfers between devices: 129 us -> 137 us  [_go(): self.held = lax.ppermute(array, axis, pairs)]
    ppermute x38, starting transfers between devices: 59.6 us -> 54 us  [_go(): self.held = lax.ppermute(array, axis, pairs)]
    pallas_call x4, Pallas kernels: 6.34 us -> 2.41 us  [add_split(): pl.pallas_call(add_split_kernel, grid_spec=pltpu.PrefetchScalarGridSpec(n...]
    pallas_call x10, Pallas kernels: 22.7 us -> 18.8 us  [add(): pl.pallas_call(add_kernel, grid=(steps,), in_specs=[spec] * 2, out_specs=...]
  transfers between devices with their start and end apart: 38 -> 38, of which waited for: 18 -> 20; matrix products, arithmetic and copies ran while one was open for 2% -> 2% of each run, Pallas kernels for 27% -> 26%
where the time goes in v6:
time: 366 us; the launch traced here: 360 us
  waiting for transfers between devices  137 us (37%)
  Pallas kernels  125 us (34%)
  starting transfers between devices  54 us (15%)
  local copies, waits for them, and re-layouts  36.4 us (10%)
  other arithmetic  4.72 us (1%)
    ppermute x38, waiting for transfers between devices, _go(): self.held = lax.ppermute(array, axis, pairs)  137 us
    ppermute x38, starting transfers between devices, _go(): self.held = lax.ppermute(array, axis, pairs)  54 us
    unnamed x116, local copies, waits for them, and re-layouts  31.9 us
    pallas_call x10, Pallas kernels, add(): pl.pallas_call(add_kernel, grid=(steps,), in_specs=[spec] * 2, out_specs=...  18.8 us
    pallas_call x5, Pallas kernels, collect(): pl.pallas_call(functools.partial(collect_kernel, count), grid_spec=pltpu....  17.6 us
    pallas_call x2, Pallas kernels, attend_back(): pl.pallas_call(functools.partial(attend_back_kernel, begin, heads), out_s...  14.4 us
    pallas_call x3, Pallas kernels, gradient(): pl.pallas_call(functools.partial(gradient_kernel, wide), grid_spec=pltpu....  14 us
    pallas_call x1, Pallas kernels, attend(): pl.pallas_call(functools.partial(attend_kernel, heads), out_shape=(shape(...  12.7 us
  transfers between devices with their start and end apart: 38, of which 20 were waited for; matrix products, arithmetic and copies ran while one was open for 2% of the time, Pallas kernels for 26%

profile of v6, /device:TPU:0, one launch (start us, length us, event | category | flops | bytes accessed | tf_op | source)
XLA Modules:
  0.0 360.4 jit_solution(17247016264220723975)
XLA Ops:
  14.7 10.5 %shard_map.237 = (bf16[1024,1024]{1,0:T(8,128)(2,1)S(1)}, bf16[1024,1024]{1,0:T(8,128)(2,1)S(1)}, f32[1024,768]{1,0:T(8,128)}, bf16[1024,256]{1,0:T(8,128)(2,1)S...) custom-call(bf16[1024,1024]{1,0:T(8,128)(2,1)S(1)} %copy-done.2, bf16[1024,1024]{1,0:T(8,128)(2,1)S(1)} %copy-done, ...), custom_call_target="tpu_custom_call" | custom-call | tf_op jit(solution)/shard_map/pallas_call | solution.py:297
  37.0 8.3 %shard_map.239 = (bf16[1024,1024]{1,0:T(8,128)(2,1)S(1)}, f32[1024,1024]{1,0:T(8,128)}, f32[2,1024]{1,0:T(2,128)S(1)}, f32[1,1024]{1,0:T(1,128)S(1)}) custom-call(bf16[1024,1024]{1,0:T(8,128)(2,1)S(1)} %copy-done.3, bf16[1024,1024]{1,0:T(8,128)(2,1)S(1)} %copy-done.1, f32[1024,1024]{1,0:T(8,128)} %get-tuple-element.365.slope, ...), custom_call_target="tpu_custom_call" | custom-call | tf_op jit(solution)/shard_map/pallas_call | solution.py:337
  49.8 5.1 %shard_map.241 = (f32[512,1024]{1,0:T(8,128)}, f32[512,1024]{1,0:T(8,128)S(1)}) custom-call(s32[4]{0:T(128)S(1)} %and_select_fusion.tiles, bf16[1024,1024]{1,0:T(8,128)(2,1)S(1)} %copy-done.24, bf16[1024,1024]{1,0:T(8,128)(2,1)S(1)} %get-tuple-element.382.refs_0_), custom_call_target="tpu_custom_call" | custom-call | tf_op jit(solution)/shard_map/pallas_call | solution.py:469
  56.4 6.4 %collective-permute-start.4 = (f32[512,1024]{1,0:T(8,128)}, f32[512,1024]{1,0:T(8,128)}, u32[]{:S(2)}, u32[]{:S(2)}) collective-permute-start(f32[512,1024]{1,0:T(8,128)} %shard_map.240.first), channel_id=1, source_target_pairs={{0,8},{4,12},{24,16},{28,20},{1,9},{5,13},{25,17},{29,21},{2,10},{... | collective-permute-start | bytes 6291464 | tf_op jit(solution)/shard_map/ppermute | solution.py:710
  65.0 12.7 %shard_map.242 = (bf16[1024,256]{1,0:T(8,128)(2,1)S(1)}, f32[1024,128]{1,0:T(8,128)S(1)}, bf16[4,1024,64]{2,1,0:T(8,128)(2,1)S(1)}, bf16[4,1024,64]{2,1,0:T(8,128)(2,1)S(1)}, bf16[4,1024,64]{2,1,0:T(8,128)(2,1)S(1)}) custom-call(f32[24,1024]{1,0:T(8,128)S(1)} %pad_maximum_fusion.1.angles, f32[1024,768]{1,0:T(8,128)S(1)} %copy-done.17), custom_call_target="tpu_custom_call" | custom-call | tf_op jit(solution)/shard_map/pallas_call | solution.py:197
  79.3 4.6 %shard_map.243 = (f32[256,1024]{1,0:T(8,128)S(1)}, f32[256,1024]{1,0:T(8,128)S(1)}, f32[256,1024]{1,0:T(8,128)S(1)}, f32[256,1024]{1,0:T(8,128)S(1)}) custom-call(s32[4]{0:T(128)S(1)} %get-tuple-element.458.tiles, bf16[1024,256]{1,0:T(8,128)(2,1)S(1)} %get-tuple-element.493.attended, bf16[1024,1024]{1,0:T(8,128)(2,1)S(1)} %copy-done.10, ...), custom_call_target="tpu_custom_call" | custom-call | tf_op jit(solution)/shard_map/pallas_call | solution.py:368
  87.0 7.1 %shard_map.244.refs_0_ = bf16[1024,384]{1,0:T(8,128)(2,1)S(1)} custom-call(f32[24,1024]{1,0:T(8,128)S(1)} %pad_maximum_fusion.1.angles, bf16[4,1024,64]{2,1,0:T(8,128)(2,1)S(1)} %get-tuple-element.429.q_s, bf16[4,1024,64]{2,1,0:T(8,128)(2,1)S(1)} %get-tuple-element.430.k_s, bf16[4,1024,64]{2,1,0:T(8,128)(2,1)S(1)} %get-tuple-element.431.v_s, ...), custom_call_target="tpu_custom_call" | custom-call | tf_op jit(solution)/shard_map/pallas_call | solution.py:215
  94.1 7.3 %shard_map.245.refs_1_ = bf16[1024,384]{1,0:T(8,128)(2,1)S(1)} custom-call(f32[24,1024]{1,0:T(8,128)S(1)} %pad_maximum_fusion.1.angles, bf16[4,1024,64]{2,1,0:T(8,128)(2,1)S(1)} %get-tuple-element.429.q_s, bf16[4,1024,64]{2,1,0:T(8,128)(2,1)S(1)} %get-tuple-element.430.k_s, bf16[4,1024,64]{2,1,0:T(8,128)(2,1)S(1)} %get-tuple-element.431.v_s, ...), custom_call_target="tpu_custom_call" | custom-call | tf_op jit(solution)/shard_map/pallas_call | solution.py:215
  101.4 7.3 %collective-permute-done.2.second = f32[256,1024]{1,0:T(8,128)S(1)} collective-permute-done((f32[256,1024]{1,0:T(8,128)S(1)}, f32[256,1024]{1,0:T(8,128)S(1)}, u32[]{:S(2)}, u32[]{:S(2)}) %collective-permute-start.2) | collective-permute-done | bytes 1048608 | tf_op jit(solution)/shard_map/ppermute | solution.py:710
  122.5 6.2 %shard_map.250 = (f32[256,1024]{1,0:T(8,128)S(1)}, f32[256,1024]{1,0:T(8,128)S(1)}, f32[256,1024]{1,0:T(8,128)S(1)}, f32[256,1024]{1,0:T(8,128)S(1)}, f32[2,1024...) custom-call(s32[4]{0:T(128)S(1)} %get-tuple-element.458.tiles, ...), custom_call_target="tpu_custom_call" | custom-call | tf_op jit(solution)/shard_map/pallas_call | solution.py:424
  129.8 4.9 %shard_map.251 = (f32[512,768]{1,0:T(8,128)S(1)}, f32[512,768]{1,0:T(8,128)S(1)}) custom-call(s32[4]{0:T(128)S(1)} %and_select_fusion.tiles, bf16[1024,1024]{1,0:T(8,128)(2,1)S(1)} %copy-done.22, bf16[1024,384]{1,0:T(8,128)(2,1)S(1)} %shard_map.244.refs_0_, bf16[1024,384]{1,0:T(8,128)(2,1)S(1)} %shard_map.245.refs_1_), custom_call_target="tpu_custom_call" | custom-call | tf_op jit(solution)/shard_map/pallas_call | solution.py:469
  137.7 11.4 %collective-permute-done.5.second = f32[128,1024]{1,0:T(8,128)S(1)} collective-permute-done((f32[128,1024]{1,0:T(8,128)S(1)}, f32[128,1024]{1,0:T(8,128)S(1)}, u32[]{:S(2)}, u32[]{:S(2)}) %collective-permute-start.5) | collective-permute-done | bytes 524320 | tf_op jit(solution)/shard_map/ppermute | solution.py:710
  159.1 4.4 %collective-permute-done.9.second = f32[512,1024]{1,0:T(8,128)} collective-permute-done((f32[512,1024]{1,0:T(8,128)S(1)}, f32[512,1024]{1,0:T(8,128)}, u32[]{:S(2)}, u32[]{:S(2)}) %collective-permute-start.9) | collective-permute-done | bytes 2097184 | tf_op jit(solution)/shard_map/ppermute | solution.py:710
  180.9 15.3 %collective-permute-done.15.refs_1_ = f32[256,1024]{1,0:T(8,128)} collective-permute-done((f32[256,1024]{1,0:T(8,128)S(1)}, f32[256,1024]{1,0:T(8,128)}, u32[]{:S(2)}, u32[]{:S(2)}) %collective-permute-start.15) | collective-permute-done | bytes 1048608 | tf_op jit(solution)/shard_map/ppermute | solution.py:710
  201.6 16.4 %collective-permute-done.17.second = f32[256,1024]{1,0:T(8,128)S(1)} collective-permute-done((f32[256,1024]{1,0:T(8,128)S(1)}, f32[256,1024]{1,0:T(8,128)S(1)}, u32[]{:S(2)}, u32[]{:S(2)}) %collective-permute-start.17) | collective-permute-done | bytes 1048608 | tf_op jit(solution)/shard_map/ppermute | solution.py:710
  224.9 5.7 %collective-permute-start.23 = (f32[512,768]{1,0:T(8,128)}, f32[512,768]{1,0:T(8,128)}, u32[]{:S(2)}, u32[]{:S(2)}) collective-permute-start(f32[512,768]{1,0:T(8,128)} %shard_map.256.first), channel_id=1, source_target_pairs={{0,8},{4,12},{24,16},{28,20},{1,9},{5,13},{25,17},{29,21},{2,10},{... | collective-permute-start | bytes 4718600 | tf_op jit(solution)/shard_map/ppermute | solution.py:710
  231.8 5.4 %shard_map.261 = bf16[1024,1024]{1,0:T(8,128)(2,1)} custom-call(s32[4]{0:T(128)S(1)} %get-tuple-element.627.order, f32[256,1024]{1,0:T(8,128)S(1)} %shard_map.257.refs_0_, f32[256,1024]{1,0:T(8,128)} %collective-permute-done.15.refs_1_, f32[256,1024]{1,0:T(8,128)S(1)} %copy-done.16, f32[256,1024]{1,0:T(8,128)} %collective-permute-done.16.refs_3_, ...), custom_call_target="tpu_custom_call" | custom-call | tf_op jit(solution)/shard_map/pallas_call | solution.py:665
  247.8 9.1 %collective-permute-done.23.second = f32[512,768]{1,0:T(8,128)} collective-permute-done((f32[512,768]{1,0:T(8,128)}, f32[512,768]{1,0:T(8,128)}, u32[]{:S(2)}, u32[]{:S(2)}) %collective-permute-start.23) | collective-permute-done | bytes 1572896 | tf_op jit(solution)/shard_map/ppermute | solution.py:710
  261.4 6.0 %collective-permute-start.27 = (f32[136,1024]{1,0:T(8,128)S(1)}, f32[136,1024]{1,0:T(8,128)S(1)}, u32[]{:S(2)}, u32[]{:S(2)}) collective-permute-start(f32[136,1024]{1,0:T(8,128)S(1)} %shard_map.267.first), channel_id=1, source_target_pairs={{0,8},{4,12},{24,16},{28,20},{1,9},{5,13},{25,17},{29,21},{2,10},{... | collective-permute-start | bytes 1671176 | tf_op jit(solution)/shard_map/ppermute | solution.py:710
  269.3 7.3 %collective-permute-done.25.other = f32[128,1024]{1,0:T(8,128)S(1)} collective-permute-done((f32[128,1024]{1,0:T(8,128)S(1)}, f32[128,1024]{1,0:T(8,128)S(1)}, u32[]{:S(2)}, u32[]{:S(2)}) %collective-permute-start.25) | collective-permute-done | bytes 524320 | tf_op jit(solution)/shard_map/ppermute | solution.py:710
  283.3 13.1 %collective-permute-done.29.first = f32[512,1024]{1,0:T(8,128)S(1)} collective-permute-done((f32[512,1024]{1,0:T(8,128)S(1)}, f32[512,1024]{1,0:T(8,128)S(1)}, u32[]{:S(2)}, u32[]{:S(2)}) %collective-permute-start.29) | collective-permute-done | bytes 2097184 | tf_op jit(solution)/shard_map/ppermute | solution.py:710
  303.0 21.7 %collective-permute-done.30.refs_1_ = f32[256,1024]{1,0:T(8,128)S(1)} collective-permute-done((f32[256,1024]{1,0:T(8,128)S(1)}, f32[256,1024]{1,0:T(8,128)S(1)}, u32[]{:S(2)}, u32[]{:S(2)}) %collective-permute-start.30) | collective-permute-done | bytes 1048608 | tf_op jit(solution)/shard_map/ppermute | solution.py:710
  333.3 6.9 %collective-permute-done.34.first = f32[512,768]{1,0:T(8,128)S(1)} collective-permute-done((f32[512,768]{1,0:T(8,128)S(1)}, f32[512,768]{1,0:T(8,128)S(1)}, u32[]{:S(2)}, u32[]{:S(2)}) %collective-permute-start.34) | collective-permute-done | bytes 1572896 | tf_op jit(solution)/shard_map/ppermute | solution.py:710
  340.4 10.9 %collective-permute-done.35.first = f32[136,1024]{1,0:T(8,128)S(1)} collective-permute-done((f32[136,1024]{1,0:T(8,128)S(1)}, f32[136,1024]{1,0:T(8,128)S(1)}, u32[]{:S(2)}, u32[]{:S(2)}) %collective-permute-start.35) | collective-permute-done | bytes 557088 | tf_op jit(solution)/shard_map/ppermute | solution.py:710
  (236 shorter events, 144.8 us)
Async XLA Ops:
  56.3 30.7 %collective-permute-start.1 = (f32[512,1024]{1,0:T(8,128)}, f32[512,1024]{1,0:T(8,128)}, u32[]{:S(2)}, u32[]{:S(2)}) collective-permute-start(f32[512,1024]{1,0:T(8,128)} %get-tuple-element.413), channel_id=1, source_target_pairs={{0,4},{4,0},{8,12},{12,8},{16,20},{20,16},{24,28},{28,24},{1,5},{5... | collective-permute-start | bytes 6291464 | tf_op jit(solution)/shard_map/ppermute | solution.py:710
  56.4 54.6 %collective-permute-start.4 = (f32[512,1024]{1,0:T(8,128)}, f32[512,1024]{1,0:T(8,128)}, u32[]{:S(2)}, u32[]{:S(2)}) collective-permute-start(f32[512,1024]{1,0:T(8,128)} %shard_map.240.first), channel_id=1, source_target_pairs={{0,8},{4,12},{24,16},{28,20},{1,9},{5,13},{25,17},{29,21},{2,10},{... | collective-permute-start | bytes 6291464 | tf_op jit(solution)/shard_map/ppermute | solution.py:710
  83.9 24.9 %collective-permute-start.2 = (f32[256,1024]{1,0:T(8,128)S(1)}, f32[256,1024]{1,0:T(8,128)S(1)}, u32[]{:S(2)}, u32[]{:S(2)}) collective-permute-start(f32[256,1024]{1,0:T(8,128)S(1)} %get-tuple-element.436), channel_id=1, source_target_pairs={{0,1},{1,0},{2,3},{3,2},{4,5},{5,4},{6,7},{7,6},{8,9},{9,8},{10,11... | collective-permute-start | bytes 3145736 | tf_op jit(solution)/shard_map/ppermute | solution.py:710
  85.5 24.5 %collective-permute-start.3 = (f32[256,1024]{1,0:T(8,128)S(1)}, f32[256,1024]{1,0:T(8,128)S(1)}, u32[]{:S(2)}, u32[]{:S(2)}) collective-permute-start(f32[256,1024]{1,0:T(8,128)S(1)} %get-tuple-element.442), channel_id=1, source_target_pairs={{0,2},{1,3},{2,0},{3,1},{4,6},{5,7},{6,4},{7,5},{8,10},{9,11},{10,... | collective-permute-start | bytes 3145736 | tf_op jit(solution)/shard_map/ppermute | solution.py:710
  114.1 41.2 %collective-permute-start.8 = (f32[512,1024]{1,0:T(8,128)S(1)}, f32[512,1024]{1,0:T(8,128)}, u32[]{:S(2)}, u32[]{:S(2)}) collective-permute-start(f32[512,1024]{1,0:T(8,128)S(1)} %shard_map.248.first), channel_id=1, source_target_pairs={{8,16},{12,20},{16,8},{20,12},{9,17},{13,21},{17,9},{21,13},{10,18... | collective-permute-start | bytes 6291464 | tf_op jit(solution)/shard_map/ppermute | solution.py:710
  118.0 45.5 %collective-permute-start.9 = (f32[512,1024]{1,0:T(8,128)S(1)}, f32[512,1024]{1,0:T(8,128)}, u32[]{:S(2)}, u32[]{:S(2)}) collective-permute-start(f32[512,1024]{1,0:T(8,128)S(1)} %shard_map.249.first), channel_id=1, source_target_pairs={{0,8},{4,12},{24,16},{28,20},{1,9},{5,13},{25,17},{29,21},{2,10},{... | collective-permute-start | bytes 6291464 | tf_op jit(solution)/shard_map/ppermute | solution.py:710
  134.7 19.3 %collective-permute-start.7 = (f32[512,768]{1,0:T(8,128)S(1)}, f32[512,768]{1,0:T(8,128)S(1)}, u32[]{:S(2)}, u32[]{:S(2)}) collective-permute-start(f32[512,768]{1,0:T(8,128)S(1)} %get-tuple-element.496), channel_id=1, source_target_pairs={{0,4},{4,0},{8,12},{12,8},{16,20},{20,16},{24,28},{28,24},{1,5},{5... | collective-permute-start | bytes 4718600 | tf_op jit(solution)/shard_map/ppermute | solution.py:710
  174.1 22.0 %collective-permute-start.15 = (f32[256,1024]{1,0:T(8,128)S(1)}, f32[256,1024]{1,0:T(8,128)}, u32[]{:S(2)}, u32[]{:S(2)}) collective-permute-start(f32[256,1024]{1,0:T(8,128)S(1)} %shard_map.257.refs_0_), channel_id=1, source_target_pairs={{0,1},{1,0},{2,3},{3,2},{4,5},{5,4},{6,7},{7,6},{8,9},{9,8},{10,11... | collective-permute-start | bytes 3145736 | tf_op jit(solution)/shard_map/ppermute | solution.py:710
  175.7 23.5 %collective-permute-start.16 = (f32[256,1024]{1,0:T(8,128)}, f32[256,1024]{1,0:T(8,128)}, u32[]{:S(2)}, u32[]{:S(2)}) collective-permute-start(f32[256,1024]{1,0:T(8,128)} %copy-done.15), channel_id=1, source_target_pairs={{0,2},{1,3},{2,0},{3,1},{4,6},{5,7},{6,4},{7,5},{8,10},{9,11},{10,... | collective-permute-start | bytes 3145736 | tf_op jit(solution)/shard_map/ppermute | solution.py:710
  178.9 61.4 %collective-permute-start.21 = (f32[512,1024]{1,0:T(8,128)}, f32[512,1024]{1,0:T(8,128)}, u32[]{:S(2)}, u32[]{:S(2)}) collective-permute-start(f32[512,1024]{1,0:T(8,128)} %shard_map.254.second), channel_id=1, source_target_pairs={{8,0},{12,4},{16,24},{20,28},{9,1},{13,5},{17,25},{21,29},{10,2},{... | collective-permute-start | bytes 6291464 | tf_op jit(solution)/shard_map/ppermute | solution.py:710
  199.2 18.8 %collective-permute-start.17 = (f32[256,1024]{1,0:T(8,128)S(1)}, f32[256,1024]{1,0:T(8,128)S(1)}, u32[]{:S(2)}, u32[]{:S(2)}) collective-permute-start(f32[256,1024]{1,0:T(8,128)S(1)} %copy-done.50), channel_id=1, source_target_pairs={{0,1},{1,0},{2,3},{3,2},{4,5},{5,4},{6,7},{7,6},{8,9},{9,8},{10,11... | collective-permute-start | bytes 3145736 | tf_op jit(solution)/shard_map/ppermute | solution.py:710
  199.2 24.0 %collective-permute-start.18 = (f32[256,1024]{1,0:T(8,128)S(1)}, f32[256,1024]{1,0:T(8,128)S(1)}, u32[]{:S(2)}, u32[]{:S(2)}) collective-permute-start(f32[256,1024]{1,0:T(8,128)S(1)} %copy-done.48), channel_id=1, source_target_pairs={{0,2},{1,3},{2,0},{3,1},{4,6},{5,7},{6,4},{7,5},{8,10},{9,11},{10,... | collective-permute-start | bytes 3145736 | tf_op jit(solution)/shard_map/ppermute | solution.py:710
  199.6 43.7 %collective-permute-start.22 = (f32[512,1024]{1,0:T(8,128)}, f32[512,1024]{1,0:T(8,128)}, u32[]{:S(2)}, u32[]{:S(2)}) collective-permute-start(f32[512,1024]{1,0:T(8,128)} %shard_map.255.first), channel_id=1, source_target_pairs={{8,16},{12,20},{16,8},{20,12},{9,17},{13,21},{17,9},{21,13},{10,18... | collective-permute-start | bytes 6291464 | tf_op jit(solution)/shard_map/ppermute | solution.py:710
  224.9 31.9 %collective-permute-start.23 = (f32[512,768]{1,0:T(8,128)}, f32[512,768]{1,0:T(8,128)}, u32[]{:S(2)}, u32[]{:S(2)}) collective-permute-start(f32[512,768]{1,0:T(8,128)} %shard_map.256.first), channel_id=1, source_target_pairs={{0,8},{4,12},{24,16},{28,20},{1,9},{5,13},{25,17},{29,21},{2,10},{... | collective-permute-start | bytes 4718600 | tf_op jit(solution)/shard_map/ppermute | solution.py:710
  243.2 25.8 %collective-permute-start.24 = (f32[512,1024]{1,0:T(8,128)S(1)}, f32[512,1024]{1,0:T(8,128)S(1)}, u32[]{:S(2)}, u32[]{:S(2)}) collective-permute-start(f32[512,1024]{1,0:T(8,128)S(1)} %shard_map.264.refs_0_), channel_id=1, source_target_pairs={{0,4},{4,0},{8,12},{12,8},{16,20},{20,16},{24,28},{28,24},{1,5},{5... | collective-permute-start | bytes 6291464 | tf_op jit(solution)/shard_map/ppermute | solution.py:710
  246.2 50.2 %collective-permute-start.29 = (f32[512,1024]{1,0:T(8,128)S(1)}, f32[512,1024]{1,0:T(8,128)S(1)}, u32[]{:S(2)}, u32[]{:S(2)}) collective-permute-start(f32[512,1024]{1,0:T(8,128)S(1)} %shard_map.265.second), channel_id=1, source_target_pairs={{8,0},{12,4},{16,24},{20,28},{9,1},{13,5},{17,25},{21,29},{10,2},{... | collective-permute-start | bytes 6291464 | tf_op jit(solution)/shard_map/ppermute | solution.py:710
  259.5 21.5 %collective-permute-start.28 = (f32[512,768]{1,0:T(8,128)S(1)}, f32[512,768]{1,0:T(8,128)}, u32[]{:S(2)}, u32[]{:S(2)}) collective-permute-start(f32[512,768]{1,0:T(8,128)S(1)} %shard_map.266.first), channel_id=1, source_target_pairs={{8,16},{12,20},{16,8},{20,12},{9,17},{13,21},{17,9},{21,13},{10,18... | collective-permute-start | bytes 4718600 | tf_op jit(solution)/shard_map/ppermute | solution.py:710
  261.4 19.6 %collective-permute-start.27 = (f32[136,1024]{1,0:T(8,128)S(1)}, f32[136,1024]{1,0:T(8,128)S(1)}, u32[]{:S(2)}, u32[]{:S(2)}) collective-permute-start(f32[136,1024]{1,0:T(8,128)S(1)} %shard_map.267.first), channel_id=1, source_target_pairs={{0,8},{4,12},{24,16},{28,20},{1,9},{5,13},{25,17},{29,21},{2,10},{... | collective-permute-start | bytes 1671176 | tf_op jit(solution)/shard_map/ppermute | solution.py:710
  298.8 30.4 %collective-permute-start.32 = (f32[512,1024]{1,0:T(8,128)S(1)}, f32[512,1024]{1,0:T(8,128)S(1)}, u32[]{:S(2)}, u32[]{:S(2)}) collective-permute-start(f32[512,1024]{1,0:T(8,128)S(1)} %shard_map.273.refs_0_), channel_id=1, source_target_pairs={{0,4},{4,0},{8,12},{12,8},{16,20},{20,16},{24,28},{28,24},{1,5},{5... | collective-permute-start | bytes 6291464 | tf_op jit(solution)/shard_map/ppermute | solution.py:710
  298.9 25.8 %collective-permute-start.30 = (f32[256,1024]{1,0:T(8,128)S(1)}, f32[256,1024]{1,0:T(8,128)S(1)}, u32[]{:S(2)}, u32[]{:S(2)}) collective-permute-start(f32[256,1024]{1,0:T(8,128)S(1)} %shard_map.268.refs_0_), channel_id=1, source_target_pairs={{0,1},{1,0},{2,3},{3,2},{4,5},{5,4},{6,7},{7,6},{8,9},{9,8},{10,11... | collective-permute-start | bytes 3145736 | tf_op jit(solution)/shard_map/ppermute | solution.py:710
  301.0 25.2 %collective-permute-start.31 = (f32[256,1024]{1,0:T(8,128)S(1)}, f32[256,1024]{1,0:T(8,128)S(1)}, u32[]{:S(2)}, u32[]{:S(2)}) collective-permute-start(f32[256,1024]{1,0:T(8,128)S(1)} %shard_map.269.refs_2_), channel_id=1, source_target_pairs={{0,2},{1,3},{2,0},{3,1},{4,6},{5,7},{6,4},{7,5},{8,10},{9,11},{10,... | collective-permute-start | bytes 3145736 | tf_op jit(solution)/shard_map/ppermute | solution.py:710
  301.1 39.1 %collective-permute-start.34 = (f32[512,768]{1,0:T(8,128)S(1)}, f32[512,768]{1,0:T(8,128)S(1)}, u32[]{:S(2)}, u32[]{:S(2)}) collective-permute-start(f32[512,768]{1,0:T(8,128)S(1)} %shard_map.272.second), channel_id=1, source_target_pairs={{8,0},{12,4},{16,24},{20,28},{9,1},{13,5},{17,25},{21,29},{10,2},{... | collective-permute-start | bytes 4718600 | tf_op jit(solution)/shard_map/ppermute | solution.py:710
  302.3 29.6 %collective-permute-start.33 = (f32[136,1024]{1,0:T(8,128)S(1)}, f32[136,1024]{1,0:T(8,128)S(1)}, u32[]{:S(2)}, u32[]{:S(2)}) collective-permute-start(f32[136,1024]{1,0:T(8,128)S(1)} %shard_map.271.first), channel_id=1, source_target_pairs={{8,16},{12,20},{16,8},{20,12},{9,17},{13,21},{17,9},{21,13},{10,18... | collective-permute-start | bytes 1671176 | tf_op jit(solution)/shard_map/ppermute | solution.py:710
  332.0 19.3 %collective-permute-start.35 = (f32[136,1024]{1,0:T(8,128)S(1)}, f32[136,1024]{1,0:T(8,128)S(1)}, u32[]{:S(2)}, u32[]{:S(2)}) collective-permute-start(f32[136,1024]{1,0:T(8,128)S(1)} %shard_map.276.second), channel_id=1, source_target_pairs={{8,0},{12,4},{16,24},{20,28},{9,1},{13,5},{17,25},{21,29},{10,2},{... | collective-permute-start | bytes 1671176 | tf_op jit(solution)/shard_map/ppermute | solution.py:710
  (70 other events, 645.9 us)

commit v7 on v6

--- a/solution.py
+++ b/solution.py
@@ -924,11 +924,11 @@
     for part in d_tokens:
         part.on()
     result = run(collect, spots, [*ended[0], *ended[1]], tokens, b_branch[None, :])
-    for part in d_tokens:
-        part.on()
     for part in (down, up, qkv):
         part.on()
     out = chain(out)
+    for part in d_tokens:
+        part.on()
     down.end()
     for part in d_tokens:
         part.on()

time: 366 us -> 366 us (level)
  waiting for transfers between devices: 137 us -> 119 us
  Pallas kernels: 125 us -> 134 us
  local copies, waits for them, and re-layouts: 36.4 us -> 41.6 us
    ppermute x38, waiting for transfers between devices: 137 us -> 119 us  [_go(): self.held = lax.ppermute(array, axis, pairs)]
    unnamed x116 -> x112, local copies, waits for them, and re-layouts: 31.9 us -> 37.1 us
  transfers between devices with their start and end apart: 38 -> 38, of which waited for: 20 -> 16; matrix products, arithmetic and copies ran while one was open for 2% -> 2% of each run, Pallas kernels for 26% -> 28%
where the time goes in v7:
time: 366 us; the launch traced here: 360 us
  Pallas kernels  134 us (37%)
  waiting for transfers between devices  119 us (33%)
  starting transfers between devices  56.7 us (15%)
  local copies, waits for them, and re-layouts  41.6 us (11%)
  other arithmetic  4.69 us (1%)
    ppermute x38, waiting for transfers between devices, _go(): self.held = lax.ppermute(array, axis, pairs)  119 us
    ppermute x38, starting transfers between devices, _go(): self.held = lax.ppermute(array, axis, pairs)  56.7 us
    unnamed x112, local copies, waits for them, and re-layouts  37.1 us
    pallas_call x10, Pallas kernels, add(): pl.pallas_call(add_kernel, grid=(steps,), in_specs=[spec] * 2, out_specs=...  20.2 us
    pallas_call x5, Pallas kernels, collect(): pl.pallas_call(functools.partial(collect_kernel, count), grid_spec=pltpu....  20.1 us
    pallas_call x2, Pallas kernels, attend_back(): pl.pallas_call(functools.partial(attend_back_kernel, begin, heads), out_s...  14.8 us
    pallas_call x3, Pallas kernels, gradient(): pl.pallas_call(functools.partial(gradient_kernel, wide), grid_spec=pltpu....  14 us
    pallas_call x1, Pallas kernels, attend(): pl.pallas_call(functools.partial(attend_kernel, heads), out_shape=(shape(...  12.7 us
  transfers between devices with their start and end apart: 38, of which 16 were waited for; matrix products, arithmetic and copies ran while one was open for 2% of the time, Pallas kernels for 28%

profile of v7, /device:TPU:0, one launch (start us, length us, event | category | flops | bytes accessed | tf_op | source)
XLA Modules:
  0.0 359.5 jit_solution(2564471096759340892)
XLA Ops:
  14.7 10.6 %shard_map.237 = (bf16[1024,1024]{1,0:T(8,128)(2,1)S(1)}, bf16[1024,1024]{1,0:T(8,128)(2,1)S(1)}, f32[1024,768]{1,0:T(8,128)}, bf16[1024,256]{1,0:T(8,128)(2,1)S...) custom-call(bf16[1024,1024]{1,0:T(8,128)(2,1)S(1)} %copy-done.2, bf16[1024,1024]{1,0:T(8,128)(2,1)S(1)} %copy-done, ...), custom_call_target="tpu_custom_call" | custom-call | tf_op jit(solution)/shard_map/pallas_call | solution.py:297
  37.1 8.4 %shard_map.239 = (bf16[1024,1024]{1,0:T(8,128)(2,1)S(1)}, f32[1024,1024]{1,0:T(8,128)}, f32[2,1024]{1,0:T(2,128)S(1)}, f32[1,1024]{1,0:T(1,128)S(1)}) custom-call(bf16[1024,1024]{1,0:T(8,128)(2,1)S(1)} %copy-done.3, bf16[1024,1024]{1,0:T(8,128)(2,1)S(1)} %copy-done.1, f32[1024,1024]{1,0:T(8,128)} %get-tuple-element.365.slope, ...), custom_call_target="tpu_custom_call" | custom-call | tf_op jit(solution)/shard_map/pallas_call | solution.py:337
  50.0 5.1 %shard_map.241 = (f32[512,1024]{1,0:T(8,128)}, f32[512,1024]{1,0:T(8,128)S(1)}) custom-call(s32[4]{0:T(128)S(1)} %and_select_fusion.tiles, bf16[1024,1024]{1,0:T(8,128)(2,1)S(1)} %copy-done.24, bf16[1024,1024]{1,0:T(8,128)(2,1)S(1)} %get-tuple-element.382.refs_0_), custom_call_target="tpu_custom_call" | custom-call | tf_op jit(solution)/shard_map/pallas_call | solution.py:469
  56.6 6.5 %collective-permute-start.4 = (f32[512,1024]{1,0:T(8,128)}, f32[512,1024]{1,0:T(8,128)}, u32[]{:S(2)}, u32[]{:S(2)}) collective-permute-start(f32[512,1024]{1,0:T(8,128)} %shard_map.240.first), channel_id=1, source_target_pairs={{0,8},{4,12},{24,16},{28,20},{1,9},{5,13},{25,17},{29,21},{2,10},{... | collective-permute-start | bytes 6291464 | tf_op jit(solution)/shard_map/ppermute | solution.py:710
  65.2 12.7 %shard_map.242 = (bf16[1024,256]{1,0:T(8,128)(2,1)S(1)}, f32[1024,128]{1,0:T(8,128)S(1)}, bf16[4,1024,64]{2,1,0:T(8,128)(2,1)S(1)}, bf16[4,1024,64]{2,1,0:T(8,128)(2,1)S(1)}, bf16[4,1024,64]{2,1,0:T(8,128)(2,1)S(1)}) custom-call(f32[24,1024]{1,0:T(8,128)S(1)} %pad_maximum_fusion.1.angles, f32[1024,768]{1,0:T(8,128)S(1)} %copy-done.17), custom_call_target="tpu_custom_call" | custom-call | tf_op jit(solution)/shard_map/pallas_call | solution.py:197
  79.6 4.5 %shard_map.243 = (f32[256,1024]{1,0:T(8,128)S(1)}, f32[256,1024]{1,0:T(8,128)S(1)}, f32[256,1024]{1,0:T(8,128)S(1)}, f32[256,1024]{1,0:T(8,128)S(1)}) custom-call(s32[4]{0:T(128)S(1)} %get-tuple-element.458.tiles, bf16[1024,256]{1,0:T(8,128)(2,1)S(1)} %get-tuple-element.493.attended, bf16[1024,1024]{1,0:T(8,128)(2,1)S(1)} %copy-done.10, ...), custom_call_target="tpu_custom_call" | custom-call | tf_op jit(solution)/shard_map/pallas_call | solution.py:368
  87.2 7.2 %shard_map.244.refs_0_ = bf16[1024,384]{1,0:T(8,128)(2,1)S(1)} custom-call(f32[24,1024]{1,0:T(8,128)S(1)} %pad_maximum_fusion.1.angles, bf16[4,1024,64]{2,1,0:T(8,128)(2,1)S(1)} %get-tuple-element.429.q_s, bf16[4,1024,64]{2,1,0:T(8,128)(2,1)S(1)} %get-tuple-element.430.k_s, bf16[4,1024,64]{2,1,0:T(8,128)(2,1)S(1)} %get-tuple-element.431.v_s, ...), custom_call_target="tpu_custom_call" | custom-call | tf_op jit(solution)/shard_map/pallas_call | solution.py:215
  94.4 7.6 %shard_map.245.refs_1_ = bf16[1024,384]{1,0:T(8,128)(2,1)S(1)} custom-call(f32[24,1024]{1,0:T(8,128)S(1)} %pad_maximum_fusion.1.angles, bf16[4,1024,64]{2,1,0:T(8,128)(2,1)S(1)} %get-tuple-element.429.q_s, bf16[4,1024,64]{2,1,0:T(8,128)(2,1)S(1)} %get-tuple-element.430.k_s, bf16[4,1024,64]{2,1,0:T(8,128)(2,1)S(1)} %get-tuple-element.431.v_s, ...), custom_call_target="tpu_custom_call" | custom-call | tf_op jit(solution)/shard_map/pallas_call | solution.py:215
  102.0 7.0 %collective-permute-done.2.second = f32[256,1024]{1,0:T(8,128)S(1)} collective-permute-done((f32[256,1024]{1,0:T(8,128)S(1)}, f32[256,1024]{1,0:T(8,128)S(1)}, u32[]{:S(2)}, u32[]{:S(2)}) %collective-permute-start.2) | collective-permute-done | bytes 1048608 | tf_op jit(solution)/shard_map/ppermute | solution.py:710
  121.6 7.5 %shard_map.250 = (f32[256,1024]{1,0:T(8,128)}, f32[256,1024]{1,0:T(8,128)}, f32[256,1024]{1,0:T(8,128)S(1)}, f32[256,1024]{1,0:T(8,128)S(1)}, f32[2,1024]{1,0:T(...) custom-call(s32[4]{0:T(128)S(1)} %get-tuple-element.458.tiles, bf16[1024,384]{1,0:T(8,128)(2,1)S(1)} %shard_map.244.refs_0_, ...), custom_call_target="tpu_custom_call" | custom-call | tf_op jit(solution)/shard_map/pallas_call | solution.py:424
  131.0 4.9 %shard_map.251 = (f32[512,768]{1,0:T(8,128)S(1)}, f32[512,768]{1,0:T(8,128)S(1)}) custom-call(s32[4]{0:T(128)S(1)} %and_select_fusion.tiles, bf16[1024,1024]{1,0:T(8,128)(2,1)S(1)} %copy-done.22, bf16[1024,384]{1,0:T(8,128)(2,1)S(1)} %shard_map.244.refs_0_, bf16[1024,384]{1,0:T(8,128)(2,1)S(1)} %shard_map.245.refs_1_), custom_call_target="tpu_custom_call" | custom-call | tf_op jit(solution)/shard_map/pallas_call | solution.py:469
  138.9 11.4 %collective-permute-done.5.second = f32[128,1024]{1,0:T(8,128)S(1)} collective-permute-done((f32[128,1024]{1,0:T(8,128)S(1)}, f32[128,1024]{1,0:T(8,128)S(1)}, u32[]{:S(2)}, u32[]{:S(2)}) %collective-permute-start.5) | collective-permute-done | bytes 524320 | tf_op jit(solution)/shard_map/ppermute | solution.py:710
  183.1 13.3 %collective-permute-done.15.refs_1_ = f32[256,1024]{1,0:T(8,128)} collective-permute-done((f32[256,1024]{1,0:T(8,128)S(1)}, f32[256,1024]{1,0:T(8,128)}, u32[]{:S(2)}, u32[]{:S(2)}) %collective-permute-start.15) | collective-permute-done | bytes 1048608 | tf_op jit(solution)/shard_map/ppermute | solution.py:710
  199.9 5.7 %collective-permute-start.21 = (f32[512,768]{1,0:T(8,128)}, f32[512,768]{1,0:T(8,128)}, u32[]{:S(2)}, u32[]{:S(2)}) collective-permute-start(f32[512,768]{1,0:T(8,128)} %shard_map.256.first), channel_id=1, source_target_pairs={{0,8},{4,12},{24,16},{28,20},{1,9},{5,13},{25,17},{29,21},{2,10},{... | collective-permute-start | bytes 4718600 | tf_op jit(solution)/shard_map/ppermute | solution.py:710
  205.7 13.3 %collective-permute-done.17.second = f32[256,1024]{1,0:T(8,128)} collective-permute-done((f32[256,1024]{1,0:T(8,128)}, f32[256,1024]{1,0:T(8,128)}, u32[]{:S(2)}, u32[]{:S(2)}) %collective-permute-start.17) | collective-permute-done | bytes 1048608 | tf_op jit(solution)/shard_map/ppermute | solution.py:710
  224.5 5.2 %shard_map.261 = bf16[1024,1024]{1,0:T(8,128)(2,1)} custom-call(s32[4]{0:T(128)S(1)} %get-tuple-element.627.order, f32[256,1024]{1,0:T(8,128)S(1)} %shard_map.257.refs_0_, f32[256,1024]{1,0:T(8,128)} %collective-permute-done.15.refs_1_, f32[256,1024]{1,0:T(8,128)S(1)} %copy-done.16, f32[256,1024]{1,0:T(8,128)} %collective-permute-done.16.refs_3_, ...), custom_call_target="tpu_custom_call" | custom-call | tf_op jit(solution)/shard_map/pallas_call | solution.py:665
  247.3 12.2 %collective-permute-done.22.second = f32[128,1024]{1,0:T(8,128)S(1)} collective-permute-done((f32[128,1024]{1,0:T(8,128)S(1)}, f32[128,1024]{1,0:T(8,128)S(1)}, u32[]{:S(2)}, u32[]{:S(2)}) %collective-permute-start.22) | collective-permute-done | bytes 524320 | tf_op jit(solution)/shard_map/ppermute | solution.py:710
  260.3 7.2 %collective-permute-start.27 = (f32[136,1024]{1,0:T(8,128)S(1)}, f32[136,1024]{1,0:T(8,128)S(1)}, u32[]{:S(2)}, u32[]{:S(2)}) collective-permute-start(f32[136,1024]{1,0:T(8,128)S(1)} %shard_map.265.first), channel_id=1, source_target_pairs={{0,8},{4,12},{24,16},{28,20},{1,9},{5,13},{25,17},{29,21},{2,10},{... | collective-permute-start | bytes 1671176 | tf_op jit(solution)/shard_map/ppermute | solution.py:710
  275.0 9.6 %collective-permute-done.25.other = f32[128,1024]{1,0:T(8,128)S(1)} collective-permute-done((f32[128,1024]{1,0:T(8,128)S(1)}, f32[128,1024]{1,0:T(8,128)S(1)}, u32[]{:S(2)}, u32[]{:S(2)}) %collective-permute-start.25) | collective-permute-done | bytes 524320 | tf_op jit(solution)/shard_map/ppermute | solution.py:710
  286.9 4.9 %shard_map.270 = f32[1024,1024]{1,0:T(8,128)} custom-call(s32[2]{0:T(128)S(1)} %pad_add_fusion.2.order, f32[512,1024]{1,0:T(8,128)} %shard_map.262.refs_0_, f32[512,1024]{1,0:T(8,128)} %collective-permute-done.24.refs_1_), custom_call_target="tpu_custom_call" | custom-call | tf_op jit(solution)/shard_map/pallas_call | solution.py:665
  302.0 21.2 %collective-permute-done.30.refs_1_ = f32[256,1024]{1,0:T(8,128)S(1)} collective-permute-done((f32[256,1024]{1,0:T(8,128)S(1)}, f32[256,1024]{1,0:T(8,128)S(1)}, u32[]{:S(2)}, u32[]{:S(2)}) %collective-permute-start.30) | collective-permute-done | bytes 1048608 | tf_op jit(solution)/shard_map/ppermute | solution.py:710
  331.1 8.0 %collective-permute-done.34.first = f32[512,768]{1,0:T(8,128)S(1)} collective-permute-done((f32[512,768]{1,0:T(8,128)S(1)}, f32[512,768]{1,0:T(8,128)S(1)}, u32[]{:S(2)}, u32[]{:S(2)}) %collective-permute-start.34) | collective-permute-done | bytes 1572896 | tf_op jit(solution)/shard_map/ppermute | solution.py:710
  340.9 9.1 %collective-permute-done.35.first = f32[136,1024]{1,0:T(8,128)S(1)} collective-permute-done((f32[136,1024]{1,0:T(8,128)S(1)}, f32[136,1024]{1,0:T(8,128)S(1)}, u32[]{:S(2)}, u32[]{:S(2)}) %collective-permute-start.35) | collective-permute-done | bytes 557088 | tf_op jit(solution)/shard_map/ppermute | solution.py:710
  355.2 4.2 %shard_map.279 = f32[1024,768]{1,0:T(8,128)} custom-call(s32[2]{0:T(128)S(1)} %pad_add_fusion.2.order, f32[512,768]{1,0:T(8,128)} %shard_map.277.refs_0_, f32[512,768]{1,0:T(8,128)} %collective-permute-done.36.refs_1_), custom_call_target="tpu_custom_call" | custom-call | tf_op jit(solution)/shard_map/pallas_call | solution.py:665
  (232 shorter events, 150.5 us)
Async XLA Ops:
  56.5 30.7 %collective-permute-start.1 = (f32[512,1024]{1,0:T(8,128)}, f32[512,1024]{1,0:T(8,128)}, u32[]{:S(2)}, u32[]{:S(2)}) collective-permute-start(f32[512,1024]{1,0:T(8,128)} %get-tuple-element.413), channel_id=1, source_target_pairs={{0,4},{4,0},{8,12},{12,8},{16,20},{20,16},{24,28},{28,24},{1,5},{5... | collective-permute-start | bytes 6291464 | tf_op jit(solution)/shard_map/ppermute | solution.py:710
  56.6 54.7 %collective-permute-start.4 = (f32[512,1024]{1,0:T(8,128)}, f32[512,1024]{1,0:T(8,128)}, u32[]{:S(2)}, u32[]{:S(2)}) collective-permute-start(f32[512,1024]{1,0:T(8,128)} %shard_map.240.first), channel_id=1, source_target_pairs={{0,8},{4,12},{24,16},{28,20},{1,9},{5,13},{25,17},{29,21},{2,10},{... | collective-permute-start | bytes 6291464 | tf_op jit(solution)/shard_map/ppermute | solution.py:710
  84.1 24.9 %collective-permute-start.2 = (f32[256,1024]{1,0:T(8,128)S(1)}, f32[256,1024]{1,0:T(8,128)S(1)}, u32[]{:S(2)}, u32[]{:S(2)}) collective-permute-start(f32[256,1024]{1,0:T(8,128)S(1)} %get-tuple-element.436), channel_id=1, source_target_pairs={{0,1},{1,0},{2,3},{3,2},{4,5},{5,4},{6,7},{7,6},{8,9},{9,8},{10,11... | collective-permute-start | bytes 3145736 | tf_op jit(solution)/shard_map/ppermute | solution.py:710
  85.7 24.6 %collective-permute-start.3 = (f32[256,1024]{1,0:T(8,128)S(1)}, f32[256,1024]{1,0:T(8,128)S(1)}, u32[]{:S(2)}, u32[]{:S(2)}) collective-permute-start(f32[256,1024]{1,0:T(8,128)S(1)} %get-tuple-element.442), channel_id=1, source_target_pairs={{0,2},{1,3},{2,0},{3,1},{4,6},{5,7},{6,4},{7,5},{8,10},{9,11},{10,... | collective-permute-start | bytes 3145736 | tf_op jit(solution)/shard_map/ppermute | solution.py:710
  114.3 42.2 %collective-permute-start.8 = (f32[512,1024]{1,0:T(8,128)S(1)}, f32[512,1024]{1,0:T(8,128)}, u32[]{:S(2)}, u32[]{:S(2)}) collective-permute-start(f32[512,1024]{1,0:T(8,128)S(1)} %shard_map.248.first), channel_id=1, source_target_pairs={{8,16},{12,20},{16,8},{20,12},{9,17},{13,21},{17,9},{21,13},{10,18... | collective-permute-start | bytes 6291464 | tf_op jit(solution)/shard_map/ppermute | solution.py:710
  118.3 45.9 %collective-permute-start.9 = (f32[512,1024]{1,0:T(8,128)S(1)}, f32[512,1024]{1,0:T(8,128)}, u32[]{:S(2)}, u32[]{:S(2)}) collective-permute-start(f32[512,1024]{1,0:T(8,128)S(1)} %shard_map.249.first), channel_id=1, source_target_pairs={{0,8},{4,12},{24,16},{28,20},{1,9},{5,13},{25,17},{29,21},{2,10},{... | collective-permute-start | bytes 6291464 | tf_op jit(solution)/shard_map/ppermute | solution.py:710
  174.7 21.7 %collective-permute-start.15 = (f32[256,1024]{1,0:T(8,128)S(1)}, f32[256,1024]{1,0:T(8,128)}, u32[]{:S(2)}, u32[]{:S(2)}) collective-permute-start(f32[256,1024]{1,0:T(8,128)S(1)} %shard_map.257.refs_0_), channel_id=1, source_target_pairs={{0,1},{1,0},{2,3},{3,2},{4,5},{5,4},{6,7},{7,6},{8,9},{9,8},{10,11... | collective-permute-start | bytes 3145736 | tf_op jit(solution)/shard_map/ppermute | solution.py:710
  176.2 23.3 %collective-permute-start.16 = (f32[256,1024]{1,0:T(8,128)}, f32[256,1024]{1,0:T(8,128)}, u32[]{:S(2)}, u32[]{:S(2)}) collective-permute-start(f32[256,1024]{1,0:T(8,128)} %copy-done.15), channel_id=1, source_target_pairs={{0,2},{1,3},{2,0},{3,1},{4,6},{5,7},{6,4},{7,5},{8,10},{9,11},{10,... | collective-permute-start | bytes 3145736 | tf_op jit(solution)/shard_map/ppermute | solution.py:710
  176.6 53.1 %collective-permute-start.19 = (f32[512,1024]{1,0:T(8,128)}, f32[512,1024]{1,0:T(8,128)}, u32[]{:S(2)}, u32[]{:S(2)}) collective-permute-start(f32[512,1024]{1,0:T(8,128)} %copy-done.6), channel_id=1, source_target_pairs={{8,0},{12,4},{16,24},{20,28},{9,1},{13,5},{17,25},{21,29},{10,2},{... | collective-permute-start | bytes 6291464 | tf_op jit(solution)/shard_map/ppermute | solution.py:710
  180.3 53.5 %collective-permute-start.20 = (f32[512,1024]{1,0:T(8,128)}, f32[512,1024]{1,0:T(8,128)}, u32[]{:S(2)}, u32[]{:S(2)}) collective-permute-start(f32[512,1024]{1,0:T(8,128)} %shard_map.255.first), channel_id=1, source_target_pairs={{8,16},{12,20},{16,8},{20,12},{9,17},{13,21},{17,9},{21,13},{10,18... | collective-permute-start | bytes 6291464 | tf_op jit(solution)/shard_map/ppermute | solution.py:710
  199.5 19.5 %collective-permute-start.17 = (f32[256,1024]{1,0:T(8,128)}, f32[256,1024]{1,0:T(8,128)}, u32[]{:S(2)}, u32[]{:S(2)}) collective-permute-start(f32[256,1024]{1,0:T(8,128)} %get-tuple-element.546), channel_id=1, source_target_pairs={{0,1},{1,0},{2,3},{3,2},{4,5},{5,4},{6,7},{7,6},{8,9},{9,8},{10,11... | collective-permute-start | bytes 3145736 | tf_op jit(solution)/shard_map/ppermute | solution.py:710
  199.5 22.9 %collective-permute-start.18 = (f32[256,1024]{1,0:T(8,128)}, f32[256,1024]{1,0:T(8,128)}, u32[]{:S(2)}, u32[]{:S(2)}) collective-permute-start(f32[256,1024]{1,0:T(8,128)} %get-tuple-element.552), channel_id=1, source_target_pairs={{0,2},{1,3},{2,0},{3,1},{4,6},{5,7},{6,4},{7,5},{8,10},{9,11},{10,... | collective-permute-start | bytes 3145736 | tf_op jit(solution)/shard_map/ppermute | solution.py:710
  199.9 39.5 %collective-permute-start.21 = (f32[512,768]{1,0:T(8,128)}, f32[512,768]{1,0:T(8,128)}, u32[]{:S(2)}, u32[]{:S(2)}) collective-permute-start(f32[512,768]{1,0:T(8,128)} %shard_map.256.first), channel_id=1, source_target_pairs={{0,8},{4,12},{24,16},{28,20},{1,9},{5,13},{25,17},{29,21},{2,10},{... | collective-permute-start | bytes 4718600 | tf_op jit(solution)/shard_map/ppermute | solution.py:710
  233.8 39.9 %collective-permute-start.24 = (f32[512,1024]{1,0:T(8,128)}, f32[512,1024]{1,0:T(8,128)}, u32[]{:S(2)}, u32[]{:S(2)}) collective-permute-start(f32[512,1024]{1,0:T(8,128)} %shard_map.262.refs_0_), channel_id=1, source_target_pairs={{0,4},{4,0},{8,12},{12,8},{16,20},{20,16},{24,28},{28,24},{1,5},{5... | collective-permute-start | bytes 6291464 | tf_op jit(solution)/shard_map/ppermute | solution.py:710
  238.0 56.5 %collective-permute-start.29 = (f32[512,1024]{1,0:T(8,128)}, f32[512,1024]{1,0:T(8,128)}, u32[]{:S(2)}, u32[]{:S(2)}) collective-permute-start(f32[512,1024]{1,0:T(8,128)} %shard_map.263.second), channel_id=1, source_target_pairs={{8,0},{12,4},{16,24},{20,28},{9,1},{13,5},{17,25},{21,29},{10,2},{... | collective-permute-start | bytes 6291464 | tf_op jit(solution)/shard_map/ppermute | solution.py:710
  243.3 48.6 %collective-permute-start.28 = (f32[512,768]{1,0:T(8,128)}, f32[512,768]{1,0:T(8,128)}, u32[]{:S(2)}, u32[]{:S(2)}) collective-permute-start(f32[512,768]{1,0:T(8,128)} %shard_map.264.first), channel_id=1, source_target_pairs={{8,16},{12,20},{16,8},{20,12},{9,17},{13,21},{17,9},{21,13},{10,18... | collective-permute-start | bytes 4718600 | tf_op jit(solution)/shard_map/ppermute | solution.py:710
  245.8 25.8 %collective-permute-start.23 = (f32[128,1024]{1,0:T(8,128)}, f32[128,1024]{1,0:T(8,128)}, u32[]{:S(2)}, u32[]{:S(2)}) collective-permute-start(f32[128,1024]{1,0:T(8,128)} %get-tuple-element.589), channel_id=1, source_target_pairs={{0,1},{1,0},{2,3},{3,2},{4,5},{5,4},{6,7},{7,6},{8,9},{9,8},{10,11... | collective-permute-start | bytes 1572872 | tf_op jit(solution)/shard_map/ppermute | solution.py:710
  260.3 31.5 %collective-permute-start.27 = (f32[136,1024]{1,0:T(8,128)S(1)}, f32[136,1024]{1,0:T(8,128)S(1)}, u32[]{:S(2)}, u32[]{:S(2)}) collective-permute-start(f32[136,1024]{1,0:T(8,128)S(1)} %shard_map.265.first), channel_id=1, source_target_pairs={{0,8},{4,12},{24,16},{28,20},{1,9},{5,13},{25,17},{29,21},{2,10},{... | collective-permute-start | bytes 1671176 | tf_op jit(solution)/shard_map/ppermute | solution.py:710
  297.5 29.6 %collective-permute-start.32 = (f32[512,1024]{1,0:T(8,128)S(1)}, f32[512,1024]{1,0:T(8,128)S(1)}, u32[]{:S(2)}, u32[]{:S(2)}) collective-permute-start(f32[512,1024]{1,0:T(8,128)S(1)} %shard_map.273.refs_0_), channel_id=1, source_target_pairs={{0,4},{4,0},{8,12},{12,8},{16,20},{20,16},{24,28},{28,24},{1,5},{5... | collective-permute-start | bytes 6291464 | tf_op jit(solution)/shard_map/ppermute | solution.py:710
  297.6 25.6 %collective-permute-start.30 = (f32[256,1024]{1,0:T(8,128)S(1)}, f32[256,1024]{1,0:T(8,128)S(1)}, u32[]{:S(2)}, u32[]{:S(2)}) collective-permute-start(f32[256,1024]{1,0:T(8,128)S(1)} %shard_map.268.refs_0_), channel_id=1, source_target_pairs={{0,1},{1,0},{2,3},{3,2},{4,5},{5,4},{6,7},{7,6},{8,9},{9,8},{10,11... | collective-permute-start | bytes 3145736 | tf_op jit(solution)/shard_map/ppermute | solution.py:710
  298.8 25.2 %collective-permute-start.31 = (f32[256,1024]{1,0:T(8,128)S(1)}, f32[256,1024]{1,0:T(8,128)S(1)}, u32[]{:S(2)}, u32[]{:S(2)}) collective-permute-start(f32[256,1024]{1,0:T(8,128)S(1)} %shard_map.269.refs_2_), channel_id=1, source_target_pairs={{0,2},{1,3},{2,0},{3,1},{4,6},{5,7},{6,4},{7,5},{8,10},{9,11},{10,... | collective-permute-start | bytes 3145736 | tf_op jit(solution)/shard_map/ppermute | solution.py:710
  300.0 39.2 %collective-permute-start.34 = (f32[512,768]{1,0:T(8,128)S(1)}, f32[512,768]{1,0:T(8,128)S(1)}, u32[]{:S(2)}, u32[]{:S(2)}) collective-permute-start(f32[512,768]{1,0:T(8,128)S(1)} %shard_map.272.second), channel_id=1, source_target_pairs={{8,0},{12,4},{16,24},{20,28},{9,1},{13,5},{17,25},{21,29},{10,2},{... | collective-permute-start | bytes 4718600 | tf_op jit(solution)/shard_map/ppermute | solution.py:710
  301.3 28.5 %collective-permute-start.33 = (f32[136,1024]{1,0:T(8,128)S(1)}, f32[136,1024]{1,0:T(8,128)S(1)}, u32[]{:S(2)}, u32[]{:S(2)}) collective-permute-start(f32[136,1024]{1,0:T(8,128)S(1)} %shard_map.271.first), channel_id=1, source_target_pairs={{8,16},{12,20},{16,8},{20,12},{9,17},{13,21},{17,9},{21,13},{10,18... | collective-permute-start | bytes 1671176 | tf_op jit(solution)/shard_map/ppermute | solution.py:710
  329.8 20.2 %collective-permute-start.35 = (f32[136,1024]{1,0:T(8,128)S(1)}, f32[136,1024]{1,0:T(8,128)S(1)}, u32[]{:S(2)}, u32[]{:S(2)}) collective-permute-start(f32[136,1024]{1,0:T(8,128)S(1)} %shard_map.276.second), channel_id=1, source_target_pairs={{8,0},{12,4},{16,24},{20,28},{9,1},{13,5},{17,25},{21,29},{10,2},{... | collective-permute-start | bytes 1671176 | tf_op jit(solution)/shard_map/ppermute | solution.py:710
  (68 other events, 397.8 us)
